TPU v7x, 32 devices: a whole 2x2x4 slice. The times are simulated.
32 devices in a mesh: out: 4 (over z), in: 8 (over y, x, core).
Axes of the slice: x: 2, y: 2, z: 4, core: 2. Of those that a mesh axis runs over, the one named last changes fastest.
Arguments:
- markov: bfloat16 [63, 2048, 2048], P(None, 'out', 'in'), may hold values from -0.03125 to 0.03125
- probes: bfloat16 [128, 32, 2048], P('out', None, 'in'), may hold values from -6 to 6
- pattern: int32 [32, 16], P('out', 'in'), may hold values 0 or 1
Outputs:
- sketch: bfloat16 [32, 2048, 128], P(None, 'out')
- corange: float32 [128, 32, 2048], P('out', None, 'in')
- gram_matrix: float32 [128, 128], replicated
All inputs are finite; a program needn't handle non-finite values. No bound on the sum of `pattern` on one device may be relied on, other than what follows from the above.
Results may differ from a plain program's by a relative error of at most 0.015.
Values may be sent and summed in bfloat16 or wider, within the bound.
No kernel may reach another device: no remote copies, remote signals or barrier semaphores. Data moves between devices by JAX's collectives and lax.ppermute only.
A program may use at most 128 MiB of HBM per device.

v0:
```python
import functools

import jax
import jax.numpy as jnp
import ml_dtypes
import numpy as np
from jax import lax
from jax.experimental import pallas as pl
from jax.experimental.pallas import tpu as pltpu
from jax.sharding import PartitionSpec as P

OUTPUT_CHANNELS = 2048
BO = 64
BI = 128
R = 32
C = 32
LAGS = 63
F = 32
PARTS = 2
MARKOV_PARTS = 1
CHUNK = 4
VMEM = 60 << 20

bf16 = jnp.bfloat16
f32 = jnp.float32


def split(a):
    hi = a.astype(ml_dtypes.bfloat16)
    lo = (a - hi.astype(np.float64)).astype(ml_dtypes.bfloat16)
    return np.concatenate([hi, lo], axis=0)


def constants():
    theta = np.pi * (2 * np.arange(F)[:, None] + 1) / 64
    lag = np.arange(64)[None]
    cos, sin = np.cos(theta * lag), np.sin(theta * lag)
    eye = np.eye(8)
    fwd = np.stack([cos, sin])
    lag_mat = np.einsum("cfk,pq->cfpkq", fwd, eye).reshape(2 * F * 8, 64 * 8)
    half = fwd[:, :, :32]
    probe_mat = np.einsum("cfj,pq->cfpqj", half, eye).reshape(2 * F * 8, 32 * 8)
    sketch_mat = np.einsum("cfj,pq->cfpjq", half, eye).reshape(2 * F * 8, 32 * 8)
    back = half / F
    raw_mat = np.einsum("cfi,pq->ipcfq", back, eye).reshape(32 * 8, 2 * F * 8)
    cor_mat = np.einsum("cfj,pq->pjcfq", back, eye).reshape(32 * 8, 2 * F * 8)
    return [split(a) for a in (lag_mat, probe_mat, sketch_mat, raw_mat, cor_mat)]


def both(mat_ref, x):
    y = jnp.dot(mat_ref[...], x, preferred_element_type=f32)
    n = y.shape[0] // 2
    return y[:n] + y[n:]


def lag_kernel(keep_ref, mat_ref, x_ref, o_ref):
    rows, m = x_ref.shape[1], x_ref.shape[2]
    keep = keep_ref[0].astype(f32)

    def body(b, _):
        at = pl.ds(pl.multiple_of(b * 16, 16), 16)
        x = x_ref[:, at, :].astype(f32) * keep[None]
        res = []
        for h in range(2):
            part = x[:, 8 * h : 8 * h + 8, :].reshape(LAGS * 8, m)
            part = jnp.concatenate([part, jnp.zeros((8, m), f32)], axis=0)
            res.append(both(mat_ref, part.astype(bf16)).reshape(2, F, 8, m))
        y = jnp.concatenate(res, axis=2).astype(bf16)
        o_ref[:, at, 0:m] = y[0]
        o_ref[:, at, m : 2 * m] = y[1]
        return 0

    lax.fori_loop(0, rows // 16, body, 0)


def lag_transform(markov, keep, mat, part):
    lags, p, m = markov.shape
    blocks = p // BO // MARKOV_PARTS
    return pl.pallas_call(
        lag_kernel,
        grid=(blocks,),
        in_specs=[
            pl.BlockSpec((1, 1, m), lambda i: (part * blocks + i, 0, 0)),
            pl.BlockSpec(mat.shape, lambda i: (0, 0)),
            pl.BlockSpec((lags, BO, m), lambda i: (0, part * blocks + i, 0)),
        ],
        out_specs=pl.BlockSpec((F, BO, 2 * m), lambda i: (0, i, 0)),
        out_shape=jax.ShapeDtypeStruct((F, p // MARKOV_PARTS, 2 * m), bf16),
        compiler_params=pltpu.CompilerParams(vmem_limit_bytes=VMEM),
        cost_estimate=pl.CostEstimate(
            flops=p * m * 1024 * 64, bytes_accessed=2 * 64 * p * m, transcendentals=0
        ),
        name="lag_transform",
    )(keep, mat, markov)


def rotate_into(hat_ref, y, at, at2, lo, hi):
    c, s = y[0].astype(bf16), y[1].astype(bf16)
    hat_ref[:, at, lo] = c
    hat_ref[:, at2, hi] = c
    hat_ref[:, at, hi] = s
    hat_ref[:, at2, lo] = -s


def fetch(m_hbms, m_ref, sems):
    rows = m_ref.shape[1] // MARKOV_PARTS

    def copies(c):
        at = pl.ds(c * CHUNK, CHUNK)
        return [
            pltpu.make_async_copy(
                m_hbm.at[at], m_ref.at[at, pl.ds(k * rows, rows)], sems.at[k, c]
            )
            for k, m_hbm in enumerate(m_hbms)
        ]

    for c in range(F // CHUNK):
        for copy in copies(c):
            copy.start()
    return copies


def over_frequencies(copies, one):
    def body(c, _):
        for copy in copies(c):
            copy.wait()
        for k in range(CHUNK):
            one(c * CHUNK + k)
        return 0

    lax.fori_loop(0, F // CHUNK, body, 0)


def back_input(freq, b, h, s_count, cols):
    re = freq[:, pl.ds(pl.multiple_of(b * 16 + 8 * h, 8), 8), cols]
    im = freq[:, pl.ds(pl.multiple_of(s_count + b * 16 + 8 * h, 8), 8), cols]
    x = jnp.concatenate([re, im], axis=0)
    return x.reshape(2 * F * 8, x.shape[-1]).astype(bf16)


def sketch_kernel(n, n_out, n_in, place_ref, fwd_ref, back_ref, *refs):
    u_refs, m_hbms, refs = refs[:n], refs[n : n + MARKOV_PARTS], refs[n + MARKOV_PARTS :]
    sums, (back, m_ref, hat, freq, sems) = refs[: 2 * PARTS], refs[2 * PARTS :]
    whole = u_refs[n_out:]
    u_refs = list(u_refs[:n_out])
    for ref in whole:
        u_refs += [ref.at[lax.rem(place_ref[0] + d, n_out)] for d in range(n_out)]
    rows, _, m = u_refs[0].shape
    s_count, p = n_out * PARTS * rows, m_ref.shape[1]
    copies = fetch(m_hbms, m_ref, sems)

    for b in range(s_count // 16):
        res = []
        for g in (2 * b, 2 * b + 1):
            first = (g * 8) % rows
            x = u_refs[g * 8 // rows][first : first + 8].reshape(8 * C, m)
            res.append(both(fwd_ref, x).reshape(2, F, 8, m))
        y = jnp.concatenate(res, axis=2)
        at, at2 = pl.ds(b * 16, 16), pl.ds(s_count + b * 16, 16)
        rotate_into(hat, y, at, at2, slice(0, m), slice(m, 2 * m))

    def one(f):
        freq[f] = lax.dot_general(
            hat[f], m_ref[f], (((1,), (1,)), ((), ())), preferred_element_type=f32
        )

    over_frequencies(copies, one)
    width = min(p, 256)
    g = R // n_in * 8
    for part in range(2):
        for k, slot in enumerate(slots(n_in)):
            at = pl.ds(pl.multiple_of(part * R * 8 + (place_ref[1] ^ slot) * g, 16), g)
            back[part * R * 8 + k * g : part * R * 8 + (k + 1) * g] = back_ref[at]

    for q in range(PARTS):
        keep_ref, send_ref = sums[2 * q : 2 * q + 2]
        part = s_count // PARTS // 16

        def body(b, _):
            at = pl.ds(pl.multiple_of(b * 16, 16), 16)
            for w in range(p // width):
                cols = slice(w * width, (w + 1) * width)
                res = []
                for h in range(2):
                    x = back_input(freq, q * part + b, h, s_count, cols)
                    res.append(both(back, x).reshape(R, 8, width))
                y = jnp.concatenate(res, axis=1)
                keep_ref[:, at, cols] = y[: R // 2]
                send_ref[:, at, cols] = y[R // 2 :].astype(bf16)
            return 0

        lax.fori_loop(0, part, body, 0)


def vmem_specs(arrays):
    return [pl.BlockSpec(memory_space=pltpu.VMEM) for _ in arrays]


def any_specs(arrays):
    return [pl.BlockSpec(memory_space=pl.ANY) for _ in arrays]


def product_cost(p, m, extra):
    return pl.CostEstimate(
        flops=2 * F * 256 * 2 * m * p * 2, bytes_accessed=4 * F * p * m + extra, transcendentals=0
    )


def sketch_part(probes, hankel, fwd, back, place, n_out, n_in):
    rows, _, m = probes[0].shape
    p = hankel[0].shape[1] * MARKOV_PARTS
    part, s_count = rows * n_out, rows * n_out * PARTS
    return pl.pallas_call(
        functools.partial(sketch_kernel, len(probes), n_out, n_in),
        in_specs=[pl.BlockSpec(memory_space=pltpu.SMEM)]
        + vmem_specs([fwd, back, *probes])
        + any_specs(hankel),
        out_specs=vmem_specs(range(2 * PARTS)),
        out_shape=[
            jax.ShapeDtypeStruct((R // 2, part, p), f32),
            jax.ShapeDtypeStruct((R // 2, part, p), bf16),
        ]
        * PARTS,
        scratch_shapes=[
            pltpu.VMEM(back.shape, bf16),
            pltpu.VMEM((F, p, 2 * m), bf16),
            pltpu.VMEM((F, 2 * s_count, 2 * m), bf16),
            pltpu.VMEM((F, 2 * s_count, p), f32),
            pltpu.SemaphoreType.DMA((MARKOV_PARTS, F // CHUNK)),
        ],
        compiler_params=pltpu.CompilerParams(vmem_limit_bytes=VMEM),
        cost_estimate=product_cost(p, m, 0),
        name="sketch_part",
    )(place, fwd, back, *probes, *hankel)


def corange_kernel(n_in, n_out, n_before, n_o, place_ref, fwd_ref, back_ref, *refs):
    k_refs, refs = refs[: n_in // 2 + 1], refs[n_in // 2 + 1 :]
    m_hbms, refs = refs[:MARKOV_PARTS], refs[MARKOV_PARTS + n_before :]
    o_refs, (fwd, m_ref, hat, freq, sems) = refs[:n_o], refs[n_o:]
    if n_o == 1:
        o_refs = [o_refs[0].at[lax.rem(place_ref[0] + d, n_out)] for d in range(n_out)]
    _, s_count, p = k_refs[0].shape
    m = m_ref.shape[2] // 2
    rows = s_count // n_out
    copies = fetch(m_hbms, m_ref, sems)
    width = min(p, 256)

    g = R // n_in * 8
    to = lax.broadcasted_iota(jnp.int32, (R * 8, R * 8), 1)
    come = lax.broadcasted_iota(jnp.int32, (R * 8, R * 8), 0)
    where = to // g
    slot = jnp.where(where < n_in // 2, 2 * where, 2 * where - (n_in - 1))
    moved = come == (place_ref[1] ^ slot) * g + to % g
    move = jnp.where(moved, 1.0, 0.0).astype(bf16)
    fwd[...] = jnp.dot(fwd_ref[...], move, preferred_element_type=f32).astype(bf16)

    def forward(b, _):
        at = pl.ds(pl.multiple_of(b * 16, 16), 16)
        at2 = pl.ds(pl.multiple_of(s_count + b * 16, 16), 16)
        for w in range(p // width):
            cols = slice(w * width, (w + 1) * width)
            k = jnp.concatenate([ref[:, at, cols] for ref in k_refs], axis=0).astype(f32)
            res = []
            for h in range(2):
                x = k[:, 8 * h : 8 * h + 8, :].reshape(R * 8, width).astype(bf16)
                res.append(both(fwd, x).reshape(2, F, 8, width))
            y = jnp.concatenate(res, axis=2)
            lo = slice(w * width, (w + 1) * width)
            hi = slice(p + w * width, p + (w + 1) * width)
            rotate_into(hat, y, at, at2, lo, hi)
        return 0

    lax.fori_loop(0, s_count // 16, forward, 0)

    def one(f):
        left = hat[f]
        freq[f] = jnp.dot(left[:, :p], m_ref[f, :, :m], preferred_element_type=f32) + jnp.dot(
            left[:, p:], m_ref[f, :, m:], preferred_element_type=f32
        )

    over_frequencies(copies, one)

    for g in range(s_count // 8):
        x = back_input(freq, g // 2, g % 2, s_count, slice(0, m))
        first = (g * 8) % rows
        o_ref = o_refs[g * 8 // rows]
        o_ref[first : first + 8] = both(back_ref, x).reshape(8, C, m).astype(o_ref.dtype)


def corange_part(pieces, hankel, fwd, back, place, n_out, n_in, before, whole):
    _, s_count, p = pieces[0].shape
    m = hankel[0].shape[2] // 2
    rows = s_count // n_out
    if whole:
        outs = [jax.ShapeDtypeStruct((n_out, rows, C, m), bf16)]
    else:
        outs = [jax.ShapeDtypeStruct((rows, C, m), bf16 if d else f32) for d in range(n_out)]
    return pl.pallas_call(
        functools.partial(corange_kernel, n_in, n_out, len(before), len(outs)),
        in_specs=[pl.BlockSpec(memory_space=pltpu.SMEM)]
        + vmem_specs([fwd, back, *pieces])
        + any_specs([*hankel, *before]),
        out_specs=vmem_specs(outs),
        out_shape=outs,
        scratch_shapes=[
            pltpu.VMEM(fwd.shape, bf16),
            pltpu.VMEM((F, p, 2 * m), bf16),
            pltpu.VMEM((F, 2 * s_count, 2 * p), bf16),
            pltpu.VMEM((F, 2 * s_count, m), f32),
            pltpu.SemaphoreType.DMA((MARKOV_PARTS, F // CHUNK)),
        ],
        compiler_params=pltpu.CompilerParams(vmem_limit_bytes=VMEM),
        cost_estimate=product_cost(p, m, 0),
        name="corange_part",
    )(place, fwd, back, *pieces, *hankel, *before)


def in_order(x, both_parts, q, z, n_out):
    rows = x.shape[0] // n_out
    x = x.astype(f32)
    for d in range(n_out):
        first = lax.rem(z + d, n_out) * (PARTS * rows) + q * rows
        both_parts[pl.ds(pl.multiple_of(first, 8), rows), :] = x[d * rows : (d + 1) * rows]


def gram_kernel(n_out, place_ref, *refs):
    k_refs, (gram_ref, both_parts) = refs[:PARTS], refs[PARTS:]
    total = jnp.zeros(gram_ref.shape, f32)
    for i in range(k_refs[0].shape[0]):
        for q, ref in enumerate(k_refs):
            in_order(ref[i], both_parts, q, place_ref[0], n_out)
        x = both_parts[...].astype(bf16)
        total += lax.dot_general(x, x, (((1,), (1,)), ((), ())), preferred_element_type=f32)
    gram_ref[...] = total


def gram_part(own, place, n_out):
    _, s_count, p = own[0].shape
    s_count *= PARTS
    return pl.pallas_call(
        functools.partial(gram_kernel, n_out),
        in_specs=[pl.BlockSpec(memory_space=pltpu.SMEM)] + vmem_specs(own),
        out_specs=pl.BlockSpec(memory_space=pltpu.VMEM),
        out_shape=jax.ShapeDtypeStruct((s_count, s_count), f32),
        scratch_shapes=[pltpu.VMEM((s_count, p), f32)],
        name="gram_part",
    )(place, *own)


def total_kernel(n, *refs):
    done, rest, o_ref = refs[:n], refs[n:-2], refs[-1]
    rows = rest[0].shape[0]
    for q, ref in enumerate(done):
        o_ref[q * rows : (q + 1) * rows] = ref[...].astype(f32)
    total = rest[0][...]
    for ref in rest[1:]:
        total += ref[...].astype(f32)
    o_ref[n * rows :] = total


def total_corange(done, own, arrived, before):
    rows, *rest = own.shape
    return pl.pallas_call(
        functools.partial(total_kernel, len(done)),
        in_specs=vmem_specs([*done, own, *arrived]) + any_specs([before]),
        out_specs=pl.BlockSpec(memory_space=pltpu.VMEM),
        out_shape=jax.ShapeDtypeStruct((rows * PARTS, *rest), f32),
        name="total_corange",
    )(*done, own, *arrived, before)


def finish_kernel(n_out, n_in, place_ref, *refs):
    o_ref, both_parts = refs[-2:]
    n = n_in // 2 + 1
    i_count = refs[0].shape[0]
    z, idx = place_ref[0], place_ref[1]
    for k, slot in enumerate(slots(n_in)):
        ref, base = min(k, n - 1), max(k - (n - 1), 0) * i_count

        def body(t, _):
            for q in range(PARTS):
                in_order(refs[q * n + ref][base + t], both_parts, q, z, n_out)
            o_ref[(idx ^ slot) * i_count + t] = both_parts[...].T.astype(bf16)
            return 0

        lax.fori_loop(0, i_count, body, 0)


def finish(pieces, place, after, n_out, n_in):
    i_count, s_count, p = pieces[0][0].shape
    flat = [x for part in pieces for x in part]
    return pl.pallas_call(
        functools.partial(finish_kernel, n_out, n_in),
        in_specs=[pl.BlockSpec(memory_space=pltpu.SMEM)] + vmem_specs(flat) + any_specs(after),
        out_specs=pl.BlockSpec(memory_space=pltpu.VMEM),
        out_shape=jax.ShapeDtypeStruct((R, p, PARTS * s_count), bf16),
        scratch_shapes=[pltpu.VMEM((PARTS * s_count, p), f32)],
        compiler_params=pltpu.CompilerParams(vmem_limit_bytes=VMEM),
        cost_estimate=pl.CostEstimate(
            flops=0, bytes_accessed=16 * R * p * s_count, transcendentals=0
        ),
        name="finish",
    )(place, *flat, *after)


def slots(n):
    return [*range(0, n, 2), *range(1, n, 2)]


def to_xor(x, axis, r, n):
    return lax.ppermute(x, axis, [(d, d ^ r) for d in range(n)])


def settle_kernel(n, keep_ref, away_ref, *refs):
    total = keep_ref[...] + away_ref[...].astype(f32)
    for ref in refs[:n]:
        total += ref[...].astype(f32)
    refs[-1][...] = total.astype(bf16)


def settle(keep, away, arrived, before):
    block = pl.BlockSpec((1, *keep.shape[1:]), lambda i: (i, 0, 0))
    return pl.pallas_call(
        functools.partial(settle_kernel, len(arrived)),
        grid=(arrived[0].shape[0],),
        in_specs=[block] * (2 + len(arrived)) + any_specs(before),
        out_specs=block,
        out_shape=jax.ShapeDtypeStruct(arrived[0].shape, bf16),
        cost_estimate=pl.CostEstimate(
            flops=0, bytes_accessed=8 * arrived[0].size, transcendentals=0
        ),
        name="settle",
    )(keep, away, *arrived, *before)


def meet(keep, send, n):
    away = to_xor(send, "in", 1, n)
    g = R // n
    arrived = []
    for k in range(1, n // 2):
        rows = slice(k * g, (k + 1) * g)
        arrived.append(to_xor((keep[rows] + away[rows].astype(f32)).astype(bf16), "in", 2 * k, n))
    return keep, away, arrived


def spread(own, n):
    return [own] + [to_xor(own, "in", 2 * k, n) for k in range(1, n // 2)]


def join_kernel(n, *refs):
    rows = refs[0].shape[0]
    for k in range(n):
        refs[-1][k * rows : (k + 1) * rows] = refs[k][...]


def join(mine, before):
    rows, *rest = mine[0].shape
    return pl.pallas_call(
        functools.partial(join_kernel, len(mine)),
        in_specs=vmem_specs(mine) + any_specs(before),
        out_specs=pl.BlockSpec(memory_space=pltpu.VMEM),
        out_shape=jax.ShapeDtypeStruct((len(mine) * rows, *rest), bf16),
        name="join",
    )(*mine, *before)


def shards(n_out, n_in, mats, markov, probes, pattern):
    lag_mat, probe_mat, sketch_mat, raw_mat, cor_mat = [jnp.asarray(a) for a in mats]
    rows = probes.shape[0] // PARTS
    z, idx = lax.axis_index("out"), lax.axis_index("in")

    place = jnp.stack([z, idx]).astype(jnp.int32)
    keep = jnp.repeat(pattern, BI, axis=1).astype(f32)[:, None, :]

    own = probes[:rows]
    gathered = [own]
    for d in range(1, n_out):
        gathered.append(lax.ppermute(own, "out", [((k + d) % n_out, k) for k in range(n_out)]))
    for q in range(1, PARTS):
        gathered.append(lax.all_gather(probes[q * rows : (q + 1) * rows], "out"))
    hankel = [lag_transform(markov, keep, lag_mat, q) for q in range(MARKOV_PARTS)]

    raws = sketch_part(gathered, hankel, probe_mat, raw_mat, place, n_out, n_in)
    met = [meet(raws[2 * q], raws[2 * q + 1], n_in) for q in range(PARTS)]
    owns, sums, summed, before = [], [], [], []
    for q, x in enumerate(met):
        owns.append(settle(*x, before))
        mine = spread(owns[q], n_in)
        last = q == PARTS - 1
        gram = [gram_part(owns, place, n_out)] if last else []
        if last:
            for bit in range(n_in.bit_length() - 1):
                gram = [gram[0] + to_xor(gram[0], "in", 1 << bit, n_in)]
        sums.append(mine + [to_xor(join(mine, gram), "in", 1, n_in)])
        cor = corange_part(
            sums[q], hankel, sketch_mat, cor_mat, place, n_out, n_in, before, not last
        )
        before = [cor[-1]]
        if not last:
            whole = cor[0].reshape((-1,) + cor[0].shape[2:])
            summed.append(lax.psum_scatter(whole, "out", scatter_dimension=0, tiled=True))

    (gram,) = gram
    for bit in range(n_out.bit_length() - 1):
        gram = gram + to_xor(gram, "out", 1 << bit, n_out)
    gram_matrix = gram / (R * OUTPUT_CHANNELS)

    arrived = [
        lax.ppermute(cor[d], "out", [(k, (k + d) % n_out) for k in range(n_out)])
        for d in range(1, n_out)
    ]
    sketch = finish(sums, place, [*summed, *before, gram_matrix], n_out, n_in)
    corange = total_corange(summed, cor[0], arrived, sketch)
    return (sketch, corange, gram_matrix)


def solution(mesh):
    body = functools.partial(shards, mesh.shape["out"], mesh.shape["in"], constants())
    return jax.shard_map(
        body,
        mesh=mesh,
        in_specs=(P(None, "out", "in"), P("out", None, "in"), P("out", "in")),
        out_specs=(P(None, "out", None), P("out", None, "in"), P()),
        check_vma=False,
    )
```

profile of v0, /device:TPU:9, one launch (start us, length us, event | category | flops | bytes accessed | tf_op | source)
XLA Modules:
  0.0 218.3 jit_solution(990164337205738287)
XLA Ops:
  7.2 1.8 fusion
  9.1 1.3 collective-permute-start.2
  10.4 1.1 collective-permute-start.1
  11.5 1.4 collective-permute-start
  12.9 0.7 convert_element_type.50
  13.6 0.7 broadcast_in_dim.4
  14.3 26.6 %lag_transform.1.refs_5_ = bf16[32,512,512]{2,1,0:T(8,128)(2,1)} custom-call(f32[8,1,256]{2,1,0:T(1,128)} %bitcast.6, bf16[1024,512]{1,0:T(8,128)(2,1)} %constant.21.clone.mat_ref, bf16[63,512,256]{2,1,0:T(8,128)(2,1)} %x_ref.1), custom_call_target="tpu_custom_call" | custom-call | flops 8589934592 | bytes 16777216 | tf_op jit(solution)/shard_map/lag_transform/pallas_call | solution.py:79
  40.9 0.7 pad_add_fusion.place_ref
  41.6 3.0 %collective-permute-done.1.refs_2_ = bf16[16,32,256]{2,1,0:T(8,128)(2,1)S(1)} collective-permute-done((bf16[16,32,256]{2,1,0:T(8,128)(2,1)S(1)}, bf16[16,32,256]{2,1,0:T(8,128)(2,1)S(1)}, u32[]{:S(2)}, u32[]{:S(2)}) %collective-permute-start.1) | collective-permute-done | bytes 262176 | tf_op jit(solution)/shard_map/ppermute | solution.py:479
  44.5 6.9 %collective-permute-done.refs_1_ = bf16[16,32,256]{2,1,0:T(8,128)(2,1)S(1)} collective-permute-done((bf16[16,32,256]{2,1,0:T(8,128)(2,1)S(1)}, bf16[16,32,256]{2,1,0:T(8,128)(2,1)S(1)}, u32[]{:S(2)}, u32[]{:S(2)}) %collective-permute-start) | collective-permute-done | bytes 262176 | tf_op jit(solution)/shard_map/ppermute | solution.py:479
  51.4 0.4 all-gather.3.cloned.1.call-done
  51.9 0.3 copy-done.21
  52.2 18.1 %sketch_part.1 = (f32[16,64,512]{2,1,0:T(8,128)}, bf16[16,64,512]{2,1,0:T(8,128)(2,1)}, f32[16,64,512]{2,1,0:T(8,128)}, bf16[16,64,512]{2,1,0:T(8,128)(2,1)}) custom-call(s32[2]{0:T(128)} %pad_add_fusion.place_ref, bf16[1024,256]{1,0:T(8,128)(2,1)} %constant.22.clone.fwd_ref, bf16[512,512]{1,0:T(8,128)(2,1)} %constant.24.clone.back_ref, ...), custom_call_target="tpu_custom_call" | custom-call | flops 8589934592 | bytes 16777216 | tf_op jit(solution)/shard_map/sketch_part/pallas_call | solution.py:213
  70.2 1.3 collective-permute-start.3
  71.5 2.5 %collective-permute-done.3.away_ref = bf16[16,64,512]{2,1,0:T(8,128)(2,1)S(1)} collective-permute-done((bf16[16,64,512]{2,1,0:T(8,128)(2,1)}, bf16[16,64,512]{2,1,0:T(8,128)(2,1)S(1)}, u32[]{:S(2)}, u32[]{:S(2)}) %collective-permute-start.3) | collective-permute-done | bytes 1048608 | tf_op jit(solution)/shard_map/ppermute | solution.py:412
  74.0 2.0 add_convert_fusion.3
  76.0 2.2 %collective-permute-start.6 = (bf16[4,64,512]{2,1,0:T(8,128)(2,1)S(1)}, bf16[4,64,512]{2,1,0:T(8,128)(2,1)S(1)}, u32[]{:S(2)}, u32[]{:S(2)}) collective-permute-start(bf16[4,64,512]{2,1,0:T(8,128)(2,1)S(1)} %get-tuple-element.22), channel_id=1, source_target_pairs={{0,6},{1,7},{2,4},{3,5},{4,2},{5,3},{6,0},{7,1},{8,14},{9,15},{10,... | collective-permute-start | bytes 786440 | tf_op jit(solution)/shard_map/ppermute | solution.py:412
  78.7 1.2 collective-permute-start.11
  80.0 4.6 %collective-permute-done.6.refs_2_ = bf16[4,64,512]{2,1,0:T(8,128)(2,1)S(1)} collective-permute-done((bf16[4,64,512]{2,1,0:T(8,128)(2,1)S(1)}, bf16[4,64,512]{2,1,0:T(8,128)(2,1)S(1)}, u32[]{:S(2)}, u32[]{:S(2)}) %collective-permute-start.6) | collective-permute-done | bytes 262176 | tf_op jit(solution)/shard_map/ppermute | solution.py:412
  84.6 6.3 %collective-permute-done.5.refs_1_ = bf16[4,64,512]{2,1,0:T(8,128)(2,1)S(1)} collective-permute-done((bf16[4,64,512]{2,1,0:T(8,128)(2,1)S(1)}, bf16[4,64,512]{2,1,0:T(8,128)(2,1)S(1)}, u32[]{:S(2)}, u32[]{:S(2)}) %collective-permute-start.5) | collective-permute-done | bytes 262176 | tf_op jit(solution)/shard_map/ppermute | solution.py:412
  90.9 0.7 copy-done.12
  91.5 0.7 copy-done.14
  92.3 3.3 %settle.2.refs_0_ = bf16[4,64,512]{2,1,0:T(8,128)(2,1)} custom-call(f32[16,64,512]{2,1,0:T(8,128)} %get-tuple-element.11.keep_ref, bf16[16,64,512]{2,1,0:T(8,128)(2,1)} %copy-done.2, bf16[4,64,512]{2,1,0:T(8,128)(2,1)} %copy-done.14, bf16[4,64,512]{2,1,0:T(8,128)(2,1)} %copy-done.12, bf16[4,64,512]{2,1,0:T(8,128)(2,1)} %copy-done.10), custom_call_target="tpu_custom_call" | custom-call | bytes 1048576 | tf_op jit(solution)/shard_map/settle/pallas_call | solution.py:424
  95.6 0.8 collective-permute-start.9
  96.4 1.6 collective-permute-start.8
  98.2 5.9 %collective-permute-done.9.refs_3_ = bf16[4,64,512]{2,1,0:T(8,128)(2,1)S(1)} collective-permute-done((bf16[4,64,512]{2,1,0:T(8,128)(2,1)}, bf16[4,64,512]{2,1,0:T(8,128)(2,1)S(1)}, u32[]{:S(2)}, u32[]{:S(2)}) %collective-permute-start.9) | collective-permute-done | bytes 262176 | tf_op jit(solution)/shard_map/ppermute | solution.py:412
  104.1 6.5 %collective-permute-done.8.refs_2_ = bf16[4,64,512]{2,1,0:T(8,128)(2,1)} collective-permute-done((bf16[4,64,512]{2,1,0:T(8,128)(2,1)}, bf16[4,64,512]{2,1,0:T(8,128)(2,1)}, u32[]{:S(2)}, u32[]{:S(2)}) %collective-permute-start.8) | collective-permute-done | bytes 262176 | tf_op jit(solution)/shard_map/ppermute | solution.py:412
  110.7 2.2 %join.2 = bf16[16,64,512]{2,1,0:T(8,128)(2,1)} custom-call(bf16[4,64,512]{2,1,0:T(8,128)(2,1)} %settle.2.refs_0_, bf16[4,64,512]{2,1,0:T(8,128)(2,1)} %collective-permute-done.7.refs_1_, bf16[4,64,512]{2,1,0:T(8,128)(2,1)} %collective-permute-done.8.refs_2_, bf16[4,64,512]{2,1,0:T(8,128)(2,1)} %copy-done.7), custom_call_target="tpu_custom_call" | custom-call | tf_op jit(solution)/shard_map/join/pallas_call | solution.py:459
  112.9 0.6 collective-permute-start.10
  113.7 1.2 collective-permute-start.14
  115.0 1.1 collective-permute-start.13
  116.1 0.4 collective-permute-start.12
  116.5 11.3 %corange_part.2.refs_3_.refs_6_ = bf16[4,16,32,256]{3,2,1,0:T(8,128)(2,1)} custom-call(s32[2]{0:T(128)} %pad_add_fusion.place_ref, bf16[1024,256]{1,0:T(8,128)(2,1)} %constant.23.clone.fwd_ref, bf16[512,512]{1,0:T(8,128)(2,1)} %constant.25.clone.back_ref, bf16[4,64,512]{2,1,0:T(8,128)(2,1)} %settle.2.refs_0_, ...), custom_call_target="tpu_custom_call" | custom-call | flops 8589934592 | bytes 16777216 | tf_op jit(solution)/shard_map/corange_part/pallas_call | solution.py:299
  127.8 0.8 collective-permute-done.13.refs_1_
  128.6 0.7 copy-done.11
  129.3 0.7 copy-done.13
  130.0 3.3 %settle.3.refs_1_.refs_0_.refs_5_ = bf16[4,64,512]{2,1,0:T(8,128)(2,1)} custom-call(f32[16,64,512]{2,1,0:T(8,128)} %get-tuple-element.13.keep_ref, bf16[16,64,512]{2,1,0:T(8,128)(2,1)} %copy-done.1, bf16[4,64,512]{2,1,0:T(8,128)(2,1)} %copy-done.13, bf16[4,64,512]{2,1,0:T(8,128)(2,1)} %copy-done.11, bf16[4,64,512]{2,1,0:T(8,128)(2,1)} %copy-done.9, ...), custom_call_target="tpu_custom_call" | custom-call | bytes 1048576 | tf_op jit(solution)/shard_map/settle/pallas_call | solution.py:424
  133.3 1.2 collective-permute-start.17
  134.5 1.1 collective-permute-start.16
  135.6 0.4 collective-permute-start.15
  136.0 2.2 gram_part.1
  138.1 1.3 collective-permute-start.18
  139.4 1.1 collective-permute-done.18
  140.5 0.9 add.41
  141.4 1.2 collective-permute-start.19
  142.6 6.3 %collective-permute-done.19 = f32[128,128]{1,0:T(8,128)S(1)} collective-permute-done((f32[128,128]{1,0:T(8,128)S(1)}, f32[128,128]{1,0:T(8,128)S(1)}, u32[]{:S(2)}, u32[]{:S(2)}) %collective-permute-start.19) | collective-permute-done | bytes 65568 | tf_op jit(solution)/shard_map/ppermute | solution.py:412
  148.9 0.4 collective-permute-start.20
  149.3 2.8 %collective-permute-done.20 = f32[128,128]{1,0:T(8,128)S(1)} collective-permute-done((f32[128,128]{1,0:T(8,128)S(1)}, f32[128,128]{1,0:T(8,128)S(1)}, u32[]{:S(2)}, u32[]{:S(2)}) %collective-permute-start.20) | collective-permute-done | bytes 65568 | tf_op jit(solution)/shard_map/ppermute | solution.py:412
  152.1 0.6 add.43.refs_4_
  152.7 0.7 copy-done.4
  153.5 0.7 copy-done.6
  154.2 2.2 %join.3 = bf16[16,64,512]{2,1,0:T(8,128)(2,1)} custom-call(bf16[4,64,512]{2,1,0:T(8,128)(2,1)} %settle.3.refs_1_.refs_0_.refs_5_, bf16[4,64,512]{2,1,0:T(8,128)(2,1)} %copy-done.6, bf16[4,64,512]{2,1,0:T(8,128)(2,1)} %copy-done.5, bf16[4,64,512]{2,1,0:T(8,128)(2,1)} %copy-done.4, f32[128,128]{1,0:T(8,128)} %add.43.refs_4_), custom_call_target="tpu_custom_call" | custom-call | tf_op jit(solution)/shard_map/join/pallas_call | solution.py:459
  156.4 2.5 %collective-permute-start.21 = (bf16[16,64,512]{2,1,0:T(8,128)(2,1)}, bf16[16,64,512]{2,1,0:T(8,128)(2,1)S(1)}, u32[]{:S(2)}, u32[]{:S(2)}) collective-permute-start(bf16[16,64,512]{2,1,0:T(8,128)(2,1)} %join.3), channel_id=1, source_target_pairs={{0,1},{1,0},{2,3},{3,2},{4,5},{5,4},{6,7},{7,6},{8,9},{9,8},{10,11... | collective-permute-start | bytes 3145736 | tf_op jit(solution)/shard_map/ppermute | solution.py:412
  159.0 3.7 %collective-permute-done.22 = f32[128,128]{1,0:T(8,128)S(1)} collective-permute-done((f32[128,128]{1,0:T(8,128)S(1)}, f32[128,128]{1,0:T(8,128)S(1)}, u32[]{:S(2)}, u32[]{:S(2)}) %collective-permute-start.22) | collective-permute-done | bytes 65568 | tf_op jit(solution)/shard_map/ppermute | solution.py:412
  162.7 0.8 collective-permute-start.23
  163.5 1.0 copy-done.3
  164.5 11.1 %corange_part.3 = (f32[16,32,256]{2,1,0:T(8,128)}, bf16[16,32,256]{2,1,0:T(8,128)(2,1)}, bf16[16,32,256]{2,1,0:T(8,128)(2,1)}, bf16[16,32,256]{2,1,0:T(8,128)(2,1)}) custom-call(s32[2]{0:T(128)} %pad_add_fusion.place_ref, bf16[1024,256]{1,0:T(8,128)(2,1)} %constant.23.clone.fwd_ref, bf16[512,512]{1,0:T(8,128)(2,1)} %constant.25.clone.back_ref, ...), custom_call_target="tpu_custom_call" | custom-call | flops 8589934592 | bytes 16777216 | tf_op jit(solution)/shard_map/corange_part/pallas_call | solution.py:299
  175.6 0.7 collective-permute-start.24
  176.3 2.5 %collective-permute-start.25 = (bf16[16,32,256]{2,1,0:T(8,128)(2,1)}, bf16[16,32,256]{2,1,0:T(8,128)(2,1)S(1)}, u32[]{:S(2)}, u32[]{:S(2)}) collective-permute-start(bf16[16,32,256]{2,1,0:T(8,128)(2,1)} %get-tuple-element.18), channel_id=1, source_target_pairs={{0,16},{8,24},{16,0},{24,8},{1,17},{9,25},{17,1},{25,9},{2,18},{10... | collective-permute-start | bytes 786440 | tf_op jit(solution)/shard_map/ppermute | solution.py:510
  178.8 0.6 add_multiply_fusion.refs_12_
  179.5 20.5 %reduce-scatter.2.cloned.1.call-done.refs_10_.refs_0_ = bf16[16,32,256]{2,1,0:T(8,128)(2,1)} async-done(((bf16[64,32,256]{2,1,0:T(8,128)(2,1)}), bf16[16,32,256]{2,1,0:T(8,128)(2,1)}) %reduce-scatter.2.cloned.1.call-update) | async-done | bytes 262160 | tf_op jit(solution)/shard_map/reduce_scatter | solution.py:502
  200.0 8.2 %finish.1.refs_5_ = bf16[32,512,128]{2,1,0:T(8,128)(2,1)} custom-call(s32[2]{0:T(128)} %pad_add_fusion.place_ref, bf16[4,64,512]{2,1,0:T(8,128)(2,1)} %settle.2.refs_0_, bf16[4,64,512]{2,1,0:T(8,128)(2,1)} %collective-permute-done.7.refs_1_, bf16[4,64,512]{2,1,0:T(8,128)(2,1)} %collective-permute-done.8.refs_2_, bf16[4,64,512]{2,1,0:T(8,128)(2,1)} %copy-done.7, ...), custom_call_target="tpu_custom_call" | custom-call | bytes 16777216 | tf_op jit(solution)/shard_map/finish/pallas_call | solution.py:393
  208.2 0.7 copy-done.16
  209.0 2.4 %total_corange.1 = f32[32,32,256]{2,1,0:T(8,128)} custom-call(bf16[16,32,256]{2,1,0:T(8,128)(2,1)} %reduce-scatter.2.cloned.1.call-done.refs_10_.refs_0_, f32[16,32,256]{2,1,0:T(8,128)} %get-tuple-element.16.refs_1_, bf16[16,32,256]{2,1,0:T(8,128)(2,1)} %copy-done.16, bf16[16,32,256]{2,1,0:T(8,128)(2,1)} %copy-done.17, bf16[16,32,256]{2,1,0:T(8,128)(2,1)} %copy-done.18, ...), custom_call_target="tpu_custom_call" | custom-call | tf_op jit(solution)/shard_map/total_corange/pallas_call | solution.py:364
  (63 shorter events, 1.7 us)
Async XLA Ops:
  7.2 44.7 %all-gather.3.cloned.1.call-start = ((), (), s32[]{:S(2)}) async-start(), calls=%async_computation.2 | async-start | bytes 1310720 | tf_op jit(solution)/shard_map/all_gather | solution.py:481
  9.0 31.9 %copy-start.15 = (bf16[16,32,256]{2,1,0:T(8,128)(2,1)}, bf16[16,32,256]{2,1,0:T(8,128)(2,1)S(1)}, u32[]{:S(2)}) copy-start(bf16[16,32,256]{2,1,0:T(8,128)(2,1)S(1)} %get-tuple-element.26.refs_0_) | copy-start | bytes 786436
  9.0 191.0 %reduce-scatter.2.cloned.1.call-start = ((), (), s32[]{:S(2)}) async-start(), calls=%async_computation.1 | async-start | bytes 1310720 | tf_op jit(solution)/shard_map/reduce_scatter | solution.py:502
  9.1 32.5 %collective-permute-start.2 = (bf16[16,32,256]{2,1,0:T(8,128)(2,1)S(1)}, bf16[16,32,256]{2,1,0:T(8,128)(2,1)S(1)}, u32[]{:S(2)}, u32[]{:S(2)}) collective-permute-start(bf16[16,32,256]{2,1,0:T(8,128)(2,1)S(1)} %get-tuple-element.26.refs_0_), channel_id=1, source_target_pairs={{24,0},{0,8},{8,16},{16,24},{25,1},{1,9},{9,17},{17,25},{26,2},{2,... | collective-permute-start | bytes 786440 | tf_op jit(solution)/shard_map/ppermute | solution.py:479
  10.4 34.1 %collective-permute-start.1 = (bf16[16,32,256]{2,1,0:T(8,128)(2,1)S(1)}, bf16[16,32,256]{2,1,0:T(8,128)(2,1)S(1)}, u32[]{:S(2)}, u32[]{:S(2)}) collective-permute-start(bf16[16,32,256]{2,1,0:T(8,128)(2,1)S(1)} %get-tuple-element.26.refs_0_), channel_id=1, source_target_pairs={{16,0},{24,8},{0,16},{8,24},{17,1},{25,9},{1,17},{9,25},{18,2},{26... | collective-permute-start | bytes 786440 | tf_op jit(solution)/shard_map/ppermute | solution.py:479
  11.5 40.0 %collective-permute-start = (bf16[16,32,256]{2,1,0:T(8,128)(2,1)S(1)}, bf16[16,32,256]{2,1,0:T(8,128)(2,1)S(1)}, u32[]{:S(2)}, u32[]{:S(2)}) collective-permute-start(bf16[16,32,256]{2,1,0:T(8,128)(2,1)S(1)} %get-tuple-element.26.refs_0_), channel_id=1, source_target_pairs={{8,0},{16,8},{24,16},{0,24},{9,1},{17,9},{25,17},{1,25},{10,2},{18... | collective-permute-start | bytes 786440 | tf_op jit(solution)/shard_map/ppermute | solution.py:479
  41.6 10.3 %copy-start.19 = (bf16[16,32,256]{2,1,0:T(8,128)(2,1)}, bf16[16,32,256]{2,1,0:T(8,128)(2,1)S(1)}, u32[]{:S(2)}) copy-start(bf16[16,32,256]{2,1,0:T(8,128)(2,1)S(1)} %collective-permute-done.2.refs_3_) | copy-start | bytes 786436
  44.5 7.4 %copy-start.20 = (bf16[16,32,256]{2,1,0:T(8,128)(2,1)}, bf16[16,32,256]{2,1,0:T(8,128)(2,1)S(1)}, u32[]{:S(2)}) copy-start(bf16[16,32,256]{2,1,0:T(8,128)(2,1)S(1)} %collective-permute-done.1.refs_2_) | copy-start | bytes 786436
  51.4 0.7 copy-start.21
  70.2 3.8 %collective-permute-start.3 = (bf16[16,64,512]{2,1,0:T(8,128)(2,1)}, bf16[16,64,512]{2,1,0:T(8,128)(2,1)S(1)}, u32[]{:S(2)}, u32[]{:S(2)}) collective-permute-start(bf16[16,64,512]{2,1,0:T(8,128)(2,1)} %get-tuple-element.12), channel_id=1, source_target_pairs={{0,1},{1,0},{2,3},{3,2},{4,5},{5,4},{6,7},{7,6},{8,9},{9,8},{10,11... | collective-permute-start | bytes 3145736 | tf_op jit(solution)/shard_map/ppermute | solution.py:412
  74.0 16.8 %copy-start.2 = (bf16[16,64,512]{2,1,0:T(8,128)(2,1)}, bf16[16,64,512]{2,1,0:T(8,128)(2,1)S(1)}, u32[]{:S(2)}) copy-start(bf16[16,64,512]{2,1,0:T(8,128)(2,1)S(1)} %collective-permute-done.3.away_ref) | copy-start | bytes 3145732
  76.0 8.5 %collective-permute-start.6 = (bf16[4,64,512]{2,1,0:T(8,128)(2,1)S(1)}, bf16[4,64,512]{2,1,0:T(8,128)(2,1)S(1)}, u32[]{:S(2)}, u32[]{:S(2)}) collective-permute-start(bf16[4,64,512]{2,1,0:T(8,128)(2,1)S(1)} %get-tuple-element.22), channel_id=1, source_target_pairs={{0,6},{1,7},{2,4},{3,5},{4,2},{5,3},{6,0},{7,1},{8,14},{9,15},{10,... | collective-permute-start | bytes 786440 | tf_op jit(solution)/shard_map/ppermute | solution.py:412
  78.2 12.6 %collective-permute-start.5 = (bf16[4,64,512]{2,1,0:T(8,128)(2,1)S(1)}, bf16[4,64,512]{2,1,0:T(8,128)(2,1)S(1)}, u32[]{:S(2)}, u32[]{:S(2)}) collective-permute-start(bf16[4,64,512]{2,1,0:T(8,128)(2,1)S(1)} %get-tuple-element.23), channel_id=1, source_target_pairs={{0,4},{1,5},{2,6},{3,7},{4,0},{5,1},{6,2},{7,3},{8,12},{9,13},{10,... | collective-permute-start | bytes 786440 | tf_op jit(solution)/shard_map/ppermute | solution.py:412
  78.5 12.4 %collective-permute-start.4 = (bf16[4,64,512]{2,1,0:T(8,128)(2,1)S(1)}, bf16[4,64,512]{2,1,0:T(8,128)(2,1)S(1)}, u32[]{:S(2)}, u32[]{:S(2)}) collective-permute-start(bf16[4,64,512]{2,1,0:T(8,128)(2,1)S(1)} %get-tuple-element.24), channel_id=1, source_target_pairs={{0,2},{1,3},{2,0},{3,1},{4,6},{5,7},{6,4},{7,5},{8,10},{9,11},{10,... | collective-permute-start | bytes 786440 | tf_op jit(solution)/shard_map/ppermute | solution.py:412
  78.7 34.7 %collective-permute-start.11 = (bf16[16,64,512]{2,1,0:T(8,128)(2,1)}, bf16[16,64,512]{2,1,0:T(8,128)(2,1)S(1)}, u32[]{:S(2)}, u32[]{:S(2)}) collective-permute-start(bf16[16,64,512]{2,1,0:T(8,128)(2,1)} %get-tuple-element.14), channel_id=1, source_target_pairs={{0,1},{1,0},{2,3},{3,2},{4,5},{5,4},{6,7},{7,6},{8,9},{9,8},{10,11... | collective-permute-start | bytes 3145736 | tf_op jit(solution)/shard_map/ppermute | solution.py:412
  84.6 6.3 %copy-start.10 = (bf16[4,64,512]{2,1,0:T(8,128)(2,1)}, bf16[4,64,512]{2,1,0:T(8,128)(2,1)S(1)}, u32[]{:S(2)}) copy-start(bf16[4,64,512]{2,1,0:T(8,128)(2,1)S(1)} %collective-permute-done.6.refs_2_) | copy-start | bytes 786436
  90.8 0.7 copy-start.12
  91.5 0.7 copy-start.14
  95.6 17.9 %copy-start = (f32[16,64,512]{2,1,0:T(8,128)S(1)}, f32[16,64,512]{2,1,0:T(8,128)}, u32[]{:S(2)}) copy-start(f32[16,64,512]{2,1,0:T(8,128)} %get-tuple-element.13.keep_ref) | copy-start | bytes 6291460
  95.6 8.5 %collective-permute-start.9 = (bf16[4,64,512]{2,1,0:T(8,128)(2,1)}, bf16[4,64,512]{2,1,0:T(8,128)(2,1)S(1)}, u32[]{:S(2)}, u32[]{:S(2)}) collective-permute-start(bf16[4,64,512]{2,1,0:T(8,128)(2,1)} %settle.2.refs_0_), channel_id=1, source_target_pairs={{0,6},{1,7},{2,4},{3,5},{4,2},{5,3},{6,0},{7,1},{8,14},{9,15},{10,... | collective-permute-start | bytes 786440 | tf_op jit(solution)/shard_map/ppermute | solution.py:412
  96.4 14.3 %collective-permute-start.8 = (bf16[4,64,512]{2,1,0:T(8,128)(2,1)}, bf16[4,64,512]{2,1,0:T(8,128)(2,1)}, u32[]{:S(2)}, u32[]{:S(2)}) collective-permute-start(bf16[4,64,512]{2,1,0:T(8,128)(2,1)} %settle.2.refs_0_), channel_id=1, source_target_pairs={{0,4},{1,5},{2,6},{3,7},{4,0},{5,1},{6,2},{7,3},{8,12},{9,13},{10,... | collective-permute-start | bytes 786440 | tf_op jit(solution)/shard_map/ppermute | solution.py:412
  98.0 12.7 %collective-permute-start.7 = (bf16[4,64,512]{2,1,0:T(8,128)(2,1)}, bf16[4,64,512]{2,1,0:T(8,128)(2,1)}, u32[]{:S(2)}, u32[]{:S(2)}) collective-permute-start(bf16[4,64,512]{2,1,0:T(8,128)(2,1)} %settle.2.refs_0_), channel_id=1, source_target_pairs={{0,2},{1,3},{2,0},{3,1},{4,6},{5,7},{6,4},{7,5},{8,10},{9,11},{10,... | collective-permute-start | bytes 786440 | tf_op jit(solution)/shard_map/ppermute | solution.py:412
  104.1 6.5 %copy-start.7 = (bf16[4,64,512]{2,1,0:T(8,128)(2,1)}, bf16[4,64,512]{2,1,0:T(8,128)(2,1)S(1)}, u32[]{:S(2)}) copy-start(bf16[4,64,512]{2,1,0:T(8,128)(2,1)S(1)} %collective-permute-done.9.refs_3_) | copy-start | bytes 786436
  112.9 3.6 %collective-permute-start.10 = (bf16[16,64,512]{2,1,0:T(8,128)(2,1)}, bf16[16,64,512]{2,1,0:T(8,128)(2,1)}, u32[]{:S(2)}, u32[]{:S(2)}) collective-permute-start(bf16[16,64,512]{2,1,0:T(8,128)(2,1)} %join.2), channel_id=1, source_target_pairs={{0,1},{1,0},{2,3},{3,2},{4,5},{5,4},{6,7},{7,6},{8,9},{9,8},{10,11... | collective-permute-start | bytes 3145736 | tf_op jit(solution)/shard_map/ppermute | solution.py:412
  113.5 14.3 %copy-start.1 = (bf16[16,64,512]{2,1,0:T(8,128)(2,1)}, bf16[16,64,512]{2,1,0:T(8,128)(2,1)S(1)}, u32[]{:S(2)}) copy-start(bf16[16,64,512]{2,1,0:T(8,128)(2,1)S(1)} %collective-permute-done.11.away_ref) | copy-start | bytes 3145732
  113.7 14.1 %collective-permute-start.14 = (bf16[4,64,512]{2,1,0:T(8,128)(2,1)S(1)}, bf16[4,64,512]{2,1,0:T(8,128)(2,1)S(1)}, u32[]{:S(2)}, u32[]{:S(2)}) collective-permute-start(bf16[4,64,512]{2,1,0:T(8,128)(2,1)S(1)} %get-tuple-element.19), channel_id=1, source_target_pairs={{0,6},{1,7},{2,4},{3,5},{4,2},{5,3},{6,0},{7,1},{8,14},{9,15},{10,... | collective-permute-start | bytes 786440 | tf_op jit(solution)/shard_map/ppermute | solution.py:412
  115.0 13.6 %collective-permute-start.13 = (bf16[4,64,512]{2,1,0:T(8,128)(2,1)S(1)}, bf16[4,64,512]{2,1,0:T(8,128)(2,1)S(1)}, u32[]{:S(2)}, u32[]{:S(2)}) collective-permute-start(bf16[4,64,512]{2,1,0:T(8,128)(2,1)S(1)} %get-tuple-element.20), channel_id=1, source_target_pairs={{0,4},{1,5},{2,6},{3,7},{4,0},{5,1},{6,2},{7,3},{8,12},{9,13},{10,... | collective-permute-start | bytes 786440 | tf_op jit(solution)/shard_map/ppermute | solution.py:412
  116.1 12.5 %collective-permute-start.12 = (bf16[4,64,512]{2,1,0:T(8,128)(2,1)S(1)}, bf16[4,64,512]{2,1,0:T(8,128)(2,1)S(1)}, u32[]{:S(2)}, u32[]{:S(2)}) collective-permute-start(bf16[4,64,512]{2,1,0:T(8,128)(2,1)S(1)} %get-tuple-element.21), channel_id=1, source_target_pairs={{0,2},{1,3},{2,0},{3,1},{4,6},{5,7},{6,4},{7,5},{8,10},{9,11},{10,... | collective-permute-start | bytes 786440 | tf_op jit(solution)/shard_map/ppermute | solution.py:412
  127.8 0.8 copy-start.9
  128.6 0.7 copy-start.11
  129.3 0.7 copy-start.13
  133.3 19.4 %collective-permute-start.17 = (bf16[4,64,512]{2,1,0:T(8,128)(2,1)}, bf16[4,64,512]{2,1,0:T(8,128)(2,1)S(1)}, u32[]{:S(2)}, u32[]{:S(2)}) collective-permute-start(bf16[4,64,512]{2,1,0:T(8,128)(2,1)} %settle.3.refs_1_.refs_0_.refs_5_), channel_id=1, source_target_pairs={{0,6},{1,7},{2,4},{3,5},{4,2},{5,3},{6,0},{7,1},{8,14},{9,15},{10,... | collective-permute-start | bytes 786440 | tf_op jit(solution)/shard_map/ppermute | solution.py:412
  134.5 18.2 %collective-permute-start.16 = (bf16[4,64,512]{2,1,0:T(8,128)(2,1)}, bf16[4,64,512]{2,1,0:T(8,128)(2,1)S(1)}, u32[]{:S(2)}, u32[]{:S(2)}) collective-permute-start(bf16[4,64,512]{2,1,0:T(8,128)(2,1)} %settle.3.refs_1_.refs_0_.refs_5_), channel_id=1, source_target_pairs={{0,4},{1,5},{2,6},{3,7},{4,0},{5,1},{6,2},{7,3},{8,12},{9,13},{10,... | collective-permute-start | bytes 786440 | tf_op jit(solution)/shard_map/ppermute | solution.py:412
  135.6 17.1 %collective-permute-start.15 = (bf16[4,64,512]{2,1,0:T(8,128)(2,1)}, bf16[4,64,512]{2,1,0:T(8,128)(2,1)S(1)}, u32[]{:S(2)}, u32[]{:S(2)}) collective-permute-start(bf16[4,64,512]{2,1,0:T(8,128)(2,1)} %settle.3.refs_1_.refs_0_.refs_5_), channel_id=1, source_target_pairs={{0,2},{1,3},{2,0},{3,1},{4,6},{5,7},{6,4},{7,5},{8,10},{9,11},{10,... | collective-permute-start | bytes 786440 | tf_op jit(solution)/shard_map/ppermute | solution.py:412
  138.1 2.4 %collective-permute-start.18 = (f32[128,128]{1,0:T(8,128)}, f32[128,128]{1,0:T(8,128)S(1)}, u32[]{:S(2)}, u32[]{:S(2)}) collective-permute-start(f32[128,128]{1,0:T(8,128)} %gram_part.1), channel_id=1, source_target_pairs={{0,1},{1,0},{2,3},{3,2},{4,5},{5,4},{6,7},{7,6},{8,9},{9,8},{10,11... | collective-permute-start | bytes 196616 | tf_op jit(solution)/shard_map/ppermute | solution.py:412
  141.4 7.5 %collective-permute-start.19 = (f32[128,128]{1,0:T(8,128)S(1)}, f32[128,128]{1,0:T(8,128)S(1)}, u32[]{:S(2)}, u32[]{:S(2)}) collective-permute-start(f32[128,128]{1,0:T(8,128)S(1)} %add.41), channel_id=1, source_target_pairs={{0,2},{1,3},{2,0},{3,1},{4,6},{5,7},{6,4},{7,5},{8,10},{9,11},{10,... | collective-permute-start | bytes 196616 | tf_op jit(solution)/shard_map/ppermute | solution.py:412
  148.9 3.2 %collective-permute-start.20 = (f32[128,128]{1,0:T(8,128)S(1)}, f32[128,128]{1,0:T(8,128)S(1)}, u32[]{:S(2)}, u32[]{:S(2)}) collective-permute-start(f32[128,128]{1,0:T(8,128)S(1)} %add.42), channel_id=1, source_target_pairs={{0,4},{1,5},{2,6},{3,7},{4,0},{5,1},{6,2},{7,3},{8,12},{9,13},{10,... | collective-permute-start | bytes 196616 | tf_op jit(solution)/shard_map/ppermute | solution.py:412
  152.7 6.2 %copy-start.8 = (f32[128,128]{1,0:T(8,128)S(1)}, f32[128,128]{1,0:T(8,128)}, u32[]{:S(2)}) copy-start(f32[128,128]{1,0:T(8,128)} %add.43.refs_4_) | copy-start | bytes 196612
  152.7 0.7 copy-start.4
  152.7 0.8 copy-start.5
  153.5 0.7 copy-start.6
  156.4 7.1 %collective-permute-start.21 = (bf16[16,64,512]{2,1,0:T(8,128)(2,1)}, bf16[16,64,512]{2,1,0:T(8,128)(2,1)S(1)}, u32[]{:S(2)}, u32[]{:S(2)}) collective-permute-start(bf16[16,64,512]{2,1,0:T(8,128)(2,1)} %join.3), channel_id=1, source_target_pairs={{0,1},{1,0},{2,3},{3,2},{4,5},{5,4},{6,7},{7,6},{8,9},{9,8},{10,11... | collective-permute-start | bytes 3145736 | tf_op jit(solution)/shard_map/ppermute | solution.py:412
  158.9 3.8 %collective-permute-start.22 = (f32[128,128]{1,0:T(8,128)S(1)}, f32[128,128]{1,0:T(8,128)S(1)}, u32[]{:S(2)}, u32[]{:S(2)}) collective-permute-start(f32[128,128]{1,0:T(8,128)S(1)} %copy-done.8), channel_id=1, source_target_pairs={{0,8},{8,0},{16,24},{24,16},{1,9},{9,1},{17,25},{25,17},{2,10},{10... | collective-permute-start | bytes 196616 | tf_op jit(solution)/shard_map/ppermute | solution.py:412
  162.7 16.1 %collective-permute-start.23 = (f32[128,128]{1,0:T(8,128)S(1)}, f32[128,128]{1,0:T(8,128)S(1)}, u32[]{:S(2)}, u32[]{:S(2)}) collective-permute-start(f32[128,128]{1,0:T(8,128)S(1)} %add.44), channel_id=1, source_target_pairs={{0,16},{8,24},{16,0},{24,8},{1,17},{9,25},{17,1},{25,9},{2,18},{10... | collective-permute-start | bytes 196616 | tf_op jit(solution)/shard_map/ppermute | solution.py:412
  163.5 1.0 copy-start.3
  175.6 32.5 %collective-permute-start.24 = (bf16[16,32,256]{2,1,0:T(8,128)(2,1)}, bf16[16,32,256]{2,1,0:T(8,128)(2,1)S(1)}, u32[]{:S(2)}, u32[]{:S(2)}) collective-permute-start(bf16[16,32,256]{2,1,0:T(8,128)(2,1)} %get-tuple-element.17), channel_id=1, source_target_pairs={{0,8},{8,16},{16,24},{24,0},{1,9},{9,17},{17,25},{25,1},{2,10},{10... | collective-permute-start | bytes 786440 | tf_op jit(solution)/shard_map/ppermute | solution.py:510
  176.3 31.8 %collective-permute-start.25 = (bf16[16,32,256]{2,1,0:T(8,128)(2,1)}, bf16[16,32,256]{2,1,0:T(8,128)(2,1)S(1)}, u32[]{:S(2)}, u32[]{:S(2)}) collective-permute-start(bf16[16,32,256]{2,1,0:T(8,128)(2,1)} %get-tuple-element.18), channel_id=1, source_target_pairs={{0,16},{8,24},{16,0},{24,8},{1,17},{9,25},{17,1},{25,9},{2,18},{10... | collective-permute-start | bytes 786440 | tf_op jit(solution)/shard_map/ppermute | solution.py:510
  178.8 29.4 %collective-permute-start.26 = (bf16[16,32,256]{2,1,0:T(8,128)(2,1)}, bf16[16,32,256]{2,1,0:T(8,128)(2,1)S(1)}, u32[]{:S(2)}, u32[]{:S(2)}) collective-permute-start(bf16[16,32,256]{2,1,0:T(8,128)(2,1)} %get-tuple-element.15.refs_11_), channel_id=1, source_target_pairs={{0,24},{8,0},{16,8},{24,16},{1,25},{9,1},{17,9},{25,17},{2,26},{10... | collective-permute-start | bytes 786440 | tf_op jit(solution)/shard_map/ppermute | solution.py:510
  208.1 0.7 copy-start.16
  208.2 0.8 copy-start.17
  208.2 0.9 copy-start.18
Sparse Core Ops, SparseCore 0:
  10.1 41.6 all-gather.2
  159.0 40.8 reduce-scatter.1
where the time goes:
time: 219 us; the launch traced here: 218 us
  Pallas kernels  90.9 us (42%)
  waiting for transfers between devices  71.3 us (33%)
  starting transfers between devices  27.1 us (12%)
  between operations  14.2 us (6%)
  local copies, waits for them, and re-layouts  9.02 us (4%)
  other arithmetic  5.74 us (3%)
    ppermute x21, waiting for transfers between devices, to_xor(): return lax.ppermute(x, axis, [(d, d ^ r) for d in range(n)])  40.5 us
    pallas_call x1, Pallas kernels, lag_transform(): pl.pallas_call(lag_kernel, grid=(blocks,), in_specs=[pl.BlockSpec((1, 1,...  26.6 us
    pallas_call x2, Pallas kernels, corange_part(): pl.pallas_call(functools.partial(corange_kernel, n_in, n_out, len(before)...  22.4 us
    reduce_scatter x1, waiting for transfers between devices, shards(): lax.psum_scatter(whole, 'out', scatter_dimension=0, tiled=True)  20.5 us
    ppermute x21, starting transfers between devices, to_xor(): return lax.ppermute(x, axis, [(d, d ^ r) for d in range(n)])  20 us
    pallas_call x1, Pallas kernels, sketch_part(): pl.pallas_call(functools.partial(sketch_kernel, len(probes), n_out, n_in)...  18.1 us
    ppermute x3, waiting for transfers between devices, shards(): lax.ppermute(own, 'out', [((k + d) % n_out, k) for k in range(n_out)])  9.89 us
    pallas_call x1, Pallas kernels, finish(): pl.pallas_call(functools.partial(finish_kernel, n_out, n_in), in_specs=[p...  8.17 us
  transfers between devices with their start and end apart: 29, of which 14 were waited for; matrix products, arithmetic and copies ran while one was open for 2% of the time, Pallas kernels for 30%

commit v1 on v0

--- a/solution.py
+++ b/solution.py
@@ -198,6 +198,9 @@
 
 def any_specs(arrays):
     return [pl.BlockSpec(memory_space=pl.ANY) for _ in arrays]
+
+
+NO_COST = pl.CostEstimate(flops=0, bytes_accessed=1, transcendentals=0)
 
 
 def product_cost(p, m, extra):
@@ -311,7 +314,7 @@
             pltpu.SemaphoreType.DMA((MARKOV_PARTS, F // CHUNK)),
         ],
         compiler_params=pltpu.CompilerParams(vmem_limit_bytes=VMEM),
-        cost_estimate=product_cost(p, m, 0),
+        cost_estimate=product_cost(p, m, 0) if whole else NO_COST,
         name="corange_part",
     )(place, fwd, back, *pieces, *hankel, *before)
 
@@ -326,26 +329,32 @@
 
 def gram_kernel(n_out, place_ref, *refs):
     k_refs, (gram_ref, both_parts) = refs[:PARTS], refs[PARTS:]
-    total = jnp.zeros(gram_ref.shape, f32)
-    for i in range(k_refs[0].shape[0]):
+    gram_ref[...] = jnp.zeros(gram_ref.shape, f32)
+
+    def body(i, _):
         for q, ref in enumerate(k_refs):
             in_order(ref[i], both_parts, q, place_ref[0], n_out)
         x = both_parts[...].astype(bf16)
-        total += lax.dot_general(x, x, (((1,), (1,)), ((), ())), preferred_element_type=f32)
-    gram_ref[...] = total
-
-
-def gram_part(own, place, n_out):
-    _, s_count, p = own[0].shape
+        gram_ref[...] += lax.dot_general(
+            x, x, (((1,), (1,)), ((), ())), preferred_element_type=f32
+        )
+        return 0
+
+    lax.fori_loop(0, k_refs[0].shape[0], body, 0)
+
+
+def gram_part(joined, place, n_out):
+    _, s_count, p = joined[0].shape
     s_count *= PARTS
     return pl.pallas_call(
         functools.partial(gram_kernel, n_out),
-        in_specs=[pl.BlockSpec(memory_space=pltpu.SMEM)] + vmem_specs(own),
+        in_specs=[pl.BlockSpec(memory_space=pltpu.SMEM)] + vmem_specs(joined),
         out_specs=pl.BlockSpec(memory_space=pltpu.VMEM),
         out_shape=jax.ShapeDtypeStruct((s_count, s_count), f32),
         scratch_shapes=[pltpu.VMEM((s_count, p), f32)],
+        compiler_params=pltpu.CompilerParams(vmem_limit_bytes=VMEM),
         name="gram_part",
-    )(place, *own)
+    )(place, *joined)
 
 
 def total_kernel(n, *refs):
@@ -398,7 +407,7 @@
         scratch_shapes=[pltpu.VMEM((PARTS * s_count, p), f32)],
         compiler_params=pltpu.CompilerParams(vmem_limit_bytes=VMEM),
         cost_estimate=pl.CostEstimate(
-            flops=0, bytes_accessed=16 * R * p * s_count, transcendentals=0
+            flops=0, bytes_accessed=64 * R * p * s_count, transcendentals=0
         ),
         name="finish",
     )(place, *flat, *after)
@@ -410,6 +419,19 @@
 
 def to_xor(x, axis, r, n):
     return lax.ppermute(x, axis, [(d, d ^ r) for d in range(n)])
+
+
+def sum_by_xor(x, axis, n):
+    step = 1
+    while step < n:
+        if 4 * step <= n:
+            a, b, c = [to_xor(x, axis, k * step, n) for k in (1, 2, 3)]
+            x = (x + a) + (b + c)
+            step *= 4
+        else:
+            x = x + to_xor(x, axis, step, n)
+            step *= 2
+    return x
 
 
 def settle_kernel(n, keep_ref, away_ref, *refs):
@@ -420,13 +442,14 @@
 
 
 def settle(keep, away, arrived, before):
-    block = pl.BlockSpec((1, *keep.shape[1:]), lambda i: (i, 0, 0))
+    block = pl.BlockSpec(arrived[0].shape, lambda i: (0, 0, 0))
     return pl.pallas_call(
         functools.partial(settle_kernel, len(arrived)),
-        grid=(arrived[0].shape[0],),
+        grid=(1,),
         in_specs=[block] * (2 + len(arrived)) + any_specs(before),
         out_specs=block,
         out_shape=jax.ShapeDtypeStruct(arrived[0].shape, bf16),
+        compiler_params=pltpu.CompilerParams(vmem_limit_bytes=VMEM),
         cost_estimate=pl.CostEstimate(
             flops=0, bytes_accessed=8 * arrived[0].size, transcendentals=0
         ),
@@ -483,16 +506,13 @@
 
     raws = sketch_part(gathered, hankel, probe_mat, raw_mat, place, n_out, n_in)
     met = [meet(raws[2 * q], raws[2 * q + 1], n_in) for q in range(PARTS)]
-    owns, sums, summed, before = [], [], [], []
-    for q, x in enumerate(met):
-        owns.append(settle(*x, before))
-        mine = spread(owns[q], n_in)
+    owns = [settle(*x, []) for x in met]
+    joined, sums, summed, before = [], [], [], owns[-1:]
+    for q, own in enumerate(owns):
+        mine = spread(own, n_in)
+        joined.append(join(mine, before if q else []))
+        sums.append(mine + [to_xor(joined[q], "in", 1, n_in)])
         last = q == PARTS - 1
-        gram = [gram_part(owns, place, n_out)] if last else []
-        if last:
-            for bit in range(n_in.bit_length() - 1):
-                gram = [gram[0] + to_xor(gram[0], "in", 1 << bit, n_in)]
-        sums.append(mine + [to_xor(join(mine, gram), "in", 1, n_in)])
         cor = corange_part(
             sums[q], hankel, sketch_mat, cor_mat, place, n_out, n_in, before, not last
         )
@@ -501,15 +521,13 @@
             whole = cor[0].reshape((-1,) + cor[0].shape[2:])
             summed.append(lax.psum_scatter(whole, "out", scatter_dimension=0, tiled=True))
 
-    (gram,) = gram
-    for bit in range(n_out.bit_length() - 1):
-        gram = gram + to_xor(gram, "out", 1 << bit, n_out)
-    gram_matrix = gram / (R * OUTPUT_CHANNELS)
-
     arrived = [
         lax.ppermute(cor[d], "out", [(k, (k + d) % n_out) for k in range(n_out)])
         for d in range(1, n_out)
     ]
+    gram = gram_part(joined, place, n_out)
+    gram = sum_by_xor(gram + to_xor(gram, "in", 1, n_in), "out", n_out)
+    gram_matrix = gram / (R * OUTPUT_CHANNELS)
     sketch = finish(sums, place, [*summed, *before, gram_matrix], n_out, n_in)
     corange = total_corange(summed, cor[0], arrived, sketch)
     return (sketch, corange, gram_matrix)

time: 219 us -> 221 us (level)
  waiting for transfers between devices: 71.3 us -> 77 us
  starting transfers between devices: 27.1 us -> 23 us
    reduce_scatter x1, waiting for transfers between devices: 20.5 us -> 0.01 us  [shards(): lax.psum_scatter(whole, 'out', scatter_dimension=0, tiled=True)]
    ppermute x3, waiting for transfers between devices: 0.01 us -> 14.1 us  [shards(): lax.ppermute(cor[d], 'out', [(k, (k + d) % n_out) for k in range(n_out)])]
    ppermute x21 -> x20, waiting for transfers between devices: 40.5 us -> 52.6 us  [to_xor(): return lax.ppermute(x, axis, [(d, d ^ r) for d in range(n)])]
    ppermute x21 -> x20, starting transfers between devices: 20 us -> 16 us  [to_xor(): return lax.ppermute(x, axis, [(d, d ^ r) for d in range(n)])]
    pallas_call x1, Pallas kernels: 2.16 us -> 5.7 us  [gram_part(): pl.pallas_call(functools.partial(gram_kernel, n_out), in_specs=[pl.BlockS...]
    pallas_call x2, Pallas kernels: 6.66 us -> 4.37 us  [settle(): pl.pallas_call(functools.partial(settle_kernel, len(arrived)), grid=(1,),...]
  transfers between devices with their start and end apart: 29 -> 28, of which waited for: 14 -> 15; matrix products, arithmetic and copies ran while one was open for 2% -> 3% of each run, Pallas kernels for 30% -> 27%
where the time goes in v1:
time: 221 us; the launch traced here: 220 us
  Pallas kernels  92.2 us (42%)
  waiting for transfers between devices  77 us (35%)
  starting transfers between devices  23 us (10%)
  between operations  14.2 us (6%)
  local copies, waits for them, and re-layouts  8.75 us (4%)
  other arithmetic  5.09 us (2%)
    ppermute x20, waiting for transfers between devices, to_xor(): return lax.ppermute(x, axis, [(d, d ^ r) for d in range(n)])  52.6 us
    pallas_call x1, Pallas kernels, lag_transform(): pl.pallas_call(lag_kernel, grid=(blocks,), in_specs=[pl.BlockSpec((1, 1,...  26.6 us
    pallas_call x2, Pallas kernels, corange_part(): pl.pallas_call(functools.partial(corange_kernel, n_in, n_out, len(before)...  22.4 us
    pallas_call x1, Pallas kernels, sketch_part(): pl.pallas_call(functools.partial(sketch_kernel, len(probes), n_out, n_in)...  18 us
    ppermute x20, starting transfers between devices, to_xor(): return lax.ppermute(x, axis, [(d, d ^ r) for d in range(n)])  16 us
    ppermute x3, waiting for transfers between devices, shards(): lax.ppermute(cor[d], 'out', [(k, (k + d) % n_out) for k in range(n_out)])  14.1 us
    ppermute x3, waiting for transfers between devices, shards(): lax.ppermute(own, 'out', [((k + d) % n_out, k) for k in range(n_out)])  9.88 us
    pallas_call x1, Pallas kernels, finish(): pl.pallas_call(functools.partial(finish_kernel, n_out, n_in), in_specs=[p...  8.17 us
  transfers between devices with their start and end apart: 28, of which 15 were waited for; matrix products, arithmetic and copies ran while one was open for 3% of the time, Pallas kernels for 27%

profile of v1, /device:TPU:9, one launch (start us, length us, event | category | flops | bytes accessed | tf_op | source)
XLA Modules:
  0.0 220.2 jit_solution(11967931453254225555)
XLA Ops:
  7.2 1.8 fusion
  9.1 1.3 collective-permute-start.2
  10.4 1.1 collective-permute-start.1
  11.5 1.4 collective-permute-start
  12.9 0.7 convert_element_type.50
  13.6 0.7 broadcast_in_dim.4
  14.3 26.6 %lag_transform.1.refs_5_ = bf16[32,512,512]{2,1,0:T(8,128)(2,1)} custom-call(f32[8,1,256]{2,1,0:T(1,128)} %bitcast.6, bf16[1024,512]{1,0:T(8,128)(2,1)} %constant.21.clone.mat_ref, bf16[63,512,256]{2,1,0:T(8,128)(2,1)} %x_ref.1), custom_call_target="tpu_custom_call" | custom-call | flops 8589934592 | bytes 16777216 | tf_op jit(solution)/shard_map/lag_transform/pallas_call | solution.py:79
  40.9 0.7 pad_add_fusion.place_ref
  41.6 2.9 %collective-permute-done.1.refs_2_ = bf16[16,32,256]{2,1,0:T(8,128)(2,1)S(1)} collective-permute-done((bf16[16,32,256]{2,1,0:T(8,128)(2,1)S(1)}, bf16[16,32,256]{2,1,0:T(8,128)(2,1)S(1)}, u32[]{:S(2)}, u32[]{:S(2)}) %collective-permute-start.1) | collective-permute-done | bytes 262176 | tf_op jit(solution)/shard_map/ppermute | solution.py:502
  44.5 6.9 %collective-permute-done.refs_1_ = bf16[16,32,256]{2,1,0:T(8,128)(2,1)S(1)} collective-permute-done((bf16[16,32,256]{2,1,0:T(8,128)(2,1)S(1)}, bf16[16,32,256]{2,1,0:T(8,128)(2,1)S(1)}, u32[]{:S(2)}, u32[]{:S(2)}) %collective-permute-start) | collective-permute-done | bytes 262176 | tf_op jit(solution)/shard_map/ppermute | solution.py:502
  51.4 0.4 all-gather.3.cloned.1.call-done
  51.9 0.3 copy-done.21
  52.2 18.0 %sketch_part.1 = (f32[16,64,512]{2,1,0:T(8,128)}, bf16[16,64,512]{2,1,0:T(8,128)(2,1)}, f32[16,64,512]{2,1,0:T(8,128)}, bf16[16,64,512]{2,1,0:T(8,128)(2,1)}) custom-call(s32[2]{0:T(128)} %pad_add_fusion.place_ref, bf16[1024,256]{1,0:T(8,128)(2,1)} %constant.22.clone.fwd_ref, bf16[512,512]{1,0:T(8,128)(2,1)} %constant.24.clone.back_ref, ...), custom_call_target="tpu_custom_call" | custom-call | flops 8589934592 | bytes 16777216 | tf_op jit(solution)/shard_map/sketch_part/pallas_call | solution.py:216
  70.2 1.3 collective-permute-start.3
  71.6 2.4 %collective-permute-done.3.away_ref = bf16[16,64,512]{2,1,0:T(8,128)(2,1)S(1)} collective-permute-done((bf16[16,64,512]{2,1,0:T(8,128)(2,1)}, bf16[16,64,512]{2,1,0:T(8,128)(2,1)S(1)}, u32[]{:S(2)}, u32[]{:S(2)}) %collective-permute-start.3) | collective-permute-done | bytes 1048608 | tf_op jit(solution)/shard_map/ppermute | solution.py:421
  74.0 2.0 add_convert_fusion.3
  76.0 2.2 %collective-permute-start.6 = (bf16[4,64,512]{2,1,0:T(8,128)(2,1)S(1)}, bf16[4,64,512]{2,1,0:T(8,128)(2,1)S(1)}, u32[]{:S(2)}, u32[]{:S(2)}) collective-permute-start(bf16[4,64,512]{2,1,0:T(8,128)(2,1)S(1)} %get-tuple-element.22), channel_id=1, source_target_pairs={{0,6},{1,7},{2,4},{3,5},{4,2},{5,3},{6,0},{7,1},{8,14},{9,15},{10,... | collective-permute-start | bytes 786440 | tf_op jit(solution)/shard_map/ppermute | solution.py:421
  78.5 0.3 collective-permute-start.4
  78.8 5.8 %collective-permute-done.6.refs_2_ = bf16[4,64,512]{2,1,0:T(8,128)(2,1)S(1)} collective-permute-done((bf16[4,64,512]{2,1,0:T(8,128)(2,1)S(1)}, bf16[4,64,512]{2,1,0:T(8,128)(2,1)S(1)}, u32[]{:S(2)}, u32[]{:S(2)}) %collective-permute-start.6) | collective-permute-done | bytes 262176 | tf_op jit(solution)/shard_map/ppermute | solution.py:421
  84.6 6.3 %collective-permute-done.5.refs_1_ = bf16[4,64,512]{2,1,0:T(8,128)(2,1)S(1)} collective-permute-done((bf16[4,64,512]{2,1,0:T(8,128)(2,1)S(1)}, bf16[4,64,512]{2,1,0:T(8,128)(2,1)S(1)}, u32[]{:S(2)}, u32[]{:S(2)}) %collective-permute-start.5) | collective-permute-done | bytes 262176 | tf_op jit(solution)/shard_map/ppermute | solution.py:421
  90.9 0.7 copy-done.11
  91.6 0.7 copy-done.13
  92.3 2.2 settle.2.refs_0_
  94.5 0.8 collective-permute-start.9
  95.2 1.6 collective-permute-start.8
  96.8 0.3 collective-permute-start.7
  97.1 5.9 %collective-permute-done.9.refs_3_ = bf16[4,64,512]{2,1,0:T(8,128)(2,1)S(1)} collective-permute-done((bf16[4,64,512]{2,1,0:T(8,128)(2,1)}, bf16[4,64,512]{2,1,0:T(8,128)(2,1)S(1)}, u32[]{:S(2)}, u32[]{:S(2)}) %collective-permute-start.9) | collective-permute-done | bytes 262176 | tf_op jit(solution)/shard_map/ppermute | solution.py:421
  103.0 6.5 %collective-permute-done.8.refs_2_ = bf16[4,64,512]{2,1,0:T(8,128)(2,1)} collective-permute-done((bf16[4,64,512]{2,1,0:T(8,128)(2,1)}, bf16[4,64,512]{2,1,0:T(8,128)(2,1)}, u32[]{:S(2)}, u32[]{:S(2)}) %collective-permute-start.8) | collective-permute-done | bytes 262176 | tf_op jit(solution)/shard_map/ppermute | solution.py:421
  109.5 2.2 %join.2.refs_0_ = bf16[16,64,512]{2,1,0:T(8,128)(2,1)} custom-call(bf16[4,64,512]{2,1,0:T(8,128)(2,1)} %settle.2.refs_0_, bf16[4,64,512]{2,1,0:T(8,128)(2,1)} %collective-permute-done.7.refs_1_, bf16[4,64,512]{2,1,0:T(8,128)(2,1)} %collective-permute-done.8.refs_2_, bf16[4,64,512]{2,1,0:T(8,128)(2,1)} %copy-done.8), custom_call_target="tpu_custom_call" | custom-call | tf_op jit(solution)/shard_map/join/pallas_call | solution.py:482
  111.7 0.6 collective-permute-start.10
  112.6 1.2 collective-permute-start.14
  113.8 1.1 collective-permute-start.13
  115.0 0.4 collective-permute-start.12
  115.3 6.2 %collective-permute-done.14.refs_2_ = bf16[4,64,512]{2,1,0:T(8,128)(2,1)S(1)} collective-permute-done((bf16[4,64,512]{2,1,0:T(8,128)(2,1)S(1)}, bf16[4,64,512]{2,1,0:T(8,128)(2,1)S(1)}, u32[]{:S(2)}, u32[]{:S(2)}) %collective-permute-start.14) | collective-permute-done | bytes 262176 | tf_op jit(solution)/shard_map/ppermute | solution.py:421
  121.5 5.9 %collective-permute-done.13.refs_1_ = bf16[4,64,512]{2,1,0:T(8,128)(2,1)S(1)} collective-permute-done((bf16[4,64,512]{2,1,0:T(8,128)(2,1)S(1)}, bf16[4,64,512]{2,1,0:T(8,128)(2,1)S(1)}, u32[]{:S(2)}, u32[]{:S(2)}) %collective-permute-start.13) | collective-permute-done | bytes 262176 | tf_op jit(solution)/shard_map/ppermute | solution.py:421
  127.4 0.7 copy-done.12
  128.2 0.7 copy-done.14
  128.9 2.2 settle.3.refs_6_.refs_0_.refs_5_
  131.0 11.4 %corange_part.2.refs_4_.refs_6_ = bf16[4,16,32,256]{3,2,1,0:T(8,128)(2,1)} custom-call(s32[2]{0:T(128)} %pad_add_fusion.place_ref, bf16[1024,256]{1,0:T(8,128)(2,1)} %constant.23.clone.fwd_ref, bf16[512,512]{1,0:T(8,128)(2,1)} %constant.25.clone.back_ref, bf16[4,64,512]{2,1,0:T(8,128)(2,1)} %settle.2.refs_0_, ...), custom_call_target="tpu_custom_call" | custom-call | flops 8589934592 | bytes 16777216 | tf_op jit(solution)/shard_map/corange_part/pallas_call | solution.py:302
  142.5 1.2 collective-permute-start.17
  143.7 1.1 collective-permute-start.16
  144.8 0.3 collective-permute-start.15
  145.2 5.7 %collective-permute-done.17.refs_3_.refs_8_ = bf16[4,64,512]{2,1,0:T(8,128)(2,1)S(1)} collective-permute-done((bf16[4,64,512]{2,1,0:T(8,128)(2,1)S(1)}, bf16[4,64,512]{2,1,0:T(8,128)(2,1)S(1)}, u32[]{:S(2)}, u32[]{:S(2)}) %collective-permute-start.17) | collective-permute-done | bytes 262176 | tf_op jit(solution)/shard_map/ppermute | solution.py:421
  150.9 6.5 %collective-permute-done.16.refs_2_.refs_7_ = bf16[4,64,512]{2,1,0:T(8,128)(2,1)S(1)} collective-permute-done((bf16[4,64,512]{2,1,0:T(8,128)(2,1)S(1)}, bf16[4,64,512]{2,1,0:T(8,128)(2,1)S(1)}, u32[]{:S(2)}, u32[]{:S(2)}) %collective-permute-start.16) | collective-permute-done | bytes 262176 | tf_op jit(solution)/shard_map/ppermute | solution.py:421
  157.4 0.7 copy-done.6
  158.1 0.7 copy-done.7
  158.8 2.3 %join.3.refs_1_ = bf16[16,64,512]{2,1,0:T(8,128)(2,1)} custom-call(bf16[4,64,512]{2,1,0:T(8,128)(2,1)} %settle.3.refs_6_.refs_0_.refs_5_, bf16[4,64,512]{2,1,0:T(8,128)(2,1)} %copy-done.7, bf16[4,64,512]{2,1,0:T(8,128)(2,1)} %copy-done.6, bf16[4,64,512]{2,1,0:T(8,128)(2,1)} %copy-done.5, bf16[4,16,32,256]{3,2,1,0:T(8,128)(2,1)} %corange_part.2.refs_4_.refs_6_), custom_call_target="tpu_custom_call" | custom-call | tf_op jit(solution)/shard_map/join/pallas_call | solution.py:482
  161.0 0.4 collective-permute-start.18
  161.4 5.7 %gram_part.1 = f32[128,128]{1,0:T(8,128)} custom-call(s32[2]{0:T(128)} %pad_add_fusion.place_ref, bf16[16,64,512]{2,1,0:T(8,128)(2,1)} %join.2.refs_0_, bf16[16,64,512]{2,1,0:T(8,128)(2,1)} %join.3.refs_1_), custom_call_target="tpu_custom_call" | custom-call | tf_op jit(solution)/shard_map/gram_part/pallas_call | solution.py:349
  167.2 1.3 collective-permute-done.19
  168.6 0.9 add.38
  169.4 0.7 collective-permute-start.22
  170.3 1.9 collective-permute-start.20
  172.2 1.0 copy-done.2
  173.1 11.1 %corange_part.3 = (f32[16,32,256]{2,1,0:T(8,128)}, bf16[16,32,256]{2,1,0:T(8,128)(2,1)}, bf16[16,32,256]{2,1,0:T(8,128)(2,1)}, bf16[16,32,256]{2,1,0:T(8,128)(2,1)}) custom-call(s32[2]{0:T(128)} %pad_add_fusion.place_ref, bf16[1024,256]{1,0:T(8,128)(2,1)} %constant.23.clone.fwd_ref, bf16[512,512]{1,0:T(8,128)(2,1)} %constant.25.clone.back_ref, ...), custom_call_target="tpu_custom_call" | custom-call | bytes 1 | tf_op jit(solution)/shard_map/corange_part/pallas_call | solution.py:302
  184.2 0.7 collective-permute-start.23
  184.8 1.5 collective-permute-start.24
  186.3 1.0 collective-permute-start.25
  187.3 0.6 add_multiply_fusion.refs_12_
  187.9 8.2 %finish.1.refs_5_ = bf16[32,512,128]{2,1,0:T(8,128)(2,1)} custom-call(s32[2]{0:T(128)} %pad_add_fusion.place_ref, bf16[4,64,512]{2,1,0:T(8,128)(2,1)} %settle.2.refs_0_, bf16[4,64,512]{2,1,0:T(8,128)(2,1)} %collective-permute-done.7.refs_1_, bf16[4,64,512]{2,1,0:T(8,128)(2,1)} %collective-permute-done.8.refs_2_, bf16[4,64,512]{2,1,0:T(8,128)(2,1)} %copy-done.8, ...), custom_call_target="tpu_custom_call" | custom-call | bytes 67108864 | tf_op jit(solution)/shard_map/finish/pallas_call | solution.py:402
  196.1 10.5 %collective-permute-done.24.refs_3_ = bf16[16,32,256]{2,1,0:T(8,128)(2,1)S(1)} collective-permute-done((bf16[16,32,256]{2,1,0:T(8,128)(2,1)}, bf16[16,32,256]{2,1,0:T(8,128)(2,1)S(1)}, u32[]{:S(2)}, u32[]{:S(2)}) %collective-permute-start.24) | collective-permute-done | bytes 262176 | tf_op jit(solution)/shard_map/ppermute | solution.py:525
  206.6 3.6 %collective-permute-done.25.refs_4_ = bf16[16,32,256]{2,1,0:T(8,128)(2,1)S(1)} collective-permute-done((bf16[16,32,256]{2,1,0:T(8,128)(2,1)}, bf16[16,32,256]{2,1,0:T(8,128)(2,1)S(1)}, u32[]{:S(2)}, u32[]{:S(2)}) %collective-permute-start.25) | collective-permute-done | bytes 262176 | tf_op jit(solution)/shard_map/ppermute | solution.py:525
  210.2 0.7 copy-done.18
  210.9 2.4 %total_corange.1 = f32[32,32,256]{2,1,0:T(8,128)} custom-call(bf16[16,32,256]{2,1,0:T(8,128)(2,1)} %reduce-scatter.2.cloned.1.call-done.refs_10_.refs_0_, f32[16,32,256]{2,1,0:T(8,128)} %get-tuple-element.16.refs_1_, bf16[16,32,256]{2,1,0:T(8,128)(2,1)} %copy-done.16, bf16[16,32,256]{2,1,0:T(8,128)(2,1)} %copy-done.17, bf16[16,32,256]{2,1,0:T(8,128)(2,1)} %copy-done.18, ...), custom_call_target="tpu_custom_call" | custom-call | tf_op jit(solution)/shard_map/total_corange/pallas_call | solution.py:373
  (58 shorter events, 1.1 us)
Async XLA Ops:
  7.2 44.7 %all-gather.3.cloned.1.call-start = ((), (), s32[]{:S(2)}) async-start(), calls=%async_computation.2 | async-start | bytes 1310720 | tf_op jit(solution)/shard_map/all_gather | solution.py:504
  9.0 31.9 %copy-start.15 = (bf16[16,32,256]{2,1,0:T(8,128)(2,1)}, bf16[16,32,256]{2,1,0:T(8,128)(2,1)S(1)}, u32[]{:S(2)}) copy-start(bf16[16,32,256]{2,1,0:T(8,128)(2,1)S(1)} %get-tuple-element.26.refs_0_) | copy-start | bytes 786436
  9.0 178.9 %reduce-scatter.2.cloned.1.call-start = ((), (), s32[]{:S(2)}) async-start(), calls=%async_computation.1 | async-start | bytes 1310720 | tf_op jit(solution)/shard_map/reduce_scatter | solution.py:522
  9.1 32.5 %collective-permute-start.2 = (bf16[16,32,256]{2,1,0:T(8,128)(2,1)S(1)}, bf16[16,32,256]{2,1,0:T(8,128)(2,1)S(1)}, u32[]{:S(2)}, u32[]{:S(2)}) collective-permute-start(bf16[16,32,256]{2,1,0:T(8,128)(2,1)S(1)} %get-tuple-element.26.refs_0_), channel_id=1, source_target_pairs={{24,0},{0,8},{8,16},{16,24},{25,1},{1,9},{9,17},{17,25},{26,2},{2,... | collective-permute-start | bytes 786440 | tf_op jit(solution)/shard_map/ppermute | solution.py:502
  10.4 34.1 %collective-permute-start.1 = (bf16[16,32,256]{2,1,0:T(8,128)(2,1)S(1)}, bf16[16,32,256]{2,1,0:T(8,128)(2,1)S(1)}, u32[]{:S(2)}, u32[]{:S(2)}) collective-permute-start(bf16[16,32,256]{2,1,0:T(8,128)(2,1)S(1)} %get-tuple-element.26.refs_0_), channel_id=1, source_target_pairs={{16,0},{24,8},{0,16},{8,24},{17,1},{25,9},{1,17},{9,25},{18,2},{26... | collective-permute-start | bytes 786440 | tf_op jit(solution)/shard_map/ppermute | solution.py:502
  11.5 40.0 %collective-permute-start = (bf16[16,32,256]{2,1,0:T(8,128)(2,1)S(1)}, bf16[16,32,256]{2,1,0:T(8,128)(2,1)S(1)}, u32[]{:S(2)}, u32[]{:S(2)}) collective-permute-start(bf16[16,32,256]{2,1,0:T(8,128)(2,1)S(1)} %get-tuple-element.26.refs_0_), channel_id=1, source_target_pairs={{8,0},{16,8},{24,16},{0,24},{9,1},{17,9},{25,17},{1,25},{10,2},{18... | collective-permute-start | bytes 786440 | tf_op jit(solution)/shard_map/ppermute | solution.py:502
  41.6 10.3 %copy-start.19 = (bf16[16,32,256]{2,1,0:T(8,128)(2,1)}, bf16[16,32,256]{2,1,0:T(8,128)(2,1)S(1)}, u32[]{:S(2)}) copy-start(bf16[16,32,256]{2,1,0:T(8,128)(2,1)S(1)} %collective-permute-done.2.refs_3_) | copy-start | bytes 786436
  44.5 7.4 %copy-start.20 = (bf16[16,32,256]{2,1,0:T(8,128)(2,1)}, bf16[16,32,256]{2,1,0:T(8,128)(2,1)S(1)}, u32[]{:S(2)}) copy-start(bf16[16,32,256]{2,1,0:T(8,128)(2,1)S(1)} %collective-permute-done.1.refs_2_) | copy-start | bytes 786436
  51.4 0.7 copy-start.21
  70.2 3.8 %collective-permute-start.3 = (bf16[16,64,512]{2,1,0:T(8,128)(2,1)}, bf16[16,64,512]{2,1,0:T(8,128)(2,1)S(1)}, u32[]{:S(2)}, u32[]{:S(2)}) collective-permute-start(bf16[16,64,512]{2,1,0:T(8,128)(2,1)} %get-tuple-element.12), channel_id=1, source_target_pairs={{0,1},{1,0},{2,3},{3,2},{4,5},{5,4},{6,7},{7,6},{8,9},{9,8},{10,11... | collective-permute-start | bytes 3145736 | tf_op jit(solution)/shard_map/ppermute | solution.py:421
  71.5 40.8 %collective-permute-start.11 = (bf16[16,64,512]{2,1,0:T(8,128)(2,1)}, bf16[16,64,512]{2,1,0:T(8,128)(2,1)S(1)}, u32[]{:S(2)}, u32[]{:S(2)}) collective-permute-start(bf16[16,64,512]{2,1,0:T(8,128)(2,1)} %get-tuple-element.14), channel_id=1, source_target_pairs={{0,1},{1,0},{2,3},{3,2},{4,5},{5,4},{6,7},{7,6},{8,9},{9,8},{10,11... | collective-permute-start | bytes 3145736 | tf_op jit(solution)/shard_map/ppermute | solution.py:421
  74.0 16.8 %copy-start.4 = (bf16[16,64,512]{2,1,0:T(8,128)(2,1)}, bf16[16,64,512]{2,1,0:T(8,128)(2,1)S(1)}, u32[]{:S(2)}) copy-start(bf16[16,64,512]{2,1,0:T(8,128)(2,1)S(1)} %collective-permute-done.3.away_ref) | copy-start | bytes 3145732
  76.0 8.5 %collective-permute-start.6 = (bf16[4,64,512]{2,1,0:T(8,128)(2,1)S(1)}, bf16[4,64,512]{2,1,0:T(8,128)(2,1)S(1)}, u32[]{:S(2)}, u32[]{:S(2)}) collective-permute-start(bf16[4,64,512]{2,1,0:T(8,128)(2,1)S(1)} %get-tuple-element.22), channel_id=1, source_target_pairs={{0,6},{1,7},{2,4},{3,5},{4,2},{5,3},{6,0},{7,1},{8,14},{9,15},{10,... | collective-permute-start | bytes 786440 | tf_op jit(solution)/shard_map/ppermute | solution.py:421
  78.2 12.6 %collective-permute-start.5 = (bf16[4,64,512]{2,1,0:T(8,128)(2,1)S(1)}, bf16[4,64,512]{2,1,0:T(8,128)(2,1)S(1)}, u32[]{:S(2)}, u32[]{:S(2)}) collective-permute-start(bf16[4,64,512]{2,1,0:T(8,128)(2,1)S(1)} %get-tuple-element.23), channel_id=1, source_target_pairs={{0,4},{1,5},{2,6},{3,7},{4,0},{5,1},{6,2},{7,3},{8,12},{9,13},{10,... | collective-permute-start | bytes 786440 | tf_op jit(solution)/shard_map/ppermute | solution.py:421
  78.5 12.4 %collective-permute-start.4 = (bf16[4,64,512]{2,1,0:T(8,128)(2,1)S(1)}, bf16[4,64,512]{2,1,0:T(8,128)(2,1)S(1)}, u32[]{:S(2)}, u32[]{:S(2)}) collective-permute-start(bf16[4,64,512]{2,1,0:T(8,128)(2,1)S(1)} %get-tuple-element.24), channel_id=1, source_target_pairs={{0,2},{1,3},{2,0},{3,1},{4,6},{5,7},{6,4},{7,5},{8,10},{9,11},{10,... | collective-permute-start | bytes 786440 | tf_op jit(solution)/shard_map/ppermute | solution.py:421
  84.6 6.3 %copy-start.9 = (bf16[4,64,512]{2,1,0:T(8,128)(2,1)}, bf16[4,64,512]{2,1,0:T(8,128)(2,1)S(1)}, u32[]{:S(2)}) copy-start(bf16[4,64,512]{2,1,0:T(8,128)(2,1)S(1)} %collective-permute-done.6.refs_2_) | copy-start | bytes 786436
  90.8 0.7 copy-start.11
  91.6 0.7 copy-start.13
  94.5 17.9 %copy-start = (f32[16,64,512]{2,1,0:T(8,128)S(1)}, f32[16,64,512]{2,1,0:T(8,128)}, u32[]{:S(2)}) copy-start(f32[16,64,512]{2,1,0:T(8,128)} %get-tuple-element.13.keep_ref) | copy-start | bytes 6291460
  94.5 8.5 %collective-permute-start.9 = (bf16[4,64,512]{2,1,0:T(8,128)(2,1)}, bf16[4,64,512]{2,1,0:T(8,128)(2,1)S(1)}, u32[]{:S(2)}, u32[]{:S(2)}) collective-permute-start(bf16[4,64,512]{2,1,0:T(8,128)(2,1)} %settle.2.refs_0_), channel_id=1, source_target_pairs={{0,6},{1,7},{2,4},{3,5},{4,2},{5,3},{6,0},{7,1},{8,14},{9,15},{10,... | collective-permute-start | bytes 786440 | tf_op jit(solution)/shard_map/ppermute | solution.py:421
  95.2 14.3 %collective-permute-start.8 = (bf16[4,64,512]{2,1,0:T(8,128)(2,1)}, bf16[4,64,512]{2,1,0:T(8,128)(2,1)}, u32[]{:S(2)}, u32[]{:S(2)}) collective-permute-start(bf16[4,64,512]{2,1,0:T(8,128)(2,1)} %settle.2.refs_0_), channel_id=1, source_target_pairs={{0,4},{1,5},{2,6},{3,7},{4,0},{5,1},{6,2},{7,3},{8,12},{9,13},{10,... | collective-permute-start | bytes 786440 | tf_op jit(solution)/shard_map/ppermute | solution.py:421
  96.8 12.7 %collective-permute-start.7 = (bf16[4,64,512]{2,1,0:T(8,128)(2,1)}, bf16[4,64,512]{2,1,0:T(8,128)(2,1)}, u32[]{:S(2)}, u32[]{:S(2)}) collective-permute-start(bf16[4,64,512]{2,1,0:T(8,128)(2,1)} %settle.2.refs_0_), channel_id=1, source_target_pairs={{0,2},{1,3},{2,0},{3,1},{4,6},{5,7},{6,4},{7,5},{8,10},{9,11},{10,... | collective-permute-start | bytes 786440 | tf_op jit(solution)/shard_map/ppermute | solution.py:421
  103.0 6.5 %copy-start.8 = (bf16[4,64,512]{2,1,0:T(8,128)(2,1)}, bf16[4,64,512]{2,1,0:T(8,128)(2,1)S(1)}, u32[]{:S(2)}) copy-start(bf16[4,64,512]{2,1,0:T(8,128)(2,1)S(1)} %collective-permute-done.9.refs_3_) | copy-start | bytes 786436
  111.7 19.3 %collective-permute-start.10 = (bf16[16,64,512]{2,1,0:T(8,128)(2,1)}, bf16[16,64,512]{2,1,0:T(8,128)(2,1)}, u32[]{:S(2)}, u32[]{:S(2)}) collective-permute-start(bf16[16,64,512]{2,1,0:T(8,128)(2,1)} %join.2.refs_0_), channel_id=1, source_target_pairs={{0,1},{1,0},{2,3},{3,2},{4,5},{5,4},{6,7},{7,6},{8,9},{9,8},{10,11... | collective-permute-start | bytes 3145736 | tf_op jit(solution)/shard_map/ppermute | solution.py:421
  112.3 15.1 %copy-start.3 = (bf16[16,64,512]{2,1,0:T(8,128)(2,1)}, bf16[16,64,512]{2,1,0:T(8,128)(2,1)S(1)}, u32[]{:S(2)}) copy-start(bf16[16,64,512]{2,1,0:T(8,128)(2,1)S(1)} %collective-permute-done.11.away_ref) | copy-start | bytes 3145732
  112.6 8.9 %collective-permute-start.14 = (bf16[4,64,512]{2,1,0:T(8,128)(2,1)S(1)}, bf16[4,64,512]{2,1,0:T(8,128)(2,1)S(1)}, u32[]{:S(2)}, u32[]{:S(2)}) collective-permute-start(bf16[4,64,512]{2,1,0:T(8,128)(2,1)S(1)} %get-tuple-element.19), channel_id=1, source_target_pairs={{0,6},{1,7},{2,4},{3,5},{4,2},{5,3},{6,0},{7,1},{8,14},{9,15},{10,... | collective-permute-start | bytes 786440 | tf_op jit(solution)/shard_map/ppermute | solution.py:421
  113.8 13.6 %collective-permute-start.13 = (bf16[4,64,512]{2,1,0:T(8,128)(2,1)S(1)}, bf16[4,64,512]{2,1,0:T(8,128)(2,1)S(1)}, u32[]{:S(2)}, u32[]{:S(2)}) collective-permute-start(bf16[4,64,512]{2,1,0:T(8,128)(2,1)S(1)} %get-tuple-element.20), channel_id=1, source_target_pairs={{0,4},{1,5},{2,6},{3,7},{4,0},{5,1},{6,2},{7,3},{8,12},{9,13},{10,... | collective-permute-start | bytes 786440 | tf_op jit(solution)/shard_map/ppermute | solution.py:421
  115.0 12.5 %collective-permute-start.12 = (bf16[4,64,512]{2,1,0:T(8,128)(2,1)S(1)}, bf16[4,64,512]{2,1,0:T(8,128)(2,1)S(1)}, u32[]{:S(2)}, u32[]{:S(2)}) collective-permute-start(bf16[4,64,512]{2,1,0:T(8,128)(2,1)S(1)} %get-tuple-element.21), channel_id=1, source_target_pairs={{0,2},{1,3},{2,0},{3,1},{4,6},{5,7},{6,4},{7,5},{8,10},{9,11},{10,... | collective-permute-start | bytes 786440 | tf_op jit(solution)/shard_map/ppermute | solution.py:421
  121.5 5.9 %copy-start.10 = (bf16[4,64,512]{2,1,0:T(8,128)(2,1)}, bf16[4,64,512]{2,1,0:T(8,128)(2,1)S(1)}, u32[]{:S(2)}) copy-start(bf16[4,64,512]{2,1,0:T(8,128)(2,1)S(1)} %collective-permute-done.14.refs_2_) | copy-start | bytes 786436
  127.4 0.7 copy-start.12
  128.2 0.7 copy-start.14
  131.0 11.4 %copy-start.1 = (bf16[4,64,512]{2,1,0:T(8,128)(2,1)S(1)}, bf16[4,64,512]{2,1,0:T(8,128)(2,1)}, u32[]{:S(2)}) copy-start(bf16[4,64,512]{2,1,0:T(8,128)(2,1)} %settle.3.refs_6_.refs_0_.refs_5_) | copy-start | bytes 786436
  142.5 8.4 %collective-permute-start.17 = (bf16[4,64,512]{2,1,0:T(8,128)(2,1)S(1)}, bf16[4,64,512]{2,1,0:T(8,128)(2,1)S(1)}, u32[]{:S(2)}, u32[]{:S(2)}) collective-permute-start(bf16[4,64,512]{2,1,0:T(8,128)(2,1)S(1)} %copy-done.1), channel_id=1, source_target_pairs={{0,6},{1,7},{2,4},{3,5},{4,2},{5,3},{6,0},{7,1},{8,14},{9,15},{10,... | collective-permute-start | bytes 786440 | tf_op jit(solution)/shard_map/ppermute | solution.py:421
  143.7 13.7 %collective-permute-start.16 = (bf16[4,64,512]{2,1,0:T(8,128)(2,1)S(1)}, bf16[4,64,512]{2,1,0:T(8,128)(2,1)S(1)}, u32[]{:S(2)}, u32[]{:S(2)}) collective-permute-start(bf16[4,64,512]{2,1,0:T(8,128)(2,1)S(1)} %copy-done.1), channel_id=1, source_target_pairs={{0,4},{1,5},{2,6},{3,7},{4,0},{5,1},{6,2},{7,3},{8,12},{9,13},{10,... | collective-permute-start | bytes 786440 | tf_op jit(solution)/shard_map/ppermute | solution.py:421
  144.8 12.6 %collective-permute-start.15 = (bf16[4,64,512]{2,1,0:T(8,128)(2,1)S(1)}, bf16[4,64,512]{2,1,0:T(8,128)(2,1)S(1)}, u32[]{:S(2)}, u32[]{:S(2)}) collective-permute-start(bf16[4,64,512]{2,1,0:T(8,128)(2,1)S(1)} %copy-done.1), channel_id=1, source_target_pairs={{0,2},{1,3},{2,0},{3,1},{4,6},{5,7},{6,4},{7,5},{8,10},{9,11},{10,... | collective-permute-start | bytes 786440 | tf_op jit(solution)/shard_map/ppermute | solution.py:421
  150.9 6.5 %copy-start.5 = (bf16[4,64,512]{2,1,0:T(8,128)(2,1)}, bf16[4,64,512]{2,1,0:T(8,128)(2,1)S(1)}, u32[]{:S(2)}) copy-start(bf16[4,64,512]{2,1,0:T(8,128)(2,1)S(1)} %collective-permute-done.17.refs_3_.refs_8_) | copy-start | bytes 786436
  157.4 0.7 copy-start.6
  158.1 0.7 copy-start.7
  161.0 11.1 %collective-permute-start.18 = (bf16[16,64,512]{2,1,0:T(8,128)(2,1)}, bf16[16,64,512]{2,1,0:T(8,128)(2,1)S(1)}, u32[]{:S(2)}, u32[]{:S(2)}) collective-permute-start(bf16[16,64,512]{2,1,0:T(8,128)(2,1)} %join.3.refs_1_), channel_id=1, source_target_pairs={{0,1},{1,0},{2,3},{3,2},{4,5},{5,4},{6,7},{7,6},{8,9},{9,8},{10,11... | collective-permute-start | bytes 3145736 | tf_op jit(solution)/shard_map/ppermute | solution.py:421
  167.1 1.5 collective-permute-start.19
  169.4 16.9 %collective-permute-start.22 = (f32[128,128]{1,0:T(8,128)S(1)}, f32[128,128]{1,0:T(8,128)S(1)}, u32[]{:S(2)}, u32[]{:S(2)}) collective-permute-start(f32[128,128]{1,0:T(8,128)S(1)} %add.38), channel_id=1, source_target_pairs={{0,24},{8,16},{16,8},{24,0},{1,25},{9,17},{17,9},{25,1},{2,26},{10... | collective-permute-start | bytes 196616 | tf_op jit(solution)/shard_map/ppermute | solution.py:421
  170.1 17.2 %collective-permute-start.21 = (f32[128,128]{1,0:T(8,128)S(1)}, f32[128,128]{1,0:T(8,128)S(1)}, u32[]{:S(2)}, u32[]{:S(2)}) collective-permute-start(f32[128,128]{1,0:T(8,128)S(1)} %add.38), channel_id=1, source_target_pairs={{0,16},{8,24},{16,0},{24,8},{1,17},{9,25},{17,1},{25,9},{2,18},{10... | collective-permute-start | bytes 196616 | tf_op jit(solution)/shard_map/ppermute | solution.py:421
  170.3 17.0 %collective-permute-start.20 = (f32[128,128]{1,0:T(8,128)S(1)}, f32[128,128]{1,0:T(8,128)S(1)}, u32[]{:S(2)}, u32[]{:S(2)}) collective-permute-start(f32[128,128]{1,0:T(8,128)S(1)} %add.38), channel_id=1, source_target_pairs={{0,8},{8,0},{16,24},{24,16},{1,9},{9,1},{17,25},{25,17},{2,10},{10... | collective-permute-start | bytes 196616 | tf_op jit(solution)/shard_map/ppermute | solution.py:421
  172.2 1.0 copy-start.2
  184.2 11.9 %collective-permute-start.23 = (bf16[16,32,256]{2,1,0:T(8,128)(2,1)}, bf16[16,32,256]{2,1,0:T(8,128)(2,1)S(1)}, u32[]{:S(2)}, u32[]{:S(2)}) collective-permute-start(bf16[16,32,256]{2,1,0:T(8,128)(2,1)} %get-tuple-element.17), channel_id=1, source_target_pairs={{0,8},{8,16},{16,24},{24,0},{1,9},{9,17},{17,25},{25,1},{2,10},{10... | collective-permute-start | bytes 786440 | tf_op jit(solution)/shard_map/ppermute | solution.py:525
  184.8 21.8 %collective-permute-start.24 = (bf16[16,32,256]{2,1,0:T(8,128)(2,1)}, bf16[16,32,256]{2,1,0:T(8,128)(2,1)S(1)}, u32[]{:S(2)}, u32[]{:S(2)}) collective-permute-start(bf16[16,32,256]{2,1,0:T(8,128)(2,1)} %get-tuple-element.18), channel_id=1, source_target_pairs={{0,16},{8,24},{16,0},{24,8},{1,17},{9,25},{17,1},{25,9},{2,18},{10... | collective-permute-start | bytes 786440 | tf_op jit(solution)/shard_map/ppermute | solution.py:525
  186.3 23.9 %collective-permute-start.25 = (bf16[16,32,256]{2,1,0:T(8,128)(2,1)}, bf16[16,32,256]{2,1,0:T(8,128)(2,1)S(1)}, u32[]{:S(2)}, u32[]{:S(2)}) collective-permute-start(bf16[16,32,256]{2,1,0:T(8,128)(2,1)} %get-tuple-element.15.refs_11_), channel_id=1, source_target_pairs={{0,24},{8,0},{16,8},{24,16},{1,25},{9,1},{17,9},{25,17},{2,26},{10... | collective-permute-start | bytes 786440 | tf_op jit(solution)/shard_map/ppermute | solution.py:525
  196.1 14.1 %copy-start.16 = (bf16[16,32,256]{2,1,0:T(8,128)(2,1)}, bf16[16,32,256]{2,1,0:T(8,128)(2,1)S(1)}, u32[]{:S(2)}) copy-start(bf16[16,32,256]{2,1,0:T(8,128)(2,1)S(1)} %collective-permute-done.23.refs_2_) | copy-start | bytes 786436
  206.6 3.6 %copy-start.17 = (bf16[16,32,256]{2,1,0:T(8,128)(2,1)}, bf16[16,32,256]{2,1,0:T(8,128)(2,1)S(1)}, u32[]{:S(2)}) copy-start(bf16[16,32,256]{2,1,0:T(8,128)(2,1)S(1)} %collective-permute-done.24.refs_3_) | copy-start | bytes 786436
  210.2 0.7 copy-start.18
Sparse Core Ops, SparseCore 0:
  10.1 41.6 all-gather.2
  142.6 23.4 reduce-scatter.1

commit v2 on v1

--- a/solution.py
+++ b/solution.py
@@ -198,9 +198,6 @@
 
 def any_specs(arrays):
     return [pl.BlockSpec(memory_space=pl.ANY) for _ in arrays]
-
-
-NO_COST = pl.CostEstimate(flops=0, bytes_accessed=1, transcendentals=0)
 
 
 def product_cost(p, m, extra):
@@ -314,7 +311,7 @@
             pltpu.SemaphoreType.DMA((MARKOV_PARTS, F // CHUNK)),
         ],
         compiler_params=pltpu.CompilerParams(vmem_limit_bytes=VMEM),
-        cost_estimate=product_cost(p, m, 0) if whole else NO_COST,
+        cost_estimate=product_cost(p, m, 0),
         name="corange_part",
     )(place, fwd, back, *pieces, *hankel, *before)
 
@@ -328,30 +325,27 @@
 
 
 def gram_kernel(n_out, place_ref, *refs):
-    k_refs, (gram_ref, both_parts) = refs[:PARTS], refs[PARTS:]
-    gram_ref[...] = jnp.zeros(gram_ref.shape, f32)
-
-    def body(i, _):
-        for q, ref in enumerate(k_refs):
-            in_order(ref[i], both_parts, q, place_ref[0], n_out)
-        x = both_parts[...].astype(bf16)
-        gram_ref[...] += lax.dot_general(
-            x, x, (((1,), (1,)), ((), ())), preferred_element_type=f32
-        )
-        return 0
-
-    lax.fori_loop(0, k_refs[0].shape[0], body, 0)
+    k_refs, (gram_ref, moved) = refs[:PARTS], refs[PARTS:]
+    s_count = k_refs[0].shape[1]
+    total = jnp.zeros(gram_ref.shape, f32)
+    for i in range(k_refs[0].shape[0]):
+        x = jnp.concatenate([ref[i] for ref in k_refs], axis=0)
+        total += lax.dot_general(x, x, (((1,), (1,)), ((), ())), preferred_element_type=f32)
+    for _ in range(2):
+        for q in range(PARTS):
+            in_order(total[q * s_count : (q + 1) * s_count], moved, q, place_ref[0], n_out)
+        total = moved[...].T
+    gram_ref[...] = total
 
 
 def gram_part(joined, place, n_out):
-    _, s_count, p = joined[0].shape
-    s_count *= PARTS
+    s_count = PARTS * joined[0].shape[1]
     return pl.pallas_call(
         functools.partial(gram_kernel, n_out),
         in_specs=[pl.BlockSpec(memory_space=pltpu.SMEM)] + vmem_specs(joined),
         out_specs=pl.BlockSpec(memory_space=pltpu.VMEM),
         out_shape=jax.ShapeDtypeStruct((s_count, s_count), f32),
-        scratch_shapes=[pltpu.VMEM((s_count, p), f32)],
+        scratch_shapes=[pltpu.VMEM((s_count, s_count), f32)],
         compiler_params=pltpu.CompilerParams(vmem_limit_bytes=VMEM),
         name="gram_part",
     )(place, *joined)
@@ -528,7 +522,7 @@
     gram = gram_part(joined, place, n_out)
     gram = sum_by_xor(gram + to_xor(gram, "in", 1, n_in), "out", n_out)
     gram_matrix = gram / (R * OUTPUT_CHANNELS)
-    sketch = finish(sums, place, [*summed, *before, gram_matrix], n_out, n_in)
+    sketch = finish(sums, place, [*before, gram_matrix], n_out, n_in)
     corange = total_corange(summed, cor[0], arrived, sketch)
     return (sketch, corange, gram_matrix)
 

time: 221 us -> 212 us (0.959)
  waiting for transfers between devices: 77 us -> 71.1 us
  Pallas kernels: 92.2 us -> 89.6 us
    ppermute x20, waiting for transfers between devices: 52.6 us -> 41.4 us  [to_xor(): return lax.ppermute(x, axis, [(d, d ^ r) for d in range(n)])]
    ppermute x3, waiting for transfers between devices: 14.1 us -> 19.2 us  [shards(): lax.ppermute(cor[d], 'out', [(k, (k + d) % n_out) for k in range(n_out)])]
    pallas_call x1, Pallas kernels: 5.7 us -> 3.09 us  [gram_part(): pl.pallas_call(functools.partial(gram_kernel, n_out), in_specs=[pl.BlockS...]
    unnamed x44 -> x42, local copies, waits for them, and re-layouts: 6.23 us -> 6.19 us
  transfers between devices with their start and end apart: 28 -> 28, of which waited for: 15 -> 15; matrix products, arithmetic and copies ran while one was open for 3% -> 3% of each run, Pallas kernels for 27% -> 32%
where the time goes in v2:
time: 212 us; the launch traced here: 211 us
  Pallas kernels  89.6 us (42%)
  waiting for transfers between devices  71.1 us (34%)
  starting transfers between devices  23 us (11%)
  between operations  14.2 us (7%)
  local copies, waits for them, and re-layouts  8.72 us (4%)
  other arithmetic  5 us (2%)
    ppermute x20, waiting for transfers between devices, to_xor(): return lax.ppermute(x, axis, [(d, d ^ r) for d in range(n)])  41.4 us
    pallas_call x1, Pallas kernels, lag_transform(): pl.pallas_call(lag_kernel, grid=(blocks,), in_specs=[pl.BlockSpec((1, 1,...  26.6 us
    pallas_call x2, Pallas kernels, corange_part(): pl.pallas_call(functools.partial(corange_kernel, n_in, n_out, len(before)...  22.4 us
    ppermute x3, waiting for transfers between devices, shards(): lax.ppermute(cor[d], 'out', [(k, (k + d) % n_out) for k in range(n_out)])  19.2 us
    pallas_call x1, Pallas kernels, sketch_part(): pl.pallas_call(functools.partial(sketch_kernel, len(probes), n_out, n_in)...  18.1 us
    ppermute x20, starting transfers between devices, to_xor(): return lax.ppermute(x, axis, [(d, d ^ r) for d in range(n)])  15.9 us
    ppermute x3, waiting for transfers between devices, shards(): lax.ppermute(own, 'out', [((k + d) % n_out, k) for k in range(n_out)])  9.97 us
    pallas_call x1, Pallas kernels, finish(): pl.pallas_call(functools.partial(finish_kernel, n_out, n_in), in_specs=[p...  8.17 us
  transfers between devices with their start and end apart: 28, of which 15 were waited for; matrix products, arithmetic and copies ran while one was open for 3% of the time, Pallas kernels for 32%

profile of v2, /device:TPU:9, one launch (start us, length us, event | category | flops | bytes accessed | tf_op | source)
XLA Modules:
  0.0 211.5 jit_solution(14966302231468511119)
XLA Ops:
  7.2 1.8 fusion
  9.1 1.3 collective-permute-start.2
  10.4 1.1 collective-permute-start.1
  11.5 1.4 collective-permute-start
  12.9 0.7 convert_element_type.50
  13.6 0.7 broadcast_in_dim.4
  14.3 26.6 %lag_transform.1.refs_5_ = bf16[32,512,512]{2,1,0:T(8,128)(2,1)} custom-call(f32[8,1,256]{2,1,0:T(1,128)} %bitcast.6, bf16[1024,512]{1,0:T(8,128)(2,1)} %constant.21.clone.mat_ref, bf16[63,512,256]{2,1,0:T(8,128)(2,1)} %x_ref.1), custom_call_target="tpu_custom_call" | custom-call | flops 8589934592 | bytes 16777216 | tf_op jit(solution)/shard_map/lag_transform/pallas_call | solution.py:79
  40.9 0.6 pad_add_fusion.place_ref
  41.5 3.0 %collective-permute-done.1.refs_2_ = bf16[16,32,256]{2,1,0:T(8,128)(2,1)S(1)} collective-permute-done((bf16[16,32,256]{2,1,0:T(8,128)(2,1)S(1)}, bf16[16,32,256]{2,1,0:T(8,128)(2,1)S(1)}, u32[]{:S(2)}, u32[]{:S(2)}) %collective-permute-start.1) | collective-permute-done | bytes 262176 | tf_op jit(solution)/shard_map/ppermute | solution.py:496
  44.5 6.9 %collective-permute-done.refs_1_ = bf16[16,32,256]{2,1,0:T(8,128)(2,1)S(1)} collective-permute-done((bf16[16,32,256]{2,1,0:T(8,128)(2,1)S(1)}, bf16[16,32,256]{2,1,0:T(8,128)(2,1)S(1)}, u32[]{:S(2)}, u32[]{:S(2)}) %collective-permute-start) | collective-permute-done | bytes 262176 | tf_op jit(solution)/shard_map/ppermute | solution.py:496
  51.4 0.4 all-gather.3.cloned.1.call-done
  51.9 0.3 copy-done.20
  52.1 18.1 %sketch_part.1 = (f32[16,64,512]{2,1,0:T(8,128)}, bf16[16,64,512]{2,1,0:T(8,128)(2,1)}, f32[16,64,512]{2,1,0:T(8,128)}, bf16[16,64,512]{2,1,0:T(8,128)(2,1)}) custom-call(s32[2]{0:T(128)} %pad_add_fusion.place_ref, bf16[1024,256]{1,0:T(8,128)(2,1)} %constant.22.clone.fwd_ref, bf16[512,512]{1,0:T(8,128)(2,1)} %constant.24.clone.back_ref, ...), custom_call_target="tpu_custom_call" | custom-call | flops 8589934592 | bytes 16777216 | tf_op jit(solution)/shard_map/sketch_part/pallas_call | solution.py:213
  70.2 1.3 collective-permute-start.3
  71.6 2.4 %collective-permute-done.3.away_ref = bf16[16,64,512]{2,1,0:T(8,128)(2,1)S(1)} collective-permute-done((bf16[16,64,512]{2,1,0:T(8,128)(2,1)}, bf16[16,64,512]{2,1,0:T(8,128)(2,1)S(1)}, u32[]{:S(2)}, u32[]{:S(2)}) %collective-permute-start.3) | collective-permute-done | bytes 1048608 | tf_op jit(solution)/shard_map/ppermute | solution.py:415
  74.0 2.0 add_convert_fusion.3
  76.0 2.2 %collective-permute-start.6 = (bf16[4,64,512]{2,1,0:T(8,128)(2,1)S(1)}, bf16[4,64,512]{2,1,0:T(8,128)(2,1)S(1)}, u32[]{:S(2)}, u32[]{:S(2)}) collective-permute-start(bf16[4,64,512]{2,1,0:T(8,128)(2,1)S(1)} %get-tuple-element.22), channel_id=1, source_target_pairs={{0,6},{1,7},{2,4},{3,5},{4,2},{5,3},{6,0},{7,1},{8,14},{9,15},{10,... | collective-permute-start | bytes 786440 | tf_op jit(solution)/shard_map/ppermute | solution.py:415
  78.5 0.3 collective-permute-start.4
  78.8 5.8 %collective-permute-done.6.refs_2_ = bf16[4,64,512]{2,1,0:T(8,128)(2,1)S(1)} collective-permute-done((bf16[4,64,512]{2,1,0:T(8,128)(2,1)S(1)}, bf16[4,64,512]{2,1,0:T(8,128)(2,1)S(1)}, u32[]{:S(2)}, u32[]{:S(2)}) %collective-permute-start.6) | collective-permute-done | bytes 262176 | tf_op jit(solution)/shard_map/ppermute | solution.py:415
  84.6 6.3 %collective-permute-done.5.refs_1_ = bf16[4,64,512]{2,1,0:T(8,128)(2,1)S(1)} collective-permute-done((bf16[4,64,512]{2,1,0:T(8,128)(2,1)S(1)}, bf16[4,64,512]{2,1,0:T(8,128)(2,1)S(1)}, u32[]{:S(2)}, u32[]{:S(2)}) %collective-permute-start.5) | collective-permute-done | bytes 262176 | tf_op jit(solution)/shard_map/ppermute | solution.py:415
  90.9 0.7 copy-done.10
  91.6 0.7 copy-done.12
  92.3 2.2 %settle.2.refs_0_ = bf16[4,64,512]{2,1,0:T(8,128)(2,1)} custom-call(f32[16,64,512]{2,1,0:T(8,128)} %get-tuple-element.11.keep_ref, bf16[16,64,512]{2,1,0:T(8,128)(2,1)} %copy-done.2, bf16[4,64,512]{2,1,0:T(8,128)(2,1)} %copy-done.12, bf16[4,64,512]{2,1,0:T(8,128)(2,1)} %copy-done.10, bf16[4,64,512]{2,1,0:T(8,128)(2,1)} %copy-done.8), custom_call_target="tpu_custom_call" | custom-call | bytes 1048576 | tf_op jit(solution)/shard_map/settle/pallas_call | solution.py:440
  94.5 0.8 collective-permute-start.9
  95.2 1.6 collective-permute-start.8
  96.8 0.3 collective-permute-start.7
  97.1 5.9 %collective-permute-done.9.refs_3_ = bf16[4,64,512]{2,1,0:T(8,128)(2,1)S(1)} collective-permute-done((bf16[4,64,512]{2,1,0:T(8,128)(2,1)}, bf16[4,64,512]{2,1,0:T(8,128)(2,1)S(1)}, u32[]{:S(2)}, u32[]{:S(2)}) %collective-permute-start.9) | collective-permute-done | bytes 262176 | tf_op jit(solution)/shard_map/ppermute | solution.py:415
  103.0 6.5 %collective-permute-done.8.refs_2_ = bf16[4,64,512]{2,1,0:T(8,128)(2,1)} collective-permute-done((bf16[4,64,512]{2,1,0:T(8,128)(2,1)}, bf16[4,64,512]{2,1,0:T(8,128)(2,1)}, u32[]{:S(2)}, u32[]{:S(2)}) %collective-permute-start.8) | collective-permute-done | bytes 262176 | tf_op jit(solution)/shard_map/ppermute | solution.py:415
  109.5 2.2 %join.2.refs_0_ = bf16[16,64,512]{2,1,0:T(8,128)(2,1)} custom-call(bf16[4,64,512]{2,1,0:T(8,128)(2,1)} %settle.2.refs_0_, bf16[4,64,512]{2,1,0:T(8,128)(2,1)} %collective-permute-done.7.refs_1_, bf16[4,64,512]{2,1,0:T(8,128)(2,1)} %collective-permute-done.8.refs_2_, bf16[4,64,512]{2,1,0:T(8,128)(2,1)} %copy-done.7), custom_call_target="tpu_custom_call" | custom-call | tf_op jit(solution)/shard_map/join/pallas_call | solution.py:476
  111.8 0.6 collective-permute-start.10
  112.6 1.2 collective-permute-start.14
  113.8 1.1 collective-permute-start.13
  115.0 0.4 collective-permute-start.12
  115.3 6.2 %collective-permute-done.14.refs_2_ = bf16[4,64,512]{2,1,0:T(8,128)(2,1)S(1)} collective-permute-done((bf16[4,64,512]{2,1,0:T(8,128)(2,1)S(1)}, bf16[4,64,512]{2,1,0:T(8,128)(2,1)S(1)}, u32[]{:S(2)}, u32[]{:S(2)}) %collective-permute-start.14) | collective-permute-done | bytes 262176 | tf_op jit(solution)/shard_map/ppermute | solution.py:415
  121.5 5.9 %collective-permute-done.13.refs_1_ = bf16[4,64,512]{2,1,0:T(8,128)(2,1)S(1)} collective-permute-done((bf16[4,64,512]{2,1,0:T(8,128)(2,1)S(1)}, bf16[4,64,512]{2,1,0:T(8,128)(2,1)S(1)}, u32[]{:S(2)}, u32[]{:S(2)}) %collective-permute-start.13) | collective-permute-done | bytes 262176 | tf_op jit(solution)/shard_map/ppermute | solution.py:415
  127.5 0.7 copy-done.11
  128.1 0.7 copy-done.13
  128.8 2.2 %settle.3.refs_6_.refs_0_.refs_5_ = bf16[4,64,512]{2,1,0:T(8,128)(2,1)} custom-call(f32[16,64,512]{2,1,0:T(8,128)} %get-tuple-element.13.keep_ref, bf16[16,64,512]{2,1,0:T(8,128)(2,1)} %copy-done.1, bf16[4,64,512]{2,1,0:T(8,128)(2,1)} %copy-done.13, bf16[4,64,512]{2,1,0:T(8,128)(2,1)} %copy-done.11, bf16[4,64,512]{2,1,0:T(8,128)(2,1)} %copy-done.9), custom_call_target="tpu_custom_call" | custom-call | bytes 1048576 | tf_op jit(solution)/shard_map/settle/pallas_call | solution.py:440
  131.0 1.2 collective-permute-start.17
  132.2 1.1 collective-permute-start.16
  133.3 0.4 collective-permute-start.15
  133.7 11.4 %corange_part.2.refs_4_.refs_6_ = bf16[4,16,32,256]{3,2,1,0:T(8,128)(2,1)} custom-call(s32[2]{0:T(128)} %pad_add_fusion.place_ref, bf16[1024,256]{1,0:T(8,128)(2,1)} %constant.23.clone.fwd_ref, bf16[512,512]{1,0:T(8,128)(2,1)} %constant.25.clone.back_ref, bf16[4,64,512]{2,1,0:T(8,128)(2,1)} %settle.2.refs_0_, ...), custom_call_target="tpu_custom_call" | custom-call | flops 8589934592 | bytes 16777216 | tf_op jit(solution)/shard_map/corange_part/pallas_call | solution.py:299
  145.1 0.9 collective-permute-done.16.refs_2_.refs_7_
  146.0 0.7 copy-done.5
  146.7 0.7 copy-done.6
  147.4 2.2 %join.3.refs_1_ = bf16[16,64,512]{2,1,0:T(8,128)(2,1)} custom-call(bf16[4,64,512]{2,1,0:T(8,128)(2,1)} %settle.3.refs_6_.refs_0_.refs_5_, bf16[4,64,512]{2,1,0:T(8,128)(2,1)} %copy-done.6, bf16[4,64,512]{2,1,0:T(8,128)(2,1)} %copy-done.5, bf16[4,64,512]{2,1,0:T(8,128)(2,1)} %copy-done.4, bf16[4,16,32,256]{3,2,1,0:T(8,128)(2,1)} %corange_part.2.refs_4_.refs_6_), custom_call_target="tpu_custom_call" | custom-call | tf_op jit(solution)/shard_map/join/pallas_call | solution.py:476
  149.6 0.5 collective-permute-start.18
  150.1 3.1 %gram_part.1 = f32[128,128]{1,0:T(8,128)} custom-call(s32[2]{0:T(128)} %pad_add_fusion.place_ref, bf16[16,64,512]{2,1,0:T(8,128)(2,1)} %join.2.refs_0_, bf16[16,64,512]{2,1,0:T(8,128)(2,1)} %join.3.refs_1_), custom_call_target="tpu_custom_call" | custom-call | tf_op jit(solution)/shard_map/gram_part/pallas_call | solution.py:343
  153.3 1.4 collective-permute-done.19
  154.7 0.9 add.38
  155.6 0.7 collective-permute-start.22
  156.4 1.9 collective-permute-start.20
  158.3 1.0 copy-done.3
  159.2 11.1 %corange_part.3 = (f32[16,32,256]{2,1,0:T(8,128)}, bf16[16,32,256]{2,1,0:T(8,128)(2,1)}, bf16[16,32,256]{2,1,0:T(8,128)(2,1)}, bf16[16,32,256]{2,1,0:T(8,128)(2,1)}) custom-call(s32[2]{0:T(128)} %pad_add_fusion.place_ref, bf16[1024,256]{1,0:T(8,128)(2,1)} %constant.23.clone.fwd_ref, bf16[512,512]{1,0:T(8,128)(2,1)} %constant.25.clone.back_ref, ...), custom_call_target="tpu_custom_call" | custom-call | flops 8589934592 | bytes 16777216 | tf_op jit(solution)/shard_map/corange_part/pallas_call | solution.py:299
  170.3 0.7 collective-permute-start.23
  171.0 1.5 collective-permute-start.24
  172.4 1.0 collective-permute-start.25
  173.5 0.6 add_multiply_fusion.refs_11_
  174.1 8.2 %finish.1.refs_5_ = bf16[32,512,128]{2,1,0:T(8,128)(2,1)} custom-call(s32[2]{0:T(128)} %pad_add_fusion.place_ref, bf16[4,64,512]{2,1,0:T(8,128)(2,1)} %settle.2.refs_0_, bf16[4,64,512]{2,1,0:T(8,128)(2,1)} %collective-permute-done.7.refs_1_, bf16[4,64,512]{2,1,0:T(8,128)(2,1)} %collective-permute-done.8.refs_2_, bf16[4,64,512]{2,1,0:T(8,128)(2,1)} %copy-done.7, ...), custom_call_target="tpu_custom_call" | custom-call | bytes 67108864 | tf_op jit(solution)/shard_map/finish/pallas_call | solution.py:396
  182.3 11.5 %collective-permute-done.23.refs_2_ = bf16[16,32,256]{2,1,0:T(8,128)(2,1)S(1)} collective-permute-done((bf16[16,32,256]{2,1,0:T(8,128)(2,1)}, bf16[16,32,256]{2,1,0:T(8,128)(2,1)S(1)}, u32[]{:S(2)}, u32[]{:S(2)}) %collective-permute-start.23) | collective-permute-done | bytes 262176 | tf_op jit(solution)/shard_map/ppermute | solution.py:519
  193.8 5.6 %collective-permute-done.24.refs_3_ = bf16[16,32,256]{2,1,0:T(8,128)(2,1)S(1)} collective-permute-done((bf16[16,32,256]{2,1,0:T(8,128)(2,1)}, bf16[16,32,256]{2,1,0:T(8,128)(2,1)S(1)}, u32[]{:S(2)}, u32[]{:S(2)}) %collective-permute-start.24) | collective-permute-done | bytes 262176 | tf_op jit(solution)/shard_map/ppermute | solution.py:519
  199.4 2.1 collective-permute-done.25.refs_4_
  201.5 0.7 copy-done.17
  202.2 2.4 %total_corange.1 = f32[32,32,256]{2,1,0:T(8,128)} custom-call(bf16[16,32,256]{2,1,0:T(8,128)(2,1)} %reduce-scatter.2.cloned.1.call-done.refs_0_, f32[16,32,256]{2,1,0:T(8,128)} %get-tuple-element.16.refs_1_, bf16[16,32,256]{2,1,0:T(8,128)(2,1)} %copy-done.15, bf16[16,32,256]{2,1,0:T(8,128)(2,1)} %copy-done.16, bf16[16,32,256]{2,1,0:T(8,128)(2,1)} %copy-done.17, ...), custom_call_target="tpu_custom_call" | custom-call | tf_op jit(solution)/shard_map/total_corange/pallas_call | solution.py:367
  (56 shorter events, 1.0 us)
Async XLA Ops:
  7.2 44.7 %all-gather.3.cloned.1.call-start = ((), (), s32[]{:S(2)}) async-start(), calls=%async_computation.2 | async-start | bytes 1310720 | tf_op jit(solution)/shard_map/all_gather | solution.py:498
  9.0 31.9 %copy-start.14 = (bf16[16,32,256]{2,1,0:T(8,128)(2,1)}, bf16[16,32,256]{2,1,0:T(8,128)(2,1)S(1)}, u32[]{:S(2)}) copy-start(bf16[16,32,256]{2,1,0:T(8,128)(2,1)S(1)} %get-tuple-element.26.refs_0_) | copy-start | bytes 786436
  9.0 192.5 %reduce-scatter.2.cloned.1.call-start = ((), (), s32[]{:S(2)}) async-start(), calls=%async_computation.1 | async-start | bytes 1310720 | tf_op jit(solution)/shard_map/reduce_scatter | solution.py:516
  9.1 32.4 %collective-permute-start.2 = (bf16[16,32,256]{2,1,0:T(8,128)(2,1)S(1)}, bf16[16,32,256]{2,1,0:T(8,128)(2,1)S(1)}, u32[]{:S(2)}, u32[]{:S(2)}) collective-permute-start(bf16[16,32,256]{2,1,0:T(8,128)(2,1)S(1)} %get-tuple-element.26.refs_0_), channel_id=1, source_target_pairs={{24,0},{0,8},{8,16},{16,24},{25,1},{1,9},{9,17},{17,25},{26,2},{2,... | collective-permute-start | bytes 786440 | tf_op jit(solution)/shard_map/ppermute | solution.py:496
  10.4 34.1 %collective-permute-start.1 = (bf16[16,32,256]{2,1,0:T(8,128)(2,1)S(1)}, bf16[16,32,256]{2,1,0:T(8,128)(2,1)S(1)}, u32[]{:S(2)}, u32[]{:S(2)}) collective-permute-start(bf16[16,32,256]{2,1,0:T(8,128)(2,1)S(1)} %get-tuple-element.26.refs_0_), channel_id=1, source_target_pairs={{16,0},{24,8},{0,16},{8,24},{17,1},{25,9},{1,17},{9,25},{18,2},{26... | collective-permute-start | bytes 786440 | tf_op jit(solution)/shard_map/ppermute | solution.py:496
  11.5 40.0 %collective-permute-start = (bf16[16,32,256]{2,1,0:T(8,128)(2,1)S(1)}, bf16[16,32,256]{2,1,0:T(8,128)(2,1)S(1)}, u32[]{:S(2)}, u32[]{:S(2)}) collective-permute-start(bf16[16,32,256]{2,1,0:T(8,128)(2,1)S(1)} %get-tuple-element.26.refs_0_), channel_id=1, source_target_pairs={{8,0},{16,8},{24,16},{0,24},{9,1},{17,9},{25,17},{1,25},{10,2},{18... | collective-permute-start | bytes 786440 | tf_op jit(solution)/shard_map/ppermute | solution.py:496
  41.5 10.4 %copy-start.18 = (bf16[16,32,256]{2,1,0:T(8,128)(2,1)}, bf16[16,32,256]{2,1,0:T(8,128)(2,1)S(1)}, u32[]{:S(2)}) copy-start(bf16[16,32,256]{2,1,0:T(8,128)(2,1)S(1)} %collective-permute-done.2.refs_3_) | copy-start | bytes 786436
  44.5 7.4 %copy-start.19 = (bf16[16,32,256]{2,1,0:T(8,128)(2,1)}, bf16[16,32,256]{2,1,0:T(8,128)(2,1)S(1)}, u32[]{:S(2)}) copy-start(bf16[16,32,256]{2,1,0:T(8,128)(2,1)S(1)} %collective-permute-done.1.refs_2_) | copy-start | bytes 786436
  51.4 0.7 copy-start.20
  70.2 3.8 %collective-permute-start.3 = (bf16[16,64,512]{2,1,0:T(8,128)(2,1)}, bf16[16,64,512]{2,1,0:T(8,128)(2,1)S(1)}, u32[]{:S(2)}, u32[]{:S(2)}) collective-permute-start(bf16[16,64,512]{2,1,0:T(8,128)(2,1)} %get-tuple-element.12), channel_id=1, source_target_pairs={{0,1},{1,0},{2,3},{3,2},{4,5},{5,4},{6,7},{7,6},{8,9},{9,8},{10,11... | collective-permute-start | bytes 3145736 | tf_op jit(solution)/shard_map/ppermute | solution.py:415
  71.5 40.8 %collective-permute-start.11 = (bf16[16,64,512]{2,1,0:T(8,128)(2,1)}, bf16[16,64,512]{2,1,0:T(8,128)(2,1)S(1)}, u32[]{:S(2)}, u32[]{:S(2)}) collective-permute-start(bf16[16,64,512]{2,1,0:T(8,128)(2,1)} %get-tuple-element.14), channel_id=1, source_target_pairs={{0,1},{1,0},{2,3},{3,2},{4,5},{5,4},{6,7},{7,6},{8,9},{9,8},{10,11... | collective-permute-start | bytes 3145736 | tf_op jit(solution)/shard_map/ppermute | solution.py:415
  74.0 16.8 %copy-start.2 = (bf16[16,64,512]{2,1,0:T(8,128)(2,1)}, bf16[16,64,512]{2,1,0:T(8,128)(2,1)S(1)}, u32[]{:S(2)}) copy-start(bf16[16,64,512]{2,1,0:T(8,128)(2,1)S(1)} %collective-permute-done.3.away_ref) | copy-start | bytes 3145732
  76.0 8.5 %collective-permute-start.6 = (bf16[4,64,512]{2,1,0:T(8,128)(2,1)S(1)}, bf16[4,64,512]{2,1,0:T(8,128)(2,1)S(1)}, u32[]{:S(2)}, u32[]{:S(2)}) collective-permute-start(bf16[4,64,512]{2,1,0:T(8,128)(2,1)S(1)} %get-tuple-element.22), channel_id=1, source_target_pairs={{0,6},{1,7},{2,4},{3,5},{4,2},{5,3},{6,0},{7,1},{8,14},{9,15},{10,... | collective-permute-start | bytes 786440 | tf_op jit(solution)/shard_map/ppermute | solution.py:415
  78.3 12.6 %collective-permute-start.5 = (bf16[4,64,512]{2,1,0:T(8,128)(2,1)S(1)}, bf16[4,64,512]{2,1,0:T(8,128)(2,1)S(1)}, u32[]{:S(2)}, u32[]{:S(2)}) collective-permute-start(bf16[4,64,512]{2,1,0:T(8,128)(2,1)S(1)} %get-tuple-element.23), channel_id=1, source_target_pairs={{0,4},{1,5},{2,6},{3,7},{4,0},{5,1},{6,2},{7,3},{8,12},{9,13},{10,... | collective-permute-start | bytes 786440 | tf_op jit(solution)/shard_map/ppermute | solution.py:415
  78.5 12.4 %collective-permute-start.4 = (bf16[4,64,512]{2,1,0:T(8,128)(2,1)S(1)}, bf16[4,64,512]{2,1,0:T(8,128)(2,1)S(1)}, u32[]{:S(2)}, u32[]{:S(2)}) collective-permute-start(bf16[4,64,512]{2,1,0:T(8,128)(2,1)S(1)} %get-tuple-element.24), channel_id=1, source_target_pairs={{0,2},{1,3},{2,0},{3,1},{4,6},{5,7},{6,4},{7,5},{8,10},{9,11},{10,... | collective-permute-start | bytes 786440 | tf_op jit(solution)/shard_map/ppermute | solution.py:415
  84.6 6.3 %copy-start.8 = (bf16[4,64,512]{2,1,0:T(8,128)(2,1)}, bf16[4,64,512]{2,1,0:T(8,128)(2,1)S(1)}, u32[]{:S(2)}) copy-start(bf16[4,64,512]{2,1,0:T(8,128)(2,1)S(1)} %collective-permute-done.6.refs_2_) | copy-start | bytes 786436
  90.8 0.7 copy-start.10
  91.5 0.7 copy-start.12
  94.5 17.9 %copy-start = (f32[16,64,512]{2,1,0:T(8,128)S(1)}, f32[16,64,512]{2,1,0:T(8,128)}, u32[]{:S(2)}) copy-start(f32[16,64,512]{2,1,0:T(8,128)} %get-tuple-element.13.keep_ref) | copy-start | bytes 6291460
  94.5 8.5 %collective-permute-start.9 = (bf16[4,64,512]{2,1,0:T(8,128)(2,1)}, bf16[4,64,512]{2,1,0:T(8,128)(2,1)S(1)}, u32[]{:S(2)}, u32[]{:S(2)}) collective-permute-start(bf16[4,64,512]{2,1,0:T(8,128)(2,1)} %settle.2.refs_0_), channel_id=1, source_target_pairs={{0,6},{1,7},{2,4},{3,5},{4,2},{5,3},{6,0},{7,1},{8,14},{9,15},{10,... | collective-permute-start | bytes 786440 | tf_op jit(solution)/shard_map/ppermute | solution.py:415
  95.2 14.3 %collective-permute-start.8 = (bf16[4,64,512]{2,1,0:T(8,128)(2,1)}, bf16[4,64,512]{2,1,0:T(8,128)(2,1)}, u32[]{:S(2)}, u32[]{:S(2)}) collective-permute-start(bf16[4,64,512]{2,1,0:T(8,128)(2,1)} %settle.2.refs_0_), channel_id=1, source_target_pairs={{0,4},{1,5},{2,6},{3,7},{4,0},{5,1},{6,2},{7,3},{8,12},{9,13},{10,... | collective-permute-start | bytes 786440 | tf_op jit(solution)/shard_map/ppermute | solution.py:415
  96.8 12.7 %collective-permute-start.7 = (bf16[4,64,512]{2,1,0:T(8,128)(2,1)}, bf16[4,64,512]{2,1,0:T(8,128)(2,1)}, u32[]{:S(2)}, u32[]{:S(2)}) collective-permute-start(bf16[4,64,512]{2,1,0:T(8,128)(2,1)} %settle.2.refs_0_), channel_id=1, source_target_pairs={{0,2},{1,3},{2,0},{3,1},{4,6},{5,7},{6,4},{7,5},{8,10},{9,11},{10,... | collective-permute-start | bytes 786440 | tf_op jit(solution)/shard_map/ppermute | solution.py:415
  103.0 6.5 %copy-start.7 = (bf16[4,64,512]{2,1,0:T(8,128)(2,1)}, bf16[4,64,512]{2,1,0:T(8,128)(2,1)S(1)}, u32[]{:S(2)}) copy-start(bf16[4,64,512]{2,1,0:T(8,128)(2,1)S(1)} %collective-permute-done.9.refs_3_) | copy-start | bytes 786436
  111.8 21.9 %collective-permute-start.10 = (bf16[16,64,512]{2,1,0:T(8,128)(2,1)}, bf16[16,64,512]{2,1,0:T(8,128)(2,1)}, u32[]{:S(2)}, u32[]{:S(2)}) collective-permute-start(bf16[16,64,512]{2,1,0:T(8,128)(2,1)} %join.2.refs_0_), channel_id=1, source_target_pairs={{0,1},{1,0},{2,3},{3,2},{4,5},{5,4},{6,7},{7,6},{8,9},{9,8},{10,11... | collective-permute-start | bytes 3145736 | tf_op jit(solution)/shard_map/ppermute | solution.py:415
  112.3 15.1 %copy-start.1 = (bf16[16,64,512]{2,1,0:T(8,128)(2,1)}, bf16[16,64,512]{2,1,0:T(8,128)(2,1)S(1)}, u32[]{:S(2)}) copy-start(bf16[16,64,512]{2,1,0:T(8,128)(2,1)S(1)} %collective-permute-done.11.away_ref) | copy-start | bytes 3145732
  112.6 8.9 %collective-permute-start.14 = (bf16[4,64,512]{2,1,0:T(8,128)(2,1)S(1)}, bf16[4,64,512]{2,1,0:T(8,128)(2,1)S(1)}, u32[]{:S(2)}, u32[]{:S(2)}) collective-permute-start(bf16[4,64,512]{2,1,0:T(8,128)(2,1)S(1)} %get-tuple-element.19), channel_id=1, source_target_pairs={{0,6},{1,7},{2,4},{3,5},{4,2},{5,3},{6,0},{7,1},{8,14},{9,15},{10,... | collective-permute-start | bytes 786440 | tf_op jit(solution)/shard_map/ppermute | solution.py:415
  113.8 13.6 %collective-permute-start.13 = (bf16[4,64,512]{2,1,0:T(8,128)(2,1)S(1)}, bf16[4,64,512]{2,1,0:T(8,128)(2,1)S(1)}, u32[]{:S(2)}, u32[]{:S(2)}) collective-permute-start(bf16[4,64,512]{2,1,0:T(8,128)(2,1)S(1)} %get-tuple-element.20), channel_id=1, source_target_pairs={{0,4},{1,5},{2,6},{3,7},{4,0},{5,1},{6,2},{7,3},{8,12},{9,13},{10,... | collective-permute-start | bytes 786440 | tf_op jit(solution)/shard_map/ppermute | solution.py:415
  115.0 12.5 %collective-permute-start.12 = (bf16[4,64,512]{2,1,0:T(8,128)(2,1)S(1)}, bf16[4,64,512]{2,1,0:T(8,128)(2,1)S(1)}, u32[]{:S(2)}, u32[]{:S(2)}) collective-permute-start(bf16[4,64,512]{2,1,0:T(8,128)(2,1)S(1)} %get-tuple-element.21), channel_id=1, source_target_pairs={{0,2},{1,3},{2,0},{3,1},{4,6},{5,7},{6,4},{7,5},{8,10},{9,11},{10,... | collective-permute-start | bytes 786440 | tf_op jit(solution)/shard_map/ppermute | solution.py:415
  121.5 5.9 %copy-start.9 = (bf16[4,64,512]{2,1,0:T(8,128)(2,1)}, bf16[4,64,512]{2,1,0:T(8,128)(2,1)S(1)}, u32[]{:S(2)}) copy-start(bf16[4,64,512]{2,1,0:T(8,128)(2,1)S(1)} %collective-permute-done.14.refs_2_) | copy-start | bytes 786436
  127.4 0.7 copy-start.11
  128.1 0.7 copy-start.13
  131.0 14.0 %collective-permute-start.17 = (bf16[4,64,512]{2,1,0:T(8,128)(2,1)}, bf16[4,64,512]{2,1,0:T(8,128)(2,1)S(1)}, u32[]{:S(2)}, u32[]{:S(2)}) collective-permute-start(bf16[4,64,512]{2,1,0:T(8,128)(2,1)} %settle.3.refs_6_.refs_0_.refs_5_), channel_id=1, source_target_pairs={{0,6},{1,7},{2,4},{3,5},{4,2},{5,3},{6,0},{7,1},{8,14},{9,15},{10,... | collective-permute-start | bytes 786440 | tf_op jit(solution)/shard_map/ppermute | solution.py:415
  132.2 13.8 %collective-permute-start.16 = (bf16[4,64,512]{2,1,0:T(8,128)(2,1)}, bf16[4,64,512]{2,1,0:T(8,128)(2,1)S(1)}, u32[]{:S(2)}, u32[]{:S(2)}) collective-permute-start(bf16[4,64,512]{2,1,0:T(8,128)(2,1)} %settle.3.refs_6_.refs_0_.refs_5_), channel_id=1, source_target_pairs={{0,4},{1,5},{2,6},{3,7},{4,0},{5,1},{6,2},{7,3},{8,12},{9,13},{10,... | collective-permute-start | bytes 786440 | tf_op jit(solution)/shard_map/ppermute | solution.py:415
  133.3 12.7 %collective-permute-start.15 = (bf16[4,64,512]{2,1,0:T(8,128)(2,1)}, bf16[4,64,512]{2,1,0:T(8,128)(2,1)S(1)}, u32[]{:S(2)}, u32[]{:S(2)}) collective-permute-start(bf16[4,64,512]{2,1,0:T(8,128)(2,1)} %settle.3.refs_6_.refs_0_.refs_5_), channel_id=1, source_target_pairs={{0,2},{1,3},{2,0},{3,1},{4,6},{5,7},{6,4},{7,5},{8,10},{9,11},{10,... | collective-permute-start | bytes 786440 | tf_op jit(solution)/shard_map/ppermute | solution.py:415
  145.1 0.9 copy-start.4
  146.0 0.7 copy-start.5
  146.7 0.7 copy-start.6
  149.6 8.6 %collective-permute-start.18 = (bf16[16,64,512]{2,1,0:T(8,128)(2,1)}, bf16[16,64,512]{2,1,0:T(8,128)(2,1)S(1)}, u32[]{:S(2)}, u32[]{:S(2)}) collective-permute-start(bf16[16,64,512]{2,1,0:T(8,128)(2,1)} %join.3.refs_1_), channel_id=1, source_target_pairs={{0,1},{1,0},{2,3},{3,2},{4,5},{5,4},{6,7},{7,6},{8,9},{9,8},{10,11... | collective-permute-start | bytes 3145736 | tf_op jit(solution)/shard_map/ppermute | solution.py:415
  153.2 1.5 collective-permute-start.19
  155.6 16.9 %collective-permute-start.22 = (f32[128,128]{1,0:T(8,128)S(1)}, f32[128,128]{1,0:T(8,128)S(1)}, u32[]{:S(2)}, u32[]{:S(2)}) collective-permute-start(f32[128,128]{1,0:T(8,128)S(1)} %add.38), channel_id=1, source_target_pairs={{0,24},{8,16},{16,8},{24,0},{1,25},{9,17},{17,9},{25,1},{2,26},{10... | collective-permute-start | bytes 196616 | tf_op jit(solution)/shard_map/ppermute | solution.py:415
  156.2 17.2 %collective-permute-start.21 = (f32[128,128]{1,0:T(8,128)S(1)}, f32[128,128]{1,0:T(8,128)S(1)}, u32[]{:S(2)}, u32[]{:S(2)}) collective-permute-start(f32[128,128]{1,0:T(8,128)S(1)} %add.38), channel_id=1, source_target_pairs={{0,16},{8,24},{16,0},{24,8},{1,17},{9,25},{17,1},{25,9},{2,18},{10... | collective-permute-start | bytes 196616 | tf_op jit(solution)/shard_map/ppermute | solution.py:415
  156.4 17.1 %collective-permute-start.20 = (f32[128,128]{1,0:T(8,128)S(1)}, f32[128,128]{1,0:T(8,128)S(1)}, u32[]{:S(2)}, u32[]{:S(2)}) collective-permute-start(f32[128,128]{1,0:T(8,128)S(1)} %add.38), channel_id=1, source_target_pairs={{0,8},{8,0},{16,24},{24,16},{1,9},{9,1},{17,25},{25,17},{2,10},{10... | collective-permute-start | bytes 196616 | tf_op jit(solution)/shard_map/ppermute | solution.py:415
  158.3 1.0 copy-start.3
  170.3 23.5 %collective-permute-start.23 = (bf16[16,32,256]{2,1,0:T(8,128)(2,1)}, bf16[16,32,256]{2,1,0:T(8,128)(2,1)S(1)}, u32[]{:S(2)}, u32[]{:S(2)}) collective-permute-start(bf16[16,32,256]{2,1,0:T(8,128)(2,1)} %get-tuple-element.17), channel_id=1, source_target_pairs={{0,8},{8,16},{16,24},{24,0},{1,9},{9,17},{17,25},{25,1},{2,10},{10... | collective-permute-start | bytes 786440 | tf_op jit(solution)/shard_map/ppermute | solution.py:519
  171.0 28.4 %collective-permute-start.24 = (bf16[16,32,256]{2,1,0:T(8,128)(2,1)}, bf16[16,32,256]{2,1,0:T(8,128)(2,1)S(1)}, u32[]{:S(2)}, u32[]{:S(2)}) collective-permute-start(bf16[16,32,256]{2,1,0:T(8,128)(2,1)} %get-tuple-element.18), channel_id=1, source_target_pairs={{0,16},{8,24},{16,0},{24,8},{1,17},{9,25},{17,1},{25,9},{2,18},{10... | collective-permute-start | bytes 786440 | tf_op jit(solution)/shard_map/ppermute | solution.py:519
  172.4 29.0 %collective-permute-start.25 = (bf16[16,32,256]{2,1,0:T(8,128)(2,1)}, bf16[16,32,256]{2,1,0:T(8,128)(2,1)S(1)}, u32[]{:S(2)}, u32[]{:S(2)}) collective-permute-start(bf16[16,32,256]{2,1,0:T(8,128)(2,1)} %get-tuple-element.15.refs_10_), channel_id=1, source_target_pairs={{0,24},{8,0},{16,8},{24,16},{1,25},{9,1},{17,9},{25,17},{2,26},{10... | collective-permute-start | bytes 786440 | tf_op jit(solution)/shard_map/ppermute | solution.py:519
  193.8 7.7 %copy-start.15 = (bf16[16,32,256]{2,1,0:T(8,128)(2,1)}, bf16[16,32,256]{2,1,0:T(8,128)(2,1)S(1)}, u32[]{:S(2)}) copy-start(bf16[16,32,256]{2,1,0:T(8,128)(2,1)S(1)} %collective-permute-done.23.refs_2_) | copy-start | bytes 786436
  199.4 2.1 copy-start.16
  201.5 0.7 copy-start.17
Sparse Core Ops, SparseCore 0:
  10.1 41.6 all-gather.2
  150.3 42.8 reduce-scatter.1

commit v3 on v2

--- a/solution.py
+++ b/solution.py
@@ -428,27 +428,12 @@
     return x
 
 
-def settle_kernel(n, keep_ref, away_ref, *refs):
-    total = keep_ref[...] + away_ref[...].astype(f32)
-    for ref in refs[:n]:
-        total += ref[...].astype(f32)
-    refs[-1][...] = total.astype(bf16)
-
-
-def settle(keep, away, arrived, before):
-    block = pl.BlockSpec(arrived[0].shape, lambda i: (0, 0, 0))
-    return pl.pallas_call(
-        functools.partial(settle_kernel, len(arrived)),
-        grid=(1,),
-        in_specs=[block] * (2 + len(arrived)) + any_specs(before),
-        out_specs=block,
-        out_shape=jax.ShapeDtypeStruct(arrived[0].shape, bf16),
-        compiler_params=pltpu.CompilerParams(vmem_limit_bytes=VMEM),
-        cost_estimate=pl.CostEstimate(
-            flops=0, bytes_accessed=8 * arrived[0].size, transcendentals=0
-        ),
-        name="settle",
-    )(keep, away, *arrived, *before)
+def settle(keep, away, arrived):
+    rows = arrived[0].shape[0]
+    total = keep[:rows] + away[:rows].astype(f32)
+    for x in arrived:
+        total = total + x.astype(f32)
+    return total.astype(bf16)
 
 
 def meet(keep, send, n):
@@ -500,11 +485,11 @@
 
     raws = sketch_part(gathered, hankel, probe_mat, raw_mat, place, n_out, n_in)
     met = [meet(raws[2 * q], raws[2 * q + 1], n_in) for q in range(PARTS)]
-    owns = [settle(*x, []) for x in met]
+    owns = [settle(*x) for x in met]
     joined, sums, summed, before = [], [], [], owns[-1:]
     for q, own in enumerate(owns):
         mine = spread(own, n_in)
-        joined.append(join(mine, before if q else []))
+        joined.append(join(mine, before) if q else jnp.concatenate(mine, axis=0))
         sums.append(mine + [to_xor(joined[q], "in", 1, n_in)])
         last = q == PARTS - 1
         cor = corange_part(

time: 212 us -> 205 us (0.967)
  Pallas kernels: 89.6 us -> 83 us
  waiting for transfers between devices: 71.1 us -> 67.3 us
  starting transfers between devices: 23 us -> 26.6 us
    pallas_call x2 -> x0, Pallas kernels: 4.37 us -> none  [settle(): pl.pallas_call(functools.partial(settle_kernel, len(arrived)), grid=(1,),...]
    ppermute x20, waiting for transfers between devices: 41.4 us -> 37.5 us  [to_xor(): return lax.ppermute(x, axis, [(d, d ^ r) for d in range(n)])]
    ppermute x20, starting transfers between devices: 15.9 us -> 19.5 us  [to_xor(): return lax.ppermute(x, axis, [(d, d ^ r) for d in range(n)])]
    pallas_call x2 -> x1, Pallas kernels: 4.45 us -> 2.22 us  [join(): pl.pallas_call(functools.partial(join_kernel, len(mine)), in_specs=vmem_s...]
    unnamed x42 -> x40, local copies, waits for them, and re-layouts: 6.19 us -> 4.42 us
  transfers between devices with their start and end apart: 28 -> 28, of which waited for: 15 -> 15; matrix products, arithmetic and copies ran while one was open for 3% -> 3% of each run, Pallas kernels for 32% -> 30%
where the time goes in v3:
time: 205 us; the launch traced here: 204 us
  Pallas kernels  83 us (40%)
  waiting for transfers between devices  67.3 us (33%)
  starting transfers between devices  26.6 us (13%)
  between operations  14.3 us (7%)
  local copies, waits for them, and re-layouts  6.95 us (3%)
  other arithmetic  6.26 us (3%)
    ppermute x20, waiting for transfers between devices, to_xor(): return lax.ppermute(x, axis, [(d, d ^ r) for d in range(n)])  37.5 us
    pallas_call x1, Pallas kernels, lag_transform(): pl.pallas_call(lag_kernel, grid=(blocks,), in_specs=[pl.BlockSpec((1, 1,...  26.6 us
    pallas_call x2, Pallas kernels, corange_part(): pl.pallas_call(functools.partial(corange_kernel, n_in, n_out, len(before)...  22.4 us
    ppermute x20, starting transfers between devices, to_xor(): return lax.ppermute(x, axis, [(d, d ^ r) for d in range(n)])  19.5 us
    ppermute x3, waiting for transfers between devices, shards(): lax.ppermute(cor[d], 'out', [(k, (k + d) % n_out) for k in range(n_out)])  19.4 us
    pallas_call x1, Pallas kernels, sketch_part(): pl.pallas_call(functools.partial(sketch_kernel, len(probes), n_out, n_in)...  18.1 us
    ppermute x3, waiting for transfers between devices, shards(): lax.ppermute(own, 'out', [((k + d) % n_out, k) for k in range(n_out)])  9.92 us
    pallas_call x1, Pallas kernels, finish(): pl.pallas_call(functools.partial(finish_kernel, n_out, n_in), in_specs=[p...  8.17 us
  transfers between devices with their start and end apart: 28, of which 15 were waited for; matrix products, arithmetic and copies ran while one was open for 3% of the time, Pallas kernels for 30%

profile of v3, /device:TPU:9, one launch (start us, length us, event | category | flops | bytes accessed | tf_op | source)
XLA Modules:
  0.0 204.3 jit_solution(6163752250955121572)
XLA Ops:
  7.2 1.8 fusion
  9.1 1.3 collective-permute-start.2
  10.4 1.1 collective-permute-start.1
  11.5 1.4 collective-permute-start
  12.9 0.7 convert_element_type.80
  13.6 0.7 broadcast_in_dim.4
  14.3 26.6 %lag_transform.1.refs_5_ = bf16[32,512,512]{2,1,0:T(8,128)(2,1)} custom-call(f32[8,1,256]{2,1,0:T(1,128)} %bitcast.6, bf16[1024,512]{1,0:T(8,128)(2,1)} %constant.21.clone.mat_ref, bf16[63,512,256]{2,1,0:T(8,128)(2,1)} %x_ref.1), custom_call_target="tpu_custom_call" | custom-call | flops 8589934592 | bytes 16777216 | tf_op jit(solution)/shard_map/lag_transform/pallas_call | solution.py:79
  40.9 0.6 pad_add_fusion.place_ref
  41.5 3.0 %collective-permute-done.1.refs_2_ = bf16[16,32,256]{2,1,0:T(8,128)(2,1)S(1)} collective-permute-done((bf16[16,32,256]{2,1,0:T(8,128)(2,1)S(1)}, bf16[16,32,256]{2,1,0:T(8,128)(2,1)S(1)}, u32[]{:S(2)}, u32[]{:S(2)}) %collective-permute-start.1) | collective-permute-done | bytes 262176 | tf_op jit(solution)/shard_map/ppermute | solution.py:481
  44.5 6.9 %collective-permute-done.refs_1_ = bf16[16,32,256]{2,1,0:T(8,128)(2,1)S(1)} collective-permute-done((bf16[16,32,256]{2,1,0:T(8,128)(2,1)S(1)}, bf16[16,32,256]{2,1,0:T(8,128)(2,1)S(1)}, u32[]{:S(2)}, u32[]{:S(2)}) %collective-permute-start) | collective-permute-done | bytes 262176 | tf_op jit(solution)/shard_map/ppermute | solution.py:481
  51.4 0.4 all-gather.3.cloned.1.call-done
  51.9 0.3 copy-done.19
  52.2 18.1 %sketch_part.1 = (f32[16,64,512]{2,1,0:T(8,128)}, bf16[16,64,512]{2,1,0:T(8,128)(2,1)}, f32[16,64,512]{2,1,0:T(8,128)}, bf16[16,64,512]{2,1,0:T(8,128)(2,1)}) custom-call(s32[2]{0:T(128)} %pad_add_fusion.place_ref, bf16[1024,256]{1,0:T(8,128)(2,1)} %constant.22.clone.fwd_ref, bf16[512,512]{1,0:T(8,128)(2,1)} %constant.24.clone.back_ref, ...), custom_call_target="tpu_custom_call" | custom-call | flops 8589934592 | bytes 16777216 | tf_op jit(solution)/shard_map/sketch_part/pallas_call | solution.py:213
  70.2 1.3 collective-permute-start.3
  71.5 2.5 %collective-permute-done.3 = bf16[16,64,512]{2,1,0:T(8,128)(2,1)S(1)} collective-permute-done((bf16[16,64,512]{2,1,0:T(8,128)(2,1)}, bf16[16,64,512]{2,1,0:T(8,128)(2,1)S(1)}, u32[]{:S(2)}, u32[]{:S(2)}) %collective-permute-start.3) | collective-permute-done | bytes 1048608 | tf_op jit(solution)/shard_map/ppermute | solution.py:415
  74.0 1.7 add_convert_fusion.7
  75.7 1.3 collective-permute-start.4
  77.0 1.2 collective-permute-start.6
  78.2 0.2 collective-permute-start.5
  78.4 1.2 collective-permute-start.11
  79.7 3.7 %collective-permute-done.4 = bf16[4,64,512]{2,1,0:T(8,128)(2,1)S(1)} collective-permute-done((bf16[4,64,512]{2,1,0:T(8,128)(2,1)S(1)}, bf16[4,64,512]{2,1,0:T(8,128)(2,1)S(1)}, u32[]{:S(2)}, u32[]{:S(2)}) %collective-permute-start.4) | collective-permute-done | bytes 262176 | tf_op jit(solution)/shard_map/ppermute | solution.py:415
  83.3 6.6 %collective-permute-done.6 = bf16[4,64,512]{2,1,0:T(8,128)(2,1)S(1)} collective-permute-done((bf16[4,64,512]{2,1,0:T(8,128)(2,1)S(1)}, bf16[4,64,512]{2,1,0:T(8,128)(2,1)S(1)}, u32[]{:S(2)}, u32[]{:S(2)}) %collective-permute-start.6) | collective-permute-done | bytes 262176 | tf_op jit(solution)/shard_map/ppermute | solution.py:415
  89.9 1.2 add_convert_fusion.4.refs_0_
  91.2 1.2 collective-permute-start.9
  92.4 1.2 collective-permute-start.8
  93.6 0.3 collective-permute-start.7
  93.9 3.6 %collective-permute-done.9.refs_3_ = bf16[4,64,512]{2,1,0:T(8,128)(2,1)S(1)} collective-permute-done((bf16[4,64,512]{2,1,0:T(8,128)(2,1)S(1)}, bf16[4,64,512]{2,1,0:T(8,128)(2,1)S(1)}, u32[]{:S(2)}, u32[]{:S(2)}) %collective-permute-start.9) | collective-permute-done | bytes 262176 | tf_op jit(solution)/shard_map/ppermute | solution.py:415
  97.5 8.0 %collective-permute-done.8.refs_2_ = bf16[4,64,512]{2,1,0:T(8,128)(2,1)S(1)} collective-permute-done((bf16[4,64,512]{2,1,0:T(8,128)(2,1)S(1)}, bf16[4,64,512]{2,1,0:T(8,128)(2,1)S(1)}, u32[]{:S(2)}, u32[]{:S(2)}) %collective-permute-start.8) | collective-permute-done | bytes 262176 | tf_op jit(solution)/shard_map/ppermute | solution.py:415
  105.6 1.1 collective-permute-start.10
  106.7 0.3 add_convert_fusion.3
  107.0 0.6 collective-permute-start.12
  107.6 1.0 collective-permute-start.14
  108.6 1.1 collective-permute-start.13
  109.7 5.1 %collective-permute-done.12 = bf16[4,64,512]{2,1,0:T(8,128)(2,1)S(1)} collective-permute-done((bf16[4,64,512]{2,1,0:T(8,128)(2,1)S(1)}, bf16[4,64,512]{2,1,0:T(8,128)(2,1)S(1)}, u32[]{:S(2)}, u32[]{:S(2)}) %collective-permute-start.12) | collective-permute-done | bytes 262176 | tf_op jit(solution)/shard_map/ppermute | solution.py:415
  114.8 5.8 %collective-permute-done.14 = bf16[4,64,512]{2,1,0:T(8,128)(2,1)S(1)} collective-permute-done((bf16[4,64,512]{2,1,0:T(8,128)(2,1)S(1)}, bf16[4,64,512]{2,1,0:T(8,128)(2,1)S(1)}, u32[]{:S(2)}, u32[]{:S(2)}) %collective-permute-start.14) | collective-permute-done | bytes 262176 | tf_op jit(solution)/shard_map/ppermute | solution.py:415
  120.7 0.8 collective-permute-done.13
  121.5 0.2 add_convert_fusion.refs_6_.refs_0_.refs_5_
  121.7 1.3 collective-permute-start.17
  123.0 1.1 collective-permute-start.16
  124.1 0.3 collective-permute-start.15
  124.4 1.0 copy-done.4
  125.3 11.3 %corange_part.2.refs_4_.refs_6_ = bf16[4,16,32,256]{3,2,1,0:T(8,128)(2,1)} custom-call(s32[2]{0:T(128)} %pad_add_fusion.place_ref, bf16[1024,256]{1,0:T(8,128)(2,1)} %constant.23.clone.fwd_ref, bf16[512,512]{1,0:T(8,128)(2,1)} %constant.25.clone.back_ref, bf16[4,64,512]{2,1,0:T(8,128)(2,1)} %copy-done.2, bf16[4,64,512]{2,1,0:T(8,128)(2,1)} %copy-done.11, ...), custom_call_target="tpu_custom_call" | custom-call | flops 8589934592 | bytes 16777216 | tf_op jit(solution)/shard_map/corange_part/pallas_call | solution.py:299
  136.7 0.7 copy-done.6
  137.5 0.7 copy-done.8
  138.2 2.2 %join.1.refs_1_ = bf16[16,64,512]{2,1,0:T(8,128)(2,1)} custom-call(bf16[4,64,512]{2,1,0:T(8,128)(2,1)} %copy-done.1, bf16[4,64,512]{2,1,0:T(8,128)(2,1)} %copy-done.8, bf16[4,64,512]{2,1,0:T(8,128)(2,1)} %copy-done.7, bf16[4,64,512]{2,1,0:T(8,128)(2,1)} %copy-done.6, bf16[4,16,32,256]{3,2,1,0:T(8,128)(2,1)} %corange_part.2.refs_4_.refs_6_), custom_call_target="tpu_custom_call" | custom-call | tf_op jit(solution)/shard_map/join/pallas_call | solution.py:461
  140.4 2.3 %collective-permute-start.18 = (bf16[16,64,512]{2,1,0:T(8,128)(2,1)}, bf16[16,64,512]{2,1,0:T(8,128)(2,1)S(1)}, u32[]{:S(2)}, u32[]{:S(2)}) collective-permute-start(bf16[16,64,512]{2,1,0:T(8,128)(2,1)} %join.1.refs_1_), channel_id=1, source_target_pairs={{0,1},{1,0},{2,3},{3,2},{4,5},{5,4},{6,7},{7,6},{8,9},{9,8},{10,11... | collective-permute-start | bytes 3145736 | tf_op jit(solution)/shard_map/ppermute | solution.py:415
  142.8 3.1 %gram_part.1 = f32[128,128]{1,0:T(8,128)} custom-call(s32[2]{0:T(128)} %pad_add_fusion.place_ref, bf16[16,64,512]{2,1,0:T(8,128)(2,1)} %copy-done, bf16[16,64,512]{2,1,0:T(8,128)(2,1)} %join.1.refs_1_), custom_call_target="tpu_custom_call" | custom-call | tf_op jit(solution)/shard_map/gram_part/pallas_call | solution.py:343
  145.9 1.5 collective-permute-done.19
  147.4 0.9 add.70
  148.2 0.7 collective-permute-start.22
  148.9 0.2 collective-permute-start.21
  149.0 1.9 collective-permute-start.20
  150.9 1.0 copy-done.5
  151.9 11.1 %corange_part.3 = (f32[16,32,256]{2,1,0:T(8,128)}, bf16[16,32,256]{2,1,0:T(8,128)(2,1)}, bf16[16,32,256]{2,1,0:T(8,128)(2,1)}, bf16[16,32,256]{2,1,0:T(8,128)(2,1)}) custom-call(s32[2]{0:T(128)} %pad_add_fusion.place_ref, bf16[1024,256]{1,0:T(8,128)(2,1)} %constant.23.clone.fwd_ref, bf16[512,512]{1,0:T(8,128)(2,1)} %constant.25.clone.back_ref, ...), custom_call_target="tpu_custom_call" | custom-call | flops 8589934592 | bytes 16777216 | tf_op jit(solution)/shard_map/corange_part/pallas_call | solution.py:299
  163.0 0.7 collective-permute-start.23
  163.6 1.5 collective-permute-start.24
  165.1 1.0 collective-permute-start.25
  166.1 0.6 add_multiply_fusion.refs_11_
  166.8 8.2 %finish.1.refs_5_ = bf16[32,512,128]{2,1,0:T(8,128)(2,1)} custom-call(s32[2]{0:T(128)} %pad_add_fusion.place_ref, bf16[4,64,512]{2,1,0:T(8,128)(2,1)} %copy-done.2, bf16[4,64,512]{2,1,0:T(8,128)(2,1)} %copy-done.11, bf16[4,64,512]{2,1,0:T(8,128)(2,1)} %copy-done.10, bf16[4,64,512]{2,1,0:T(8,128)(2,1)} %copy-done.9, bf16[16,64,512]{2,1,0:T(8,128)(2,1)} %copy-done.4, ...), custom_call_target="tpu_custom_call" | custom-call | bytes 67108864 | tf_op jit(solution)/shard_map/finish/pallas_call | solution.py:396
  174.9 11.8 %collective-permute-done.23.refs_2_ = bf16[16,32,256]{2,1,0:T(8,128)(2,1)S(1)} collective-permute-done((bf16[16,32,256]{2,1,0:T(8,128)(2,1)}, bf16[16,32,256]{2,1,0:T(8,128)(2,1)S(1)}, u32[]{:S(2)}, u32[]{:S(2)}) %collective-permute-start.23) | collective-permute-done | bytes 262176 | tf_op jit(solution)/shard_map/ppermute | solution.py:504
  186.7 5.6 %collective-permute-done.24.refs_3_ = bf16[16,32,256]{2,1,0:T(8,128)(2,1)S(1)} collective-permute-done((bf16[16,32,256]{2,1,0:T(8,128)(2,1)}, bf16[16,32,256]{2,1,0:T(8,128)(2,1)S(1)}, u32[]{:S(2)}, u32[]{:S(2)}) %collective-permute-start.24) | collective-permute-done | bytes 262176 | tf_op jit(solution)/shard_map/ppermute | solution.py:504
  192.3 2.0 collective-permute-done.25.refs_4_
  194.4 0.7 copy-done.15
  195.0 2.4 %total_corange.1 = f32[32,32,256]{2,1,0:T(8,128)} custom-call(bf16[16,32,256]{2,1,0:T(8,128)(2,1)} %reduce-scatter.2.cloned.1.call-done.refs_0_, f32[16,32,256]{2,1,0:T(8,128)} %get-tuple-element.16.refs_1_, bf16[16,32,256]{2,1,0:T(8,128)(2,1)} %copy-done.13, bf16[16,32,256]{2,1,0:T(8,128)(2,1)} %copy-done.14, bf16[16,32,256]{2,1,0:T(8,128)(2,1)} %copy-done.15, ...), custom_call_target="tpu_custom_call" | custom-call | tf_op jit(solution)/shard_map/total_corange/pallas_call | solution.py:367
  (54 shorter events, 0.5 us)
Async XLA Ops:
  7.2 44.7 %all-gather.3.cloned.1.call-start = ((), (), s32[]{:S(2)}) async-start(), calls=%async_computation.2 | async-start | bytes 1310720 | tf_op jit(solution)/shard_map/all_gather | solution.py:483
  9.0 32.0 %copy-start.12 = (bf16[16,32,256]{2,1,0:T(8,128)(2,1)}, bf16[16,32,256]{2,1,0:T(8,128)(2,1)S(1)}, u32[]{:S(2)}) copy-start(bf16[16,32,256]{2,1,0:T(8,128)(2,1)S(1)} %get-tuple-element.26.refs_0_) | copy-start | bytes 786436
  9.0 185.4 %reduce-scatter.2.cloned.1.call-start = ((), (), s32[]{:S(2)}) async-start(), calls=%async_computation.1 | async-start | bytes 1310720 | tf_op jit(solution)/shard_map/reduce_scatter | solution.py:501
  9.1 32.5 %collective-permute-start.2 = (bf16[16,32,256]{2,1,0:T(8,128)(2,1)S(1)}, bf16[16,32,256]{2,1,0:T(8,128)(2,1)S(1)}, u32[]{:S(2)}, u32[]{:S(2)}) collective-permute-start(bf16[16,32,256]{2,1,0:T(8,128)(2,1)S(1)} %get-tuple-element.26.refs_0_), channel_id=1, source_target_pairs={{24,0},{0,8},{8,16},{16,24},{25,1},{1,9},{9,17},{17,25},{26,2},{2,... | collective-permute-start | bytes 786440 | tf_op jit(solution)/shard_map/ppermute | solution.py:481
  10.4 34.1 %collective-permute-start.1 = (bf16[16,32,256]{2,1,0:T(8,128)(2,1)S(1)}, bf16[16,32,256]{2,1,0:T(8,128)(2,1)S(1)}, u32[]{:S(2)}, u32[]{:S(2)}) collective-permute-start(bf16[16,32,256]{2,1,0:T(8,128)(2,1)S(1)} %get-tuple-element.26.refs_0_), channel_id=1, source_target_pairs={{16,0},{24,8},{0,16},{8,24},{17,1},{25,9},{1,17},{9,25},{18,2},{26... | collective-permute-start | bytes 786440 | tf_op jit(solution)/shard_map/ppermute | solution.py:481
  11.5 40.0 %collective-permute-start = (bf16[16,32,256]{2,1,0:T(8,128)(2,1)S(1)}, bf16[16,32,256]{2,1,0:T(8,128)(2,1)S(1)}, u32[]{:S(2)}, u32[]{:S(2)}) collective-permute-start(bf16[16,32,256]{2,1,0:T(8,128)(2,1)S(1)} %get-tuple-element.26.refs_0_), channel_id=1, source_target_pairs={{8,0},{16,8},{24,16},{0,24},{9,1},{17,9},{25,17},{1,25},{10,2},{18... | collective-permute-start | bytes 786440 | tf_op jit(solution)/shard_map/ppermute | solution.py:481
  41.5 10.3 %copy-start.17 = (bf16[16,32,256]{2,1,0:T(8,128)(2,1)}, bf16[16,32,256]{2,1,0:T(8,128)(2,1)S(1)}, u32[]{:S(2)}) copy-start(bf16[16,32,256]{2,1,0:T(8,128)(2,1)S(1)} %collective-permute-done.2.refs_3_) | copy-start | bytes 786436
  44.5 7.4 %copy-start.18 = (bf16[16,32,256]{2,1,0:T(8,128)(2,1)}, bf16[16,32,256]{2,1,0:T(8,128)(2,1)S(1)}, u32[]{:S(2)}) copy-start(bf16[16,32,256]{2,1,0:T(8,128)(2,1)S(1)} %collective-permute-done.1.refs_2_) | copy-start | bytes 786436
  51.4 0.7 copy-start.19
  70.2 8.2 %copy-start.16 = (bf16[16,64,512]{2,1,0:T(8,128)(2,1)S(1)}, bf16[16,64,512]{2,1,0:T(8,128)(2,1)}, u32[]{:S(2)}) copy-start(bf16[16,64,512]{2,1,0:T(8,128)(2,1)} %get-tuple-element.14) | copy-start | bytes 3145732
  70.2 3.8 %collective-permute-start.3 = (bf16[16,64,512]{2,1,0:T(8,128)(2,1)}, bf16[16,64,512]{2,1,0:T(8,128)(2,1)S(1)}, u32[]{:S(2)}, u32[]{:S(2)}) collective-permute-start(bf16[16,64,512]{2,1,0:T(8,128)(2,1)} %get-tuple-element.12), channel_id=1, source_target_pairs={{0,1},{1,0},{2,3},{3,2},{4,5},{5,4},{6,7},{7,6},{8,9},{9,8},{10,11... | collective-permute-start | bytes 3145736 | tf_op jit(solution)/shard_map/ppermute | solution.py:415
  75.7 31.0 %copy-start.3 = (f32[16,64,512]{2,1,0:T(8,128)S(1)}, f32[16,64,512]{2,1,0:T(8,128)}, u32[]{:S(2)}) copy-start(f32[16,64,512]{2,1,0:T(8,128)} %get-tuple-element.13) | copy-start | bytes 6291460
  75.7 7.6 %collective-permute-start.4 = (bf16[4,64,512]{2,1,0:T(8,128)(2,1)S(1)}, bf16[4,64,512]{2,1,0:T(8,128)(2,1)S(1)}, u32[]{:S(2)}, u32[]{:S(2)}) collective-permute-start(bf16[4,64,512]{2,1,0:T(8,128)(2,1)S(1)} %get-tuple-element.22), channel_id=1, source_target_pairs={{0,2},{1,3},{2,0},{3,1},{4,6},{5,7},{6,4},{7,5},{8,10},{9,11},{10,... | collective-permute-start | bytes 786440 | tf_op jit(solution)/shard_map/ppermute | solution.py:415
  77.0 12.9 %collective-permute-start.6 = (bf16[4,64,512]{2,1,0:T(8,128)(2,1)S(1)}, bf16[4,64,512]{2,1,0:T(8,128)(2,1)S(1)}, u32[]{:S(2)}, u32[]{:S(2)}) collective-permute-start(bf16[4,64,512]{2,1,0:T(8,128)(2,1)S(1)} %get-tuple-element.23), channel_id=1, source_target_pairs={{0,6},{1,7},{2,4},{3,5},{4,2},{5,3},{6,0},{7,1},{8,14},{9,15},{10,... | collective-permute-start | bytes 786440 | tf_op jit(solution)/shard_map/ppermute | solution.py:415
  78.2 11.7 %collective-permute-start.5 = (bf16[4,64,512]{2,1,0:T(8,128)(2,1)S(1)}, bf16[4,64,512]{2,1,0:T(8,128)(2,1)S(1)}, u32[]{:S(2)}, u32[]{:S(2)}) collective-permute-start(bf16[4,64,512]{2,1,0:T(8,128)(2,1)S(1)} %get-tuple-element.24), channel_id=1, source_target_pairs={{0,4},{1,5},{2,6},{3,7},{4,0},{5,1},{6,2},{7,3},{8,12},{9,13},{10,... | collective-permute-start | bytes 786440 | tf_op jit(solution)/shard_map/ppermute | solution.py:415
  78.4 28.3 %collective-permute-start.11 = (bf16[16,64,512]{2,1,0:T(8,128)(2,1)S(1)}, bf16[16,64,512]{2,1,0:T(8,128)(2,1)S(1)}, u32[]{:S(2)}, u32[]{:S(2)}) collective-permute-start(bf16[16,64,512]{2,1,0:T(8,128)(2,1)S(1)} %copy-done.16), channel_id=1, source_target_pairs={{0,1},{1,0},{2,3},{3,2},{4,5},{5,4},{6,7},{7,6},{8,9},{9,8},{10,11... | collective-permute-start | bytes 3145736 | tf_op jit(solution)/shard_map/ppermute | solution.py:415
  91.2 15.8 %copy-start.2 = (bf16[4,64,512]{2,1,0:T(8,128)(2,1)}, bf16[4,64,512]{2,1,0:T(8,128)(2,1)S(1)}, u32[]{:S(2)}) copy-start(bf16[4,64,512]{2,1,0:T(8,128)(2,1)S(1)} %add_convert_fusion.4.refs_0_) | copy-start | bytes 786436
  91.2 6.3 %collective-permute-start.9 = (bf16[4,64,512]{2,1,0:T(8,128)(2,1)S(1)}, bf16[4,64,512]{2,1,0:T(8,128)(2,1)S(1)}, u32[]{:S(2)}, u32[]{:S(2)}) collective-permute-start(bf16[4,64,512]{2,1,0:T(8,128)(2,1)S(1)} %add_convert_fusion.4.refs_0_), channel_id=1, source_target_pairs={{0,6},{1,7},{2,4},{3,5},{4,2},{5,3},{6,0},{7,1},{8,14},{9,15},{10,... | collective-permute-start | bytes 786440 | tf_op jit(solution)/shard_map/ppermute | solution.py:415
  92.4 13.0 %collective-permute-start.8 = (bf16[4,64,512]{2,1,0:T(8,128)(2,1)S(1)}, bf16[4,64,512]{2,1,0:T(8,128)(2,1)S(1)}, u32[]{:S(2)}, u32[]{:S(2)}) collective-permute-start(bf16[4,64,512]{2,1,0:T(8,128)(2,1)S(1)} %add_convert_fusion.4.refs_0_), channel_id=1, source_target_pairs={{0,4},{1,5},{2,6},{3,7},{4,0},{5,1},{6,2},{7,3},{8,12},{9,13},{10,... | collective-permute-start | bytes 786440 | tf_op jit(solution)/shard_map/ppermute | solution.py:415
  93.6 11.8 %collective-permute-start.7 = (bf16[4,64,512]{2,1,0:T(8,128)(2,1)S(1)}, bf16[4,64,512]{2,1,0:T(8,128)(2,1)S(1)}, u32[]{:S(2)}, u32[]{:S(2)}) collective-permute-start(bf16[4,64,512]{2,1,0:T(8,128)(2,1)S(1)} %add_convert_fusion.4.refs_0_), channel_id=1, source_target_pairs={{0,2},{1,3},{2,0},{3,1},{4,6},{5,7},{6,4},{7,5},{8,10},{9,11},{10,... | collective-permute-start | bytes 786440 | tf_op jit(solution)/shard_map/ppermute | solution.py:415
  97.5 9.5 %copy-start.9 = (bf16[4,64,512]{2,1,0:T(8,128)(2,1)}, bf16[4,64,512]{2,1,0:T(8,128)(2,1)S(1)}, u32[]{:S(2)}) copy-start(bf16[4,64,512]{2,1,0:T(8,128)(2,1)S(1)} %collective-permute-done.9.refs_3_) | copy-start | bytes 786436
  105.4 1.6 copy-start.10
  105.4 1.6 copy-start.11
  105.6 16.0 %copy-start = (bf16[16,64,512]{2,1,0:T(8,128)(2,1)}, bf16[16,64,512]{2,1,0:T(8,128)(2,1)S(1)}, u32[]{:S(2)}) copy-start(bf16[16,64,512]{2,1,0:T(8,128)(2,1)S(1)} %pad_maximum_fusion.refs_0_) | copy-start | bytes 3145732
  105.6 18.8 %collective-permute-start.10 = (bf16[16,64,512]{2,1,0:T(8,128)(2,1)S(1)}, bf16[16,64,512]{2,1,0:T(8,128)(2,1)S(1)}, u32[]{:S(2)}, u32[]{:S(2)}) collective-permute-start(bf16[16,64,512]{2,1,0:T(8,128)(2,1)S(1)} %pad_maximum_fusion.refs_0_), channel_id=1, source_target_pairs={{0,1},{1,0},{2,3},{3,2},{4,5},{5,4},{6,7},{7,6},{8,9},{9,8},{10,11... | collective-permute-start | bytes 3145736 | tf_op jit(solution)/shard_map/ppermute | solution.py:415
  107.0 7.8 %collective-permute-start.12 = (bf16[4,64,512]{2,1,0:T(8,128)(2,1)S(1)}, bf16[4,64,512]{2,1,0:T(8,128)(2,1)S(1)}, u32[]{:S(2)}, u32[]{:S(2)}) collective-permute-start(bf16[4,64,512]{2,1,0:T(8,128)(2,1)S(1)} %get-tuple-element.19), channel_id=1, source_target_pairs={{0,2},{1,3},{2,0},{3,1},{4,6},{5,7},{6,4},{7,5},{8,10},{9,11},{10,... | collective-permute-start | bytes 786440 | tf_op jit(solution)/shard_map/ppermute | solution.py:415
  107.6 13.0 %collective-permute-start.14 = (bf16[4,64,512]{2,1,0:T(8,128)(2,1)S(1)}, bf16[4,64,512]{2,1,0:T(8,128)(2,1)S(1)}, u32[]{:S(2)}, u32[]{:S(2)}) collective-permute-start(bf16[4,64,512]{2,1,0:T(8,128)(2,1)S(1)} %get-tuple-element.20), channel_id=1, source_target_pairs={{0,6},{1,7},{2,4},{3,5},{4,2},{5,3},{6,0},{7,1},{8,14},{9,15},{10,... | collective-permute-start | bytes 786440 | tf_op jit(solution)/shard_map/ppermute | solution.py:415
  108.6 12.8 %collective-permute-start.13 = (bf16[4,64,512]{2,1,0:T(8,128)(2,1)S(1)}, bf16[4,64,512]{2,1,0:T(8,128)(2,1)S(1)}, u32[]{:S(2)}, u32[]{:S(2)}) collective-permute-start(bf16[4,64,512]{2,1,0:T(8,128)(2,1)S(1)} %get-tuple-element.21), channel_id=1, source_target_pairs={{0,4},{1,5},{2,6},{3,7},{4,0},{5,1},{6,2},{7,3},{8,12},{9,13},{10,... | collective-permute-start | bytes 786440 | tf_op jit(solution)/shard_map/ppermute | solution.py:415
  121.6 2.7 %copy-start.1 = (bf16[4,64,512]{2,1,0:T(8,128)(2,1)}, bf16[4,64,512]{2,1,0:T(8,128)(2,1)S(1)}, u32[]{:S(2)}) copy-start(bf16[4,64,512]{2,1,0:T(8,128)(2,1)S(1)} %add_convert_fusion.refs_6_.refs_0_.refs_5_) | copy-start | bytes 786436
  121.7 15.0 %collective-permute-start.17 = (bf16[4,64,512]{2,1,0:T(8,128)(2,1)S(1)}, bf16[4,64,512]{2,1,0:T(8,128)(2,1)S(1)}, u32[]{:S(2)}, u32[]{:S(2)}) collective-permute-start(bf16[4,64,512]{2,1,0:T(8,128)(2,1)S(1)} %add_convert_fusion.refs_6_.refs_0_.refs_5_), channel_id=1, source_target_pairs={{0,6},{1,7},{2,4},{3,5},{4,2},{5,3},{6,0},{7,1},{8,14},{9,15},{10,... | collective-permute-start | bytes 786440 | tf_op jit(solution)/shard_map/ppermute | solution.py:415
  123.0 13.8 %collective-permute-start.16 = (bf16[4,64,512]{2,1,0:T(8,128)(2,1)S(1)}, bf16[4,64,512]{2,1,0:T(8,128)(2,1)S(1)}, u32[]{:S(2)}, u32[]{:S(2)}) collective-permute-start(bf16[4,64,512]{2,1,0:T(8,128)(2,1)S(1)} %add_convert_fusion.refs_6_.refs_0_.refs_5_), channel_id=1, source_target_pairs={{0,4},{1,5},{2,6},{3,7},{4,0},{5,1},{6,2},{7,3},{8,12},{9,13},{10,... | collective-permute-start | bytes 786440 | tf_op jit(solution)/shard_map/ppermute | solution.py:415
  124.1 12.6 %collective-permute-start.15 = (bf16[4,64,512]{2,1,0:T(8,128)(2,1)S(1)}, bf16[4,64,512]{2,1,0:T(8,128)(2,1)S(1)}, u32[]{:S(2)}, u32[]{:S(2)}) collective-permute-start(bf16[4,64,512]{2,1,0:T(8,128)(2,1)S(1)} %add_convert_fusion.refs_6_.refs_0_.refs_5_), channel_id=1, source_target_pairs={{0,2},{1,3},{2,0},{3,1},{4,6},{5,7},{6,4},{7,5},{8,10},{9,11},{10,... | collective-permute-start | bytes 786440 | tf_op jit(solution)/shard_map/ppermute | solution.py:415
  124.4 1.0 copy-start.4
  136.7 0.7 copy-start.6
  136.7 0.8 copy-start.7
  137.5 0.7 copy-start.8
  140.4 10.5 %collective-permute-start.18 = (bf16[16,64,512]{2,1,0:T(8,128)(2,1)}, bf16[16,64,512]{2,1,0:T(8,128)(2,1)S(1)}, u32[]{:S(2)}, u32[]{:S(2)}) collective-permute-start(bf16[16,64,512]{2,1,0:T(8,128)(2,1)} %join.1.refs_1_), channel_id=1, source_target_pairs={{0,1},{1,0},{2,3},{3,2},{4,5},{5,4},{6,7},{7,6},{8,9},{9,8},{10,11... | collective-permute-start | bytes 3145736 | tf_op jit(solution)/shard_map/ppermute | solution.py:415
  145.9 1.5 collective-permute-start.19
  148.2 16.9 %collective-permute-start.22 = (f32[128,128]{1,0:T(8,128)S(1)}, f32[128,128]{1,0:T(8,128)S(1)}, u32[]{:S(2)}, u32[]{:S(2)}) collective-permute-start(f32[128,128]{1,0:T(8,128)S(1)} %add.70), channel_id=1, source_target_pairs={{0,24},{8,16},{16,8},{24,0},{1,25},{9,17},{17,9},{25,1},{2,26},{10... | collective-permute-start | bytes 196616 | tf_op jit(solution)/shard_map/ppermute | solution.py:415
  148.9 17.2 %collective-permute-start.21 = (f32[128,128]{1,0:T(8,128)S(1)}, f32[128,128]{1,0:T(8,128)S(1)}, u32[]{:S(2)}, u32[]{:S(2)}) collective-permute-start(f32[128,128]{1,0:T(8,128)S(1)} %add.70), channel_id=1, source_target_pairs={{0,16},{8,24},{16,0},{24,8},{1,17},{9,25},{17,1},{25,9},{2,18},{10... | collective-permute-start | bytes 196616 | tf_op jit(solution)/shard_map/ppermute | solution.py:415
  149.0 17.1 %collective-permute-start.20 = (f32[128,128]{1,0:T(8,128)S(1)}, f32[128,128]{1,0:T(8,128)S(1)}, u32[]{:S(2)}, u32[]{:S(2)}) collective-permute-start(f32[128,128]{1,0:T(8,128)S(1)} %add.70), channel_id=1, source_target_pairs={{0,8},{8,0},{16,24},{24,16},{1,9},{9,1},{17,25},{25,17},{2,10},{10... | collective-permute-start | bytes 196616 | tf_op jit(solution)/shard_map/ppermute | solution.py:415
  150.9 1.0 copy-start.5
  163.0 23.7 %collective-permute-start.23 = (bf16[16,32,256]{2,1,0:T(8,128)(2,1)}, bf16[16,32,256]{2,1,0:T(8,128)(2,1)S(1)}, u32[]{:S(2)}, u32[]{:S(2)}) collective-permute-start(bf16[16,32,256]{2,1,0:T(8,128)(2,1)} %get-tuple-element.17), channel_id=1, source_target_pairs={{0,8},{8,16},{16,24},{24,0},{1,9},{9,17},{17,25},{25,1},{2,10},{10... | collective-permute-start | bytes 786440 | tf_op jit(solution)/shard_map/ppermute | solution.py:504
  163.6 28.7 %collective-permute-start.24 = (bf16[16,32,256]{2,1,0:T(8,128)(2,1)}, bf16[16,32,256]{2,1,0:T(8,128)(2,1)S(1)}, u32[]{:S(2)}, u32[]{:S(2)}) collective-permute-start(bf16[16,32,256]{2,1,0:T(8,128)(2,1)} %get-tuple-element.18), channel_id=1, source_target_pairs={{0,16},{8,24},{16,0},{24,8},{1,17},{9,25},{17,1},{25,9},{2,18},{10... | collective-permute-start | bytes 786440 | tf_op jit(solution)/shard_map/ppermute | solution.py:504
  165.1 29.3 %collective-permute-start.25 = (bf16[16,32,256]{2,1,0:T(8,128)(2,1)}, bf16[16,32,256]{2,1,0:T(8,128)(2,1)S(1)}, u32[]{:S(2)}, u32[]{:S(2)}) collective-permute-start(bf16[16,32,256]{2,1,0:T(8,128)(2,1)} %get-tuple-element.15.refs_10_), channel_id=1, source_target_pairs={{0,24},{8,0},{16,8},{24,16},{1,25},{9,1},{17,9},{25,17},{2,26},{10... | collective-permute-start | bytes 786440 | tf_op jit(solution)/shard_map/ppermute | solution.py:504
  186.7 7.7 %copy-start.13 = (bf16[16,32,256]{2,1,0:T(8,128)(2,1)}, bf16[16,32,256]{2,1,0:T(8,128)(2,1)S(1)}, u32[]{:S(2)}) copy-start(bf16[16,32,256]{2,1,0:T(8,128)(2,1)S(1)} %collective-permute-done.23.refs_2_) | copy-start | bytes 786436
  192.3 2.1 %copy-start.14 = (bf16[16,32,256]{2,1,0:T(8,128)(2,1)}, bf16[16,32,256]{2,1,0:T(8,128)(2,1)S(1)}, u32[]{:S(2)}) copy-start(bf16[16,32,256]{2,1,0:T(8,128)(2,1)S(1)} %collective-permute-done.24.refs_3_) | copy-start | bytes 786436
  194.4 0.7 copy-start.15
Sparse Core Ops, SparseCore 0:
  10.1 41.6 all-gather.2
  142.9 43.3 reduce-scatter.1

commit v4 on v3

--- a/solution.py
+++ b/solution.py
@@ -48,9 +48,9 @@
 
 
 def both(mat_ref, x):
-    y = jnp.dot(mat_ref[...], x, preferred_element_type=f32)
-    n = y.shape[0] // 2
-    return y[:n] + y[n:]
+    n = mat_ref.shape[0] // 2
+    hi = jnp.dot(mat_ref[:n], x, preferred_element_type=f32)
+    return hi + jnp.dot(mat_ref[n:], x, preferred_element_type=f32)
 
 
 def lag_kernel(keep_ref, mat_ref, x_ref, o_ref):

time: 205 us -> 205 us (level)
  no operation moved by 1% of the time
where the time goes in v4:
time: 205 us; the launch traced here: 204 us
  Pallas kernels  83.2 us (41%)
  waiting for transfers between devices  67.1 us (33%)
  starting transfers between devices  26.6 us (13%)
  between operations  14.3 us (7%)
  local copies, waits for them, and re-layouts  6.95 us (3%)
  other arithmetic  6.27 us (3%)
    ppermute x20, waiting for transfers between devices, to_xor(): return lax.ppermute(x, axis, [(d, d ^ r) for d in range(n)])  37.5 us
    pallas_call x1, Pallas kernels, lag_transform(): pl.pallas_call(lag_kernel, grid=(blocks,), in_specs=[pl.BlockSpec((1, 1,...  26.8 us
    pallas_call x2, Pallas kernels, corange_part(): pl.pallas_call(functools.partial(corange_kernel, n_in, n_out, len(before)...  22.4 us
    ppermute x20, starting transfers between devices, to_xor(): return lax.ppermute(x, axis, [(d, d ^ r) for d in range(n)])  19.6 us
    ppermute x3, waiting for transfers between devices, shards(): lax.ppermute(cor[d], 'out', [(k, (k + d) % n_out) for k in range(n_out)])  19.4 us
    pallas_call x1, Pallas kernels, sketch_part(): pl.pallas_call(functools.partial(sketch_kernel, len(probes), n_out, n_in)...  18.1 us
    ppermute x3, waiting for transfers between devices, shards(): lax.ppermute(own, 'out', [((k + d) % n_out, k) for k in range(n_out)])  9.77 us
    pallas_call x1, Pallas kernels, finish(): pl.pallas_call(functools.partial(finish_kernel, n_out, n_in), in_specs=[p...  8.17 us
  transfers between devices with their start and end apart: 28, of which 15 were waited for; matrix products, arithmetic and copies ran while one was open for 3% of the time, Pallas kernels for 30%

profile of v4, /device:TPU:9, one launch (start us, length us, event | category | flops | bytes accessed | tf_op | source)
XLA Modules:
  0.0 204.4 jit_solution(1146252197659879404)
XLA Ops:
  7.2 1.8 fusion
  9.1 1.3 collective-permute-start.2
  10.4 1.1 collective-permute-start.1
  11.5 1.4 collective-permute-start
  12.9 0.7 convert_element_type.80
  13.6 0.7 broadcast_in_dim.4
  14.3 26.8 %lag_transform.1.refs_5_ = bf16[32,512,512]{2,1,0:T(8,128)(2,1)} custom-call(f32[8,1,256]{2,1,0:T(1,128)} %bitcast.6, bf16[1024,512]{1,0:T(8,128)(2,1)} %constant.21.clone.mat_ref, bf16[63,512,256]{2,1,0:T(8,128)(2,1)} %x_ref.1), custom_call_target="tpu_custom_call" | custom-call | flops 8589934592 | bytes 16777216 | tf_op jit(solution)/shard_map/lag_transform/pallas_call | solution.py:79
  41.1 0.6 pad_add_fusion.place_ref
  41.7 2.8 %collective-permute-done.1.refs_2_ = bf16[16,32,256]{2,1,0:T(8,128)(2,1)S(1)} collective-permute-done((bf16[16,32,256]{2,1,0:T(8,128)(2,1)S(1)}, bf16[16,32,256]{2,1,0:T(8,128)(2,1)S(1)}, u32[]{:S(2)}, u32[]{:S(2)}) %collective-permute-start.1) | collective-permute-done | bytes 262176 | tf_op jit(solution)/shard_map/ppermute | solution.py:481
  44.5 6.9 %collective-permute-done.refs_1_ = bf16[16,32,256]{2,1,0:T(8,128)(2,1)S(1)} collective-permute-done((bf16[16,32,256]{2,1,0:T(8,128)(2,1)S(1)}, bf16[16,32,256]{2,1,0:T(8,128)(2,1)S(1)}, u32[]{:S(2)}, u32[]{:S(2)}) %collective-permute-start) | collective-permute-done | bytes 262176 | tf_op jit(solution)/shard_map/ppermute | solution.py:481
  51.4 0.4 all-gather.3.cloned.1.call-done
  51.9 0.3 copy-done.19
  52.2 18.1 %sketch_part.1 = (f32[16,64,512]{2,1,0:T(8,128)}, bf16[16,64,512]{2,1,0:T(8,128)(2,1)}, f32[16,64,512]{2,1,0:T(8,128)}, bf16[16,64,512]{2,1,0:T(8,128)(2,1)}) custom-call(s32[2]{0:T(128)} %pad_add_fusion.place_ref, bf16[1024,256]{1,0:T(8,128)(2,1)} %constant.22.clone.fwd_ref, bf16[512,512]{1,0:T(8,128)(2,1)} %constant.24.clone.back_ref, ...), custom_call_target="tpu_custom_call" | custom-call | flops 8589934592 | bytes 16777216 | tf_op jit(solution)/shard_map/sketch_part/pallas_call | solution.py:213
  70.2 1.3 collective-permute-start.3
  71.5 2.5 %collective-permute-done.3 = bf16[16,64,512]{2,1,0:T(8,128)(2,1)S(1)} collective-permute-done((bf16[16,64,512]{2,1,0:T(8,128)(2,1)}, bf16[16,64,512]{2,1,0:T(8,128)(2,1)S(1)}, u32[]{:S(2)}, u32[]{:S(2)}) %collective-permute-start.3) | collective-permute-done | bytes 1048608 | tf_op jit(solution)/shard_map/ppermute | solution.py:415
  74.0 1.7 add_convert_fusion.7
  75.7 1.3 collective-permute-start.4
  77.0 1.2 collective-permute-start.6
  78.2 0.2 collective-permute-start.5
  78.4 1.2 collective-permute-start.11
  79.6 3.7 %collective-permute-done.4 = bf16[4,64,512]{2,1,0:T(8,128)(2,1)S(1)} collective-permute-done((bf16[4,64,512]{2,1,0:T(8,128)(2,1)S(1)}, bf16[4,64,512]{2,1,0:T(8,128)(2,1)S(1)}, u32[]{:S(2)}, u32[]{:S(2)}) %collective-permute-start.4) | collective-permute-done | bytes 262176 | tf_op jit(solution)/shard_map/ppermute | solution.py:415
  83.3 6.6 %collective-permute-done.6 = bf16[4,64,512]{2,1,0:T(8,128)(2,1)S(1)} collective-permute-done((bf16[4,64,512]{2,1,0:T(8,128)(2,1)S(1)}, bf16[4,64,512]{2,1,0:T(8,128)(2,1)S(1)}, u32[]{:S(2)}, u32[]{:S(2)}) %collective-permute-start.6) | collective-permute-done | bytes 262176 | tf_op jit(solution)/shard_map/ppermute | solution.py:415
  89.9 1.2 add_convert_fusion.4.refs_0_
  91.2 1.2 collective-permute-start.9
  92.4 1.2 collective-permute-start.8
  93.7 0.2 collective-permute-start.7
  93.9 3.6 %collective-permute-done.9.refs_3_ = bf16[4,64,512]{2,1,0:T(8,128)(2,1)S(1)} collective-permute-done((bf16[4,64,512]{2,1,0:T(8,128)(2,1)S(1)}, bf16[4,64,512]{2,1,0:T(8,128)(2,1)S(1)}, u32[]{:S(2)}, u32[]{:S(2)}) %collective-permute-start.9) | collective-permute-done | bytes 262176 | tf_op jit(solution)/shard_map/ppermute | solution.py:415
  97.5 8.0 %collective-permute-done.8.refs_2_ = bf16[4,64,512]{2,1,0:T(8,128)(2,1)S(1)} collective-permute-done((bf16[4,64,512]{2,1,0:T(8,128)(2,1)S(1)}, bf16[4,64,512]{2,1,0:T(8,128)(2,1)S(1)}, u32[]{:S(2)}, u32[]{:S(2)}) %collective-permute-start.8) | collective-permute-done | bytes 262176 | tf_op jit(solution)/shard_map/ppermute | solution.py:415
  105.6 1.1 collective-permute-start.10
  106.7 0.3 add_convert_fusion.3
  107.0 0.6 collective-permute-start.12
  107.6 1.0 collective-permute-start.14
  108.6 1.1 collective-permute-start.13
  109.7 5.1 %collective-permute-done.12 = bf16[4,64,512]{2,1,0:T(8,128)(2,1)S(1)} collective-permute-done((bf16[4,64,512]{2,1,0:T(8,128)(2,1)S(1)}, bf16[4,64,512]{2,1,0:T(8,128)(2,1)S(1)}, u32[]{:S(2)}, u32[]{:S(2)}) %collective-permute-start.12) | collective-permute-done | bytes 262176 | tf_op jit(solution)/shard_map/ppermute | solution.py:415
  114.8 5.8 %collective-permute-done.14 = bf16[4,64,512]{2,1,0:T(8,128)(2,1)S(1)} collective-permute-done((bf16[4,64,512]{2,1,0:T(8,128)(2,1)S(1)}, bf16[4,64,512]{2,1,0:T(8,128)(2,1)S(1)}, u32[]{:S(2)}, u32[]{:S(2)}) %collective-permute-start.14) | collective-permute-done | bytes 262176 | tf_op jit(solution)/shard_map/ppermute | solution.py:415
  120.7 0.8 collective-permute-done.13
  121.4 0.2 add_convert_fusion.refs_6_.refs_0_.refs_5_
  121.6 1.3 collective-permute-start.17
  123.0 1.2 collective-permute-start.16
  124.1 0.2 collective-permute-start.15
  124.4 1.0 copy-done.4
  125.3 11.4 %corange_part.2.refs_4_.refs_6_ = bf16[4,16,32,256]{3,2,1,0:T(8,128)(2,1)} custom-call(s32[2]{0:T(128)} %pad_add_fusion.place_ref, bf16[1024,256]{1,0:T(8,128)(2,1)} %constant.23.clone.fwd_ref, bf16[512,512]{1,0:T(8,128)(2,1)} %constant.25.clone.back_ref, bf16[4,64,512]{2,1,0:T(8,128)(2,1)} %copy-done.2, bf16[4,64,512]{2,1,0:T(8,128)(2,1)} %copy-done.11, ...), custom_call_target="tpu_custom_call" | custom-call | flops 8589934592 | bytes 16777216 | tf_op jit(solution)/shard_map/corange_part/pallas_call | solution.py:299
  136.8 0.7 copy-done.6
  137.5 0.7 copy-done.8
  138.2 2.2 %join.1.refs_1_ = bf16[16,64,512]{2,1,0:T(8,128)(2,1)} custom-call(bf16[4,64,512]{2,1,0:T(8,128)(2,1)} %copy-done.1, bf16[4,64,512]{2,1,0:T(8,128)(2,1)} %copy-done.8, bf16[4,64,512]{2,1,0:T(8,128)(2,1)} %copy-done.7, bf16[4,64,512]{2,1,0:T(8,128)(2,1)} %copy-done.6, bf16[4,16,32,256]{3,2,1,0:T(8,128)(2,1)} %corange_part.2.refs_4_.refs_6_), custom_call_target="tpu_custom_call" | custom-call | tf_op jit(solution)/shard_map/join/pallas_call | solution.py:461
  140.5 2.3 %collective-permute-start.18 = (bf16[16,64,512]{2,1,0:T(8,128)(2,1)}, bf16[16,64,512]{2,1,0:T(8,128)(2,1)S(1)}, u32[]{:S(2)}, u32[]{:S(2)}) collective-permute-start(bf16[16,64,512]{2,1,0:T(8,128)(2,1)} %join.1.refs_1_), channel_id=1, source_target_pairs={{0,1},{1,0},{2,3},{3,2},{4,5},{5,4},{6,7},{7,6},{8,9},{9,8},{10,11... | collective-permute-start | bytes 3145736 | tf_op jit(solution)/shard_map/ppermute | solution.py:415
  142.8 3.1 %gram_part.1 = f32[128,128]{1,0:T(8,128)} custom-call(s32[2]{0:T(128)} %pad_add_fusion.place_ref, bf16[16,64,512]{2,1,0:T(8,128)(2,1)} %copy-done, bf16[16,64,512]{2,1,0:T(8,128)(2,1)} %join.1.refs_1_), custom_call_target="tpu_custom_call" | custom-call | tf_op jit(solution)/shard_map/gram_part/pallas_call | solution.py:343
  145.9 1.4 collective-permute-done.19
  147.4 0.9 add.70
  148.2 0.7 collective-permute-start.22
  148.9 0.2 collective-permute-start.21
  149.1 1.9 collective-permute-start.20
  150.9 1.0 copy-done.5
  151.9 11.1 %corange_part.3 = (f32[16,32,256]{2,1,0:T(8,128)}, bf16[16,32,256]{2,1,0:T(8,128)(2,1)}, bf16[16,32,256]{2,1,0:T(8,128)(2,1)}, bf16[16,32,256]{2,1,0:T(8,128)(2,1)}) custom-call(s32[2]{0:T(128)} %pad_add_fusion.place_ref, bf16[1024,256]{1,0:T(8,128)(2,1)} %constant.23.clone.fwd_ref, bf16[512,512]{1,0:T(8,128)(2,1)} %constant.25.clone.back_ref, ...), custom_call_target="tpu_custom_call" | custom-call | flops 8589934592 | bytes 16777216 | tf_op jit(solution)/shard_map/corange_part/pallas_call | solution.py:299
  163.0 0.7 collective-permute-start.23
  163.7 1.5 collective-permute-start.24
  165.2 1.0 collective-permute-start.25
  166.2 0.6 add_multiply_fusion.refs_11_
  166.8 8.2 %finish.1.refs_5_ = bf16[32,512,128]{2,1,0:T(8,128)(2,1)} custom-call(s32[2]{0:T(128)} %pad_add_fusion.place_ref, bf16[4,64,512]{2,1,0:T(8,128)(2,1)} %copy-done.2, bf16[4,64,512]{2,1,0:T(8,128)(2,1)} %copy-done.11, bf16[4,64,512]{2,1,0:T(8,128)(2,1)} %copy-done.10, bf16[4,64,512]{2,1,0:T(8,128)(2,1)} %copy-done.9, bf16[16,64,512]{2,1,0:T(8,128)(2,1)} %copy-done.4, ...), custom_call_target="tpu_custom_call" | custom-call | bytes 67108864 | tf_op jit(solution)/shard_map/finish/pallas_call | solution.py:396
  175.0 11.7 %collective-permute-done.23.refs_2_ = bf16[16,32,256]{2,1,0:T(8,128)(2,1)S(1)} collective-permute-done((bf16[16,32,256]{2,1,0:T(8,128)(2,1)}, bf16[16,32,256]{2,1,0:T(8,128)(2,1)S(1)}, u32[]{:S(2)}, u32[]{:S(2)}) %collective-permute-start.23) | collective-permute-done | bytes 262176 | tf_op jit(solution)/shard_map/ppermute | solution.py:504
  186.7 5.6 %collective-permute-done.24.refs_3_ = bf16[16,32,256]{2,1,0:T(8,128)(2,1)S(1)} collective-permute-done((bf16[16,32,256]{2,1,0:T(8,128)(2,1)}, bf16[16,32,256]{2,1,0:T(8,128)(2,1)S(1)}, u32[]{:S(2)}, u32[]{:S(2)}) %collective-permute-start.24) | collective-permute-done | bytes 262176 | tf_op jit(solution)/shard_map/ppermute | solution.py:504
  192.3 2.0 %collective-permute-done.25.refs_4_ = bf16[16,32,256]{2,1,0:T(8,128)(2,1)S(1)} collective-permute-done((bf16[16,32,256]{2,1,0:T(8,128)(2,1)}, bf16[16,32,256]{2,1,0:T(8,128)(2,1)S(1)}, u32[]{:S(2)}, u32[]{:S(2)}) %collective-permute-start.25) | collective-permute-done | bytes 262176 | tf_op jit(solution)/shard_map/ppermute | solution.py:504
  194.4 0.7 copy-done.15
  195.1 2.4 %total_corange.1 = f32[32,32,256]{2,1,0:T(8,128)} custom-call(bf16[16,32,256]{2,1,0:T(8,128)(2,1)} %reduce-scatter.2.cloned.1.call-done.refs_0_, f32[16,32,256]{2,1,0:T(8,128)} %get-tuple-element.16.refs_1_, bf16[16,32,256]{2,1,0:T(8,128)(2,1)} %copy-done.13, bf16[16,32,256]{2,1,0:T(8,128)(2,1)} %copy-done.14, bf16[16,32,256]{2,1,0:T(8,128)(2,1)} %copy-done.15, ...), custom_call_target="tpu_custom_call" | custom-call | tf_op jit(solution)/shard_map/total_corange/pallas_call | solution.py:367
  (54 shorter events, 0.5 us)
Async XLA Ops:
  7.2 44.7 %all-gather.3.cloned.1.call-start = ((), (), s32[]{:S(2)}) async-start(), calls=%async_computation.2 | async-start | bytes 1310720 | tf_op jit(solution)/shard_map/all_gather | solution.py:483
  9.0 32.1 %copy-start.12 = (bf16[16,32,256]{2,1,0:T(8,128)(2,1)}, bf16[16,32,256]{2,1,0:T(8,128)(2,1)S(1)}, u32[]{:S(2)}) copy-start(bf16[16,32,256]{2,1,0:T(8,128)(2,1)S(1)} %get-tuple-element.26.refs_0_) | copy-start | bytes 786436
  9.0 185.4 %reduce-scatter.2.cloned.1.call-start = ((), (), s32[]{:S(2)}) async-start(), calls=%async_computation.1 | async-start | bytes 1310720 | tf_op jit(solution)/shard_map/reduce_scatter | solution.py:501
  9.1 32.6 %collective-permute-start.2 = (bf16[16,32,256]{2,1,0:T(8,128)(2,1)S(1)}, bf16[16,32,256]{2,1,0:T(8,128)(2,1)S(1)}, u32[]{:S(2)}, u32[]{:S(2)}) collective-permute-start(bf16[16,32,256]{2,1,0:T(8,128)(2,1)S(1)} %get-tuple-element.26.refs_0_), channel_id=1, source_target_pairs={{24,0},{0,8},{8,16},{16,24},{25,1},{1,9},{9,17},{17,25},{26,2},{2,... | collective-permute-start | bytes 786440 | tf_op jit(solution)/shard_map/ppermute | solution.py:481
  10.4 34.1 %collective-permute-start.1 = (bf16[16,32,256]{2,1,0:T(8,128)(2,1)S(1)}, bf16[16,32,256]{2,1,0:T(8,128)(2,1)S(1)}, u32[]{:S(2)}, u32[]{:S(2)}) collective-permute-start(bf16[16,32,256]{2,1,0:T(8,128)(2,1)S(1)} %get-tuple-element.26.refs_0_), channel_id=1, source_target_pairs={{16,0},{24,8},{0,16},{8,24},{17,1},{25,9},{1,17},{9,25},{18,2},{26... | collective-permute-start | bytes 786440 | tf_op jit(solution)/shard_map/ppermute | solution.py:481
  11.5 40.0 %collective-permute-start = (bf16[16,32,256]{2,1,0:T(8,128)(2,1)S(1)}, bf16[16,32,256]{2,1,0:T(8,128)(2,1)S(1)}, u32[]{:S(2)}, u32[]{:S(2)}) collective-permute-start(bf16[16,32,256]{2,1,0:T(8,128)(2,1)S(1)} %get-tuple-element.26.refs_0_), channel_id=1, source_target_pairs={{8,0},{16,8},{24,16},{0,24},{9,1},{17,9},{25,17},{1,25},{10,2},{18... | collective-permute-start | bytes 786440 | tf_op jit(solution)/shard_map/ppermute | solution.py:481
  41.7 10.2 %copy-start.17 = (bf16[16,32,256]{2,1,0:T(8,128)(2,1)}, bf16[16,32,256]{2,1,0:T(8,128)(2,1)S(1)}, u32[]{:S(2)}) copy-start(bf16[16,32,256]{2,1,0:T(8,128)(2,1)S(1)} %collective-permute-done.2.refs_3_) | copy-start | bytes 786436
  44.5 7.4 %copy-start.18 = (bf16[16,32,256]{2,1,0:T(8,128)(2,1)}, bf16[16,32,256]{2,1,0:T(8,128)(2,1)S(1)}, u32[]{:S(2)}) copy-start(bf16[16,32,256]{2,1,0:T(8,128)(2,1)S(1)} %collective-permute-done.1.refs_2_) | copy-start | bytes 786436
  51.4 0.7 copy-start.19
  70.2 8.2 %copy-start.16 = (bf16[16,64,512]{2,1,0:T(8,128)(2,1)S(1)}, bf16[16,64,512]{2,1,0:T(8,128)(2,1)}, u32[]{:S(2)}) copy-start(bf16[16,64,512]{2,1,0:T(8,128)(2,1)} %get-tuple-element.14) | copy-start | bytes 3145732
  70.2 3.8 %collective-permute-start.3 = (bf16[16,64,512]{2,1,0:T(8,128)(2,1)}, bf16[16,64,512]{2,1,0:T(8,128)(2,1)S(1)}, u32[]{:S(2)}, u32[]{:S(2)}) collective-permute-start(bf16[16,64,512]{2,1,0:T(8,128)(2,1)} %get-tuple-element.12), channel_id=1, source_target_pairs={{0,1},{1,0},{2,3},{3,2},{4,5},{5,4},{6,7},{7,6},{8,9},{9,8},{10,11... | collective-permute-start | bytes 3145736 | tf_op jit(solution)/shard_map/ppermute | solution.py:415
  75.7 31.0 %copy-start.3 = (f32[16,64,512]{2,1,0:T(8,128)S(1)}, f32[16,64,512]{2,1,0:T(8,128)}, u32[]{:S(2)}) copy-start(f32[16,64,512]{2,1,0:T(8,128)} %get-tuple-element.13) | copy-start | bytes 6291460
  75.7 7.6 %collective-permute-start.4 = (bf16[4,64,512]{2,1,0:T(8,128)(2,1)S(1)}, bf16[4,64,512]{2,1,0:T(8,128)(2,1)S(1)}, u32[]{:S(2)}, u32[]{:S(2)}) collective-permute-start(bf16[4,64,512]{2,1,0:T(8,128)(2,1)S(1)} %get-tuple-element.22), channel_id=1, source_target_pairs={{0,2},{1,3},{2,0},{3,1},{4,6},{5,7},{6,4},{7,5},{8,10},{9,11},{10,... | collective-permute-start | bytes 786440 | tf_op jit(solution)/shard_map/ppermute | solution.py:415
  77.0 12.9 %collective-permute-start.6 = (bf16[4,64,512]{2,1,0:T(8,128)(2,1)S(1)}, bf16[4,64,512]{2,1,0:T(8,128)(2,1)S(1)}, u32[]{:S(2)}, u32[]{:S(2)}) collective-permute-start(bf16[4,64,512]{2,1,0:T(8,128)(2,1)S(1)} %get-tuple-element.23), channel_id=1, source_target_pairs={{0,6},{1,7},{2,4},{3,5},{4,2},{5,3},{6,0},{7,1},{8,14},{9,15},{10,... | collective-permute-start | bytes 786440 | tf_op jit(solution)/shard_map/ppermute | solution.py:415
  78.2 11.7 %collective-permute-start.5 = (bf16[4,64,512]{2,1,0:T(8,128)(2,1)S(1)}, bf16[4,64,512]{2,1,0:T(8,128)(2,1)S(1)}, u32[]{:S(2)}, u32[]{:S(2)}) collective-permute-start(bf16[4,64,512]{2,1,0:T(8,128)(2,1)S(1)} %get-tuple-element.24), channel_id=1, source_target_pairs={{0,4},{1,5},{2,6},{3,7},{4,0},{5,1},{6,2},{7,3},{8,12},{9,13},{10,... | collective-permute-start | bytes 786440 | tf_op jit(solution)/shard_map/ppermute | solution.py:415
  78.4 28.3 %collective-permute-start.11 = (bf16[16,64,512]{2,1,0:T(8,128)(2,1)S(1)}, bf16[16,64,512]{2,1,0:T(8,128)(2,1)S(1)}, u32[]{:S(2)}, u32[]{:S(2)}) collective-permute-start(bf16[16,64,512]{2,1,0:T(8,128)(2,1)S(1)} %copy-done.16), channel_id=1, source_target_pairs={{0,1},{1,0},{2,3},{3,2},{4,5},{5,4},{6,7},{7,6},{8,9},{9,8},{10,11... | collective-permute-start | bytes 3145736 | tf_op jit(solution)/shard_map/ppermute | solution.py:415
  91.2 15.8 %copy-start.2 = (bf16[4,64,512]{2,1,0:T(8,128)(2,1)}, bf16[4,64,512]{2,1,0:T(8,128)(2,1)S(1)}, u32[]{:S(2)}) copy-start(bf16[4,64,512]{2,1,0:T(8,128)(2,1)S(1)} %add_convert_fusion.4.refs_0_) | copy-start | bytes 786436
  91.2 6.3 %collective-permute-start.9 = (bf16[4,64,512]{2,1,0:T(8,128)(2,1)S(1)}, bf16[4,64,512]{2,1,0:T(8,128)(2,1)S(1)}, u32[]{:S(2)}, u32[]{:S(2)}) collective-permute-start(bf16[4,64,512]{2,1,0:T(8,128)(2,1)S(1)} %add_convert_fusion.4.refs_0_), channel_id=1, source_target_pairs={{0,6},{1,7},{2,4},{3,5},{4,2},{5,3},{6,0},{7,1},{8,14},{9,15},{10,... | collective-permute-start | bytes 786440 | tf_op jit(solution)/shard_map/ppermute | solution.py:415
  92.4 13.0 %collective-permute-start.8 = (bf16[4,64,512]{2,1,0:T(8,128)(2,1)S(1)}, bf16[4,64,512]{2,1,0:T(8,128)(2,1)S(1)}, u32[]{:S(2)}, u32[]{:S(2)}) collective-permute-start(bf16[4,64,512]{2,1,0:T(8,128)(2,1)S(1)} %add_convert_fusion.4.refs_0_), channel_id=1, source_target_pairs={{0,4},{1,5},{2,6},{3,7},{4,0},{5,1},{6,2},{7,3},{8,12},{9,13},{10,... | collective-permute-start | bytes 786440 | tf_op jit(solution)/shard_map/ppermute | solution.py:415
  93.7 11.8 %collective-permute-start.7 = (bf16[4,64,512]{2,1,0:T(8,128)(2,1)S(1)}, bf16[4,64,512]{2,1,0:T(8,128)(2,1)S(1)}, u32[]{:S(2)}, u32[]{:S(2)}) collective-permute-start(bf16[4,64,512]{2,1,0:T(8,128)(2,1)S(1)} %add_convert_fusion.4.refs_0_), channel_id=1, source_target_pairs={{0,2},{1,3},{2,0},{3,1},{4,6},{5,7},{6,4},{7,5},{8,10},{9,11},{10,... | collective-permute-start | bytes 786440 | tf_op jit(solution)/shard_map/ppermute | solution.py:415
  97.5 9.5 %copy-start.9 = (bf16[4,64,512]{2,1,0:T(8,128)(2,1)}, bf16[4,64,512]{2,1,0:T(8,128)(2,1)S(1)}, u32[]{:S(2)}) copy-start(bf16[4,64,512]{2,1,0:T(8,128)(2,1)S(1)} %collective-permute-done.9.refs_3_) | copy-start | bytes 786436
  105.4 1.6 copy-start.10
  105.4 1.6 copy-start.11
  105.6 16.0 %copy-start = (bf16[16,64,512]{2,1,0:T(8,128)(2,1)}, bf16[16,64,512]{2,1,0:T(8,128)(2,1)S(1)}, u32[]{:S(2)}) copy-start(bf16[16,64,512]{2,1,0:T(8,128)(2,1)S(1)} %pad_maximum_fusion.refs_0_) | copy-start | bytes 3145732
  105.6 18.8 %collective-permute-start.10 = (bf16[16,64,512]{2,1,0:T(8,128)(2,1)S(1)}, bf16[16,64,512]{2,1,0:T(8,128)(2,1)S(1)}, u32[]{:S(2)}, u32[]{:S(2)}) collective-permute-start(bf16[16,64,512]{2,1,0:T(8,128)(2,1)S(1)} %pad_maximum_fusion.refs_0_), channel_id=1, source_target_pairs={{0,1},{1,0},{2,3},{3,2},{4,5},{5,4},{6,7},{7,6},{8,9},{9,8},{10,11... | collective-permute-start | bytes 3145736 | tf_op jit(solution)/shard_map/ppermute | solution.py:415
  107.0 7.8 %collective-permute-start.12 = (bf16[4,64,512]{2,1,0:T(8,128)(2,1)S(1)}, bf16[4,64,512]{2,1,0:T(8,128)(2,1)S(1)}, u32[]{:S(2)}, u32[]{:S(2)}) collective-permute-start(bf16[4,64,512]{2,1,0:T(8,128)(2,1)S(1)} %get-tuple-element.19), channel_id=1, source_target_pairs={{0,2},{1,3},{2,0},{3,1},{4,6},{5,7},{6,4},{7,5},{8,10},{9,11},{10,... | collective-permute-start | bytes 786440 | tf_op jit(solution)/shard_map/ppermute | solution.py:415
  107.6 13.0 %collective-permute-start.14 = (bf16[4,64,512]{2,1,0:T(8,128)(2,1)S(1)}, bf16[4,64,512]{2,1,0:T(8,128)(2,1)S(1)}, u32[]{:S(2)}, u32[]{:S(2)}) collective-permute-start(bf16[4,64,512]{2,1,0:T(8,128)(2,1)S(1)} %get-tuple-element.20), channel_id=1, source_target_pairs={{0,6},{1,7},{2,4},{3,5},{4,2},{5,3},{6,0},{7,1},{8,14},{9,15},{10,... | collective-permute-start | bytes 786440 | tf_op jit(solution)/shard_map/ppermute | solution.py:415
  108.6 12.8 %collective-permute-start.13 = (bf16[4,64,512]{2,1,0:T(8,128)(2,1)S(1)}, bf16[4,64,512]{2,1,0:T(8,128)(2,1)S(1)}, u32[]{:S(2)}, u32[]{:S(2)}) collective-permute-start(bf16[4,64,512]{2,1,0:T(8,128)(2,1)S(1)} %get-tuple-element.21), channel_id=1, source_target_pairs={{0,4},{1,5},{2,6},{3,7},{4,0},{5,1},{6,2},{7,3},{8,12},{9,13},{10,... | collective-permute-start | bytes 786440 | tf_op jit(solution)/shard_map/ppermute | solution.py:415
  121.6 2.7 %copy-start.1 = (bf16[4,64,512]{2,1,0:T(8,128)(2,1)}, bf16[4,64,512]{2,1,0:T(8,128)(2,1)S(1)}, u32[]{:S(2)}) copy-start(bf16[4,64,512]{2,1,0:T(8,128)(2,1)S(1)} %add_convert_fusion.refs_6_.refs_0_.refs_5_) | copy-start | bytes 786436
  121.6 15.1 %collective-permute-start.17 = (bf16[4,64,512]{2,1,0:T(8,128)(2,1)S(1)}, bf16[4,64,512]{2,1,0:T(8,128)(2,1)S(1)}, u32[]{:S(2)}, u32[]{:S(2)}) collective-permute-start(bf16[4,64,512]{2,1,0:T(8,128)(2,1)S(1)} %add_convert_fusion.refs_6_.refs_0_.refs_5_), channel_id=1, source_target_pairs={{0,6},{1,7},{2,4},{3,5},{4,2},{5,3},{6,0},{7,1},{8,14},{9,15},{10,... | collective-permute-start | bytes 786440 | tf_op jit(solution)/shard_map/ppermute | solution.py:415
  123.0 13.8 %collective-permute-start.16 = (bf16[4,64,512]{2,1,0:T(8,128)(2,1)S(1)}, bf16[4,64,512]{2,1,0:T(8,128)(2,1)S(1)}, u32[]{:S(2)}, u32[]{:S(2)}) collective-permute-start(bf16[4,64,512]{2,1,0:T(8,128)(2,1)S(1)} %add_convert_fusion.refs_6_.refs_0_.refs_5_), channel_id=1, source_target_pairs={{0,4},{1,5},{2,6},{3,7},{4,0},{5,1},{6,2},{7,3},{8,12},{9,13},{10,... | collective-permute-start | bytes 786440 | tf_op jit(solution)/shard_map/ppermute | solution.py:415
  124.1 12.6 %collective-permute-start.15 = (bf16[4,64,512]{2,1,0:T(8,128)(2,1)S(1)}, bf16[4,64,512]{2,1,0:T(8,128)(2,1)S(1)}, u32[]{:S(2)}, u32[]{:S(2)}) collective-permute-start(bf16[4,64,512]{2,1,0:T(8,128)(2,1)S(1)} %add_convert_fusion.refs_6_.refs_0_.refs_5_), channel_id=1, source_target_pairs={{0,2},{1,3},{2,0},{3,1},{4,6},{5,7},{6,4},{7,5},{8,10},{9,11},{10,... | collective-permute-start | bytes 786440 | tf_op jit(solution)/shard_map/ppermute | solution.py:415
  124.4 1.0 copy-start.4
  136.7 0.7 copy-start.6
  136.8 0.8 copy-start.7
  137.5 0.7 copy-start.8
  140.5 10.5 %collective-permute-start.18 = (bf16[16,64,512]{2,1,0:T(8,128)(2,1)}, bf16[16,64,512]{2,1,0:T(8,128)(2,1)S(1)}, u32[]{:S(2)}, u32[]{:S(2)}) collective-permute-start(bf16[16,64,512]{2,1,0:T(8,128)(2,1)} %join.1.refs_1_), channel_id=1, source_target_pairs={{0,1},{1,0},{2,3},{3,2},{4,5},{5,4},{6,7},{7,6},{8,9},{9,8},{10,11... | collective-permute-start | bytes 3145736 | tf_op jit(solution)/shard_map/ppermute | solution.py:415
  145.9 1.5 collective-permute-start.19
  148.2 16.9 %collective-permute-start.22 = (f32[128,128]{1,0:T(8,128)S(1)}, f32[128,128]{1,0:T(8,128)S(1)}, u32[]{:S(2)}, u32[]{:S(2)}) collective-permute-start(f32[128,128]{1,0:T(8,128)S(1)} %add.70), channel_id=1, source_target_pairs={{0,24},{8,16},{16,8},{24,0},{1,25},{9,17},{17,9},{25,1},{2,26},{10... | collective-permute-start | bytes 196616 | tf_op jit(solution)/shard_map/ppermute | solution.py:415
  148.9 17.3 %collective-permute-start.21 = (f32[128,128]{1,0:T(8,128)S(1)}, f32[128,128]{1,0:T(8,128)S(1)}, u32[]{:S(2)}, u32[]{:S(2)}) collective-permute-start(f32[128,128]{1,0:T(8,128)S(1)} %add.70), channel_id=1, source_target_pairs={{0,16},{8,24},{16,0},{24,8},{1,17},{9,25},{17,1},{25,9},{2,18},{10... | collective-permute-start | bytes 196616 | tf_op jit(solution)/shard_map/ppermute | solution.py:415
  149.1 17.1 %collective-permute-start.20 = (f32[128,128]{1,0:T(8,128)S(1)}, f32[128,128]{1,0:T(8,128)S(1)}, u32[]{:S(2)}, u32[]{:S(2)}) collective-permute-start(f32[128,128]{1,0:T(8,128)S(1)} %add.70), channel_id=1, source_target_pairs={{0,8},{8,0},{16,24},{24,16},{1,9},{9,1},{17,25},{25,17},{2,10},{10... | collective-permute-start | bytes 196616 | tf_op jit(solution)/shard_map/ppermute | solution.py:415
  150.9 1.0 copy-start.5
  163.0 23.7 %collective-permute-start.23 = (bf16[16,32,256]{2,1,0:T(8,128)(2,1)}, bf16[16,32,256]{2,1,0:T(8,128)(2,1)S(1)}, u32[]{:S(2)}, u32[]{:S(2)}) collective-permute-start(bf16[16,32,256]{2,1,0:T(8,128)(2,1)} %get-tuple-element.17), channel_id=1, source_target_pairs={{0,8},{8,16},{16,24},{24,0},{1,9},{9,17},{17,25},{25,1},{2,10},{10... | collective-permute-start | bytes 786440 | tf_op jit(solution)/shard_map/ppermute | solution.py:504
  163.7 28.7 %collective-permute-start.24 = (bf16[16,32,256]{2,1,0:T(8,128)(2,1)}, bf16[16,32,256]{2,1,0:T(8,128)(2,1)S(1)}, u32[]{:S(2)}, u32[]{:S(2)}) collective-permute-start(bf16[16,32,256]{2,1,0:T(8,128)(2,1)} %get-tuple-element.18), channel_id=1, source_target_pairs={{0,16},{8,24},{16,0},{24,8},{1,17},{9,25},{17,1},{25,9},{2,18},{10... | collective-permute-start | bytes 786440 | tf_op jit(solution)/shard_map/ppermute | solution.py:504
  165.2 29.2 %collective-permute-start.25 = (bf16[16,32,256]{2,1,0:T(8,128)(2,1)}, bf16[16,32,256]{2,1,0:T(8,128)(2,1)S(1)}, u32[]{:S(2)}, u32[]{:S(2)}) collective-permute-start(bf16[16,32,256]{2,1,0:T(8,128)(2,1)} %get-tuple-element.15.refs_10_), channel_id=1, source_target_pairs={{0,24},{8,0},{16,8},{24,16},{1,25},{9,1},{17,9},{25,17},{2,26},{10... | collective-permute-start | bytes 786440 | tf_op jit(solution)/shard_map/ppermute | solution.py:504
  186.7 7.7 %copy-start.13 = (bf16[16,32,256]{2,1,0:T(8,128)(2,1)}, bf16[16,32,256]{2,1,0:T(8,128)(2,1)S(1)}, u32[]{:S(2)}) copy-start(bf16[16,32,256]{2,1,0:T(8,128)(2,1)S(1)} %collective-permute-done.23.refs_2_) | copy-start | bytes 786436
  192.3 2.1 %copy-start.14 = (bf16[16,32,256]{2,1,0:T(8,128)(2,1)}, bf16[16,32,256]{2,1,0:T(8,128)(2,1)S(1)}, u32[]{:S(2)}) copy-start(bf16[16,32,256]{2,1,0:T(8,128)(2,1)S(1)} %collective-permute-done.24.refs_3_) | copy-start | bytes 786436
  194.4 0.7 copy-start.15
Sparse Core Ops, SparseCore 0:
  10.1 41.6 all-gather.2
  142.9 43.3 reduce-scatter.1
